TPU v7x, 512 devices: a whole 4x8x8 slice. The times are simulated.
512 devices in a mesh: tp: 32 (over z, y_hi), rep: 16 (over y_lo, x, core).
Axes of the slice: x: 4, y: 8 (y_hi: 4, y_lo: 2; y = y_hi * 2 + y_lo), z: 8, core: 2. Of those that a mesh axis runs over, the one named last changes fastest.
Arguments:
- tokens: bfloat16 [6144, 8192], P('rep', 'tp'), may hold values from -6 to 6
- row_lengths: int32 [32], P('rep'), may hold values from 1 to 192
- attn_gain: float32 [8192], P('tp'), may hold values from 0.1 to 1.9
- query_weight: bfloat16 [8192, 4096], P('rep', 'tp'), may hold values from -2 to 2
- key_weight: bfloat16 [8192, 512], P('rep', 'tp'), may hold values from -2 to 2
- value_matrix: bfloat16 [8192, 512], P('rep', 'tp'), may hold values from -0.0625 to 0.0625
- output_weight: bfloat16 [4096, 8192], P('rep', 'tp'), may hold values from -0.09375 to 0.09375
- final_gain: float32 [8192], P('tp'), may hold values from 0.1 to 1.9
- value_head: float32 [8192, 6], P('tp'), may hold values from -0.0625 to 0.0625
Outputs:
- resid_out: bfloat16 [6144, 8192], P('rep', 'tp')
- objective_scores: float32 [6144, 6], P('rep')
All inputs are finite; a program needn't handle non-finite values.
Results may differ from a plain program's by a relative error of at most 0.025.
Values may be sent and summed in bfloat16 or wider, within the bound.
No kernel may reach another device: no remote copies, remote signals or barrier semaphores. Data moves between devices by JAX's collectives and lax.ppermute only.
A program may use at most 64 MiB of HBM per device.

v0:
```python
import jax
import jax.numpy as jnp
from jax import lax
from jax.sharding import Mesh
from jax.sharding import PartitionSpec as P

KEY_VALUE_HEADS = 4
HEAD_SIZE = 128
TP = ("tp_0", "tp_1")
REP = ("rep_0", "rep_1", "rep_2")


EPS = 1e-05


def whole_of(x, axes, dim):
    if not axes:
        return x
    nearer = lax.all_gather(x, axes[-1], axis=dim, tiled=True)
    return whole_of(nearer, axes[:-1], dim)


def copy_for_each(x, axis):
    count = lax.axis_size(axis)
    return lax.all_to_all(jnp.broadcast_to(x[None], (count, *x.shape)), axis, 0, 0, tiled=True)


def joined_along(blocks, dim):
    blocks = jnp.moveaxis(blocks, 0, dim)
    shape = blocks.shape
    return blocks.reshape(*shape[:dim], shape[dim] * shape[dim + 1], *shape[dim + 2 :])


def gather_axes(x, axes, dim):
    far, near = axes
    blocks = copy_for_each(copy_for_each(x, far), near)
    return joined_along(blocks.swapaxes(0, 1).reshape(-1, *x.shape), dim)


def sent_together(arrays, axis, dim, along):
    widths = [a.shape[along] for a in arrays]
    both = jnp.concatenate(arrays, axis=along)
    whole = gather_axes(both, axis, dim)
    return tuple(jnp.split(whole, [sum(widths[:k]) for k in range(1, len(widths))], axis=along))


def turned_gather(arrays, axis, dims):
    turned = [jnp.moveaxis(a, dim, 0) for a, dim in zip(arrays, dims)]
    widths = [t[0].size for t in turned]
    both = jnp.concatenate([t.reshape(-1, w) for t, w in zip(turned, widths)], axis=1)
    whole = lax.all_gather(both, axis, axis=0, tiled=True)
    blocks = jnp.split(whole, [sum(widths[:k]) for k in range(1, len(widths))], axis=1)
    return tuple(
        (
            jnp.moveaxis(b.reshape(-1, *t.shape[1:]), 0, dim)
            for b, t, dim in zip(blocks, turned, dims)
        )
    )


def over_copies(x, axis):
    return copy_for_each(x, axis).sum(axis=0)


def in_one(arrays, axis):
    flat, at, finished = (jnp.concatenate([a.reshape(-1) for a in arrays]), 0, [])
    running = over_copies(flat, axis)
    for a in arrays:
        finished.append(running[at : at + a.size].reshape(a.shape))
        at += a.size
    return tuple(finished)


def local(
    tokens,
    row_lengths,
    attn_gain,
    query_weight,
    key_weight,
    value_matrix,
    output_weight,
    final_gain,
    value_head,
):
    width = tokens.shape[1] * lax.axis_size(TP)
    xfloat = tokens.astype(jnp.float32)
    whole, gains = (
        whole_of(tokens, TP, 1),
        whole_of(attn_gain.astype(jnp.bfloat16), TP, 0).astype(attn_gain.dtype),
    )
    wfloat = whole.astype(jnp.float32)
    first_scale = lax.rsqrt(jnp.mean(wfloat * wfloat, axis=1, keepdims=True) + EPS)
    normed = (wfloat * first_scale * gains).astype(jnp.bfloat16)
    rows_here = normed.shape[0]
    head_cols = query_weight.shape[1]
    pieces = sent_together(
        (query_weight, key_weight, value_matrix), (("rep_0", "rep_1"), "rep_2"), 0, 1
    )
    columns = normed
    query, key_rows, value_rows = tuple(
        (jnp.dot(columns, piece, preferred_element_type=jnp.float32) for piece in pieces)
    )
    query = query.astype(jnp.bfloat16)
    key_rows = key_rows.astype(jnp.bfloat16)
    value_rows = value_rows.astype(jnp.bfloat16)
    key_full, value_full = turned_gather((key_rows, value_rows), TP, (1, 1))
    local_heads = head_cols // HEAD_SIZE
    sequence_rows = row_lengths.shape[0]
    row_length_count = rows_here // sequence_rows
    first_head = lax.axis_index(TP) * local_heads
    key_value_index = (first_head + jnp.arange(local_heads, dtype=jnp.int32)) % KEY_VALUE_HEADS
    query4 = query.reshape(sequence_rows, row_length_count, local_heads, HEAD_SIZE)
    key_tensor4 = jnp.take(
        key_full.reshape(sequence_rows, row_length_count, KEY_VALUE_HEADS, HEAD_SIZE),
        key_value_index,
        axis=2,
    )
    value_tensor4 = jnp.take(
        value_full.reshape(sequence_rows, row_length_count, KEY_VALUE_HEADS, HEAD_SIZE),
        key_value_index,
        axis=2,
    )
    scores = jnp.einsum(
        "rqhd,rkhd->rhqk", query4, key_tensor4, preferred_element_type=jnp.float32
    ) * (1.0 / HEAD_SIZE**0.5)
    position = jnp.arange(row_length_count, dtype=jnp.int32)
    causal = position[None, :] <= position[:, None]
    allowed = causal[None, None, :, :] & (
        position[None, None, None, :] < row_lengths[:, None, None, None]
    )
    scores = jnp.where(allowed, scores, jnp.float32(-1e30))
    scores = scores - jnp.max(scores, axis=3, keepdims=True)
    expo = jnp.exp(scores)
    probs = (expo / jnp.sum(expo, axis=3, keepdims=True)).astype(jnp.bfloat16)
    attended = jnp.einsum(
        "rhqk,rkhd->rqhd", probs, value_tensor4, preferred_element_type=jnp.float32
    )
    attended = attended.astype(jnp.bfloat16).reshape(rows_here, head_cols)
    mixed_all = whole_of(attended, TP, 1)
    columns = mixed_all
    update = jnp.dot(
        columns,
        gather_axes(output_weight, (("rep_0", "rep_1"), "rep_2"), 0),
        preferred_element_type=jnp.float32,
    )
    resid_out = (xfloat + update).astype(jnp.bfloat16)
    rfloat = resid_out.astype(jnp.float32)
    squares = jnp.sum(rfloat * rfloat, axis=1)
    local_scores = jnp.dot(rfloat * final_gain, value_head, precision=lax.Precision.HIGHEST)
    total_out, weighted = in_one((squares, local_scores), TP)
    logits = weighted * lax.rsqrt(total_out / width + EPS)[:, None]
    live = (position[None, :] < row_lengths[:, None]).reshape(rows_here, 1)
    objective_scores = jnp.where(live, logits, jnp.float32(0.0))
    return (resid_out, objective_scores)


def solution(mesh):
    split = Mesh(mesh.devices.reshape(8, 4, 2, 4, 2), ("tp_0", "tp_1", "rep_0", "rep_1", "rep_2"))
    in_specs = (
        P(REP, TP),
        P(REP),
        P(TP),
        P(REP, TP),
        P(REP, TP),
        P(REP, TP),
        P(REP, TP),
        P(TP),
        P(TP, None),
    )
    out_specs = (P(REP, TP), P(REP, None))
    return jax.shard_map(local, mesh=split, in_specs=in_specs, out_specs=out_specs, check_vma=False)
```

profile of v0, /device:TPU:6, one launch (start us, length us, event | category | flops | bytes accessed | tf_op | source)
XLA Modules:
  0.0 309.5 jit_solution(3822176391573436343)
XLA Ops:
  7.2 22.4 %all_gather.21 = bf16[384,1024]{1,0:T(8,128)(2,1)} all-gather(bf16[384,256]{1,0:T(8,128)(2,1)} %param.11), channel_id=1, replica_groups=mesh['tp_0'=8,'tp_1'=4,'rep_0'=2,'rep_1'=4,'rep_2'=2] {'tp_1'}, dimensions={1}, use_global_device_ids=true | all-gather | bytes 983040 | tf_op jit(solution)/shard_map/all_gather | solution.py:19
  29.7 0.8 copy.62
  30.5 0.8 copy.61
  31.3 1.0 pad_maximum_fusion
  32.5 1.2 broadcast_in_dim.31
  33.7 5.1 %all-to-all-start = ((bf16[8,512,160]{1,2,0:T(8,128)(2,1)}), bf16[8,512,160]{1,2,0:T(8,128)(2,1)S(1)}, u32[]{:S(2)}, u32[]{:S(2)}) async-start(bf16[8,512,160]{1,2,0:T(8,128)(2,1)} %broadcast_in_dim.31), calls=%async_computation | async-start | bytes 2621440 | tf_op jit(solution)/shard_map/all_to_all | solution.py:25
  38.8 18.4 %all-gather = bf16[4,1,256]{2,1,0:T(2,128)(2,1)S(1)} all-gather(bf16[1,1,256]{2,1,0:T(2,128)(2,1)S(1)} %reshape.212), channel_id=1, replica_groups=mesh['tp_0'=8,'tp_1'=4,'rep_0'=2,'rep_1'=4,'rep_2'=2] {'tp_1'}, dimensions={0}, use_global_device_ids=true | all-gather | bytes 2560 | tf_op jit(solution)/shard_map/all_gather | solution.py:19
  57.3 27.3 %all_gather.24 = bf16[8192]{0:T(1024)(128)(2,1)S(1)} all-gather(bf16[1024]{0:T(1024)(128)(2,1)S(1)} %bitcast.49), channel_id=1, replica_groups=mesh['tp_0'=8,'tp_1'=4,'rep_0'=2,'rep_1'=4,'rep_2'=2] {'tp_0'}, dimensions={0}, use_global_device_ids=true | all-gather | bytes 18432 | tf_op jit(solution)/shard_map/all_gather | solution.py:19
  84.7 0.7 copy.64
  85.4 0.2 broadcast_in_dim.32
  85.6 5.8 %all_to_all.26 = bf16[2,8,512,160]{2,1,3,0:T(8,128)(2,1)S(1)} all-to-all(bf16[2,8,512,160]{2,1,3,0:T(8,128)(2,1)S(1)} %broadcast_in_dim.32), channel_id=1, replica_groups=mesh['tp_0'=8,'tp_1'=4,'rep_0'=2,'rep_1'=4,'rep_2'=2] {'rep_2'}, dimensions={0} | all-to-all | bytes 5242880 | tf_op jit(solution)/shard_map/all_to_all | solution.py:25
  91.4 4.1 %copy.65 = bf16[8,2,512,160]{2,1,0,3:T(2,128)(2,1)S(1)} copy(bf16[8,2,512,160]{2,0,3,1:T(8,128)(2,1)S(1)} %bitcast.46) | data formatting | bytes 5242880 | tf_op jit(solution)/shard_map/transpose | solution.py:37
  95.5 3.6 %reshape_reshape.6 = bf16[8192,160]{0,1:T(8,128)(2,1)} reshape(bf16[8,2,512,160]{2,1,0,3:T(2,128)(2,1)S(1)} %copy.65) | data formatting | bytes 5242880 | tf_op jit(solution)/shard_map/reshape;reshape | solution.py:31
  99.1 10.9 %all-gather.4.cloned.1.call-done = bf16[384,8192]{1,0:T(8,128)(2,1)} async-done(((bf16[384,1024]{1,0:T(8,128)(2,1)}), bf16[384,8192]{1,0:T(8,128)(2,1)}) %all-gather.4.cloned.1.call-update) | async-done | bytes 6291472 | tf_op jit(solution)/shard_map/all_gather | solution.py:19
  110.0 4.3 %fusion.1 = f32[384]{0:T(512)S(1)} fusion(bf16[384,8192]{1,0:T(8,128)(2,1)} %all-gather.4.cloned.1.call-done), kind=kLoop, calls=%fused_computation.3 | loop fusion | flops 9436800 | bytes 6292992 | tf_op jit(solution)/shard_map/reduce_sum | solution.py:92
  114.3 0.3 copy-done.1
  114.6 2.1 fusion.3
  116.7 1.8 fusion.10
  118.5 1.7 convolution_convert_fusion.1
  120.3 1.7 convolution_convert_fusion.2
  122.0 86.5 %all_gather.25 = bf16[512,768]{1,0:T(8,128)(2,1)S(1)} all-gather(bf16[16,768]{1,0:T(8,128)(2,1)S(1)} %pad_maximum_fusion.1), channel_id=1, replica_groups=mesh['tp_0'=8,'tp_1'=4,'rep_0'=2,'rep_1'=4,'rep_2'=2] {'tp_0','tp_1'}, dimensions={0}, use_global_device_ids=true | all-gather | bytes 811008 | tf_op jit(solution)/shard_map/all_gather | solution.py:51
  208.6 0.3 reshape.217
  208.9 0.3 reshape.216
  209.2 0.2 constant_dynamic-slice_fusion
  209.4 0.1 copy.84
  209.6 0.3 fusion.37
  209.9 0.2 fusion.8
  210.3 0.3 convolution_convert_fusion
  210.6 16.4 %all_gather.26 = bf16[384,512]{1,0:T(8,128)(2,1)} all-gather(bf16[384,128]{1,0:T(8,128)(2,1)S(1)} %bitcast.48), channel_id=1, replica_groups=mesh['tp_0'=8,'tp_1'=4,'rep_0'=2,'rep_1'=4,'rep_2'=2] {'tp_1'}, dimensions={1}, use_global_device_ids=true | all-gather | bytes 491520 | tf_op jit(solution)/shard_map/all_gather | solution.py:19
  227.0 1.0 broadcast_in_dim.34
  228.0 4.5 %all-to-all-start.2 = ((bf16[8,256,256]{2,1,0:T(8,128)(2,1)}), bf16[8,256,256]{2,1,0:T(8,128)(2,1)S(1)}, u32[]{:S(2)}, u32[]{:S(2)}) async-start(bf16[8,256,256]{2,1,0:T(8,128)(2,1)} %broadcast_in_dim.34), calls=%async_computation.2 | async-start | bytes 2097152 | tf_op jit(solution)/shard_map/all_to_all | solution.py:25
  232.5 0.2 copy.60
  232.7 9.1 %all-to-all-done.2 = bf16[8,256,256]{2,1,0:T(8,128)(2,1)S(1)} async-done(((bf16[8,256,256]{2,1,0:T(8,128)(2,1)}), bf16[8,256,256]{2,1,0:T(8,128)(2,1)S(1)}, u32[]{:S(2)}, u32[]{:S(2)}) %all-to-all-start.2) | async-done | bytes 1048608 | tf_op jit(solution)/shard_map/all_to_all | solution.py:25
  241.8 0.2 broadcast_in_dim.35
  242.0 5.4 %all_to_all.27 = bf16[2,8,256,256]{3,2,1,0:T(8,128)(2,1)S(1)} all-to-all(bf16[2,8,256,256]{3,2,1,0:T(8,128)(2,1)S(1)} %broadcast_in_dim.35), channel_id=1, replica_groups=mesh['tp_0'=8,'tp_1'=4,'rep_0'=2,'rep_1'=4,'rep_2'=2] {'rep_2'}, dimensions={0} | all-to-all | bytes 4194304 | tf_op jit(solution)/shard_map/all_to_all | solution.py:25
  247.4 0.1 copy.71
  247.6 23.5 %all-gather.6.cloned.1.call-done = bf16[384,4096]{1,0:T(8,128)(2,1)} async-done(((bf16[384,512]{1,0:T(8,128)(2,1)}), bf16[384,4096]{1,0:T(8,128)(2,1)}) %all-gather.6.cloned.1.call-update) | async-done | bytes 3145744 | tf_op jit(solution)/shard_map/all_gather | solution.py:19
  271.0 3.2 %fusion.13 = (f32[384]{0:T(512)S(1)}, bf16[384,256]{0,1:T(8,128)(2,1)S(1)}) fusion(bf16[384,4096]{1,0:T(8,128)(2,1)} %all-gather.6.cloned.1.call-done, bf16[4096,256]{1,0:T(8,128)(2,1)S(1)} %bitcast.47, bf16[384,256]{0,1:T(8,128)(2,1)S(1)} %copy.60), kind=kOutput, calls=%fused_computation.20 | convolution fusion | flops 805895808 | bytes 5637632 | tf_op jit(solution)/shard_map/dot_general | solution.py:141
  274.3 0.9 fusion.14
  275.2 0.1 reshape.153
  275.4 0.9 broadcast_in_dim.37
  276.3 9.4 %all-to-all-start.4 = ((f32[32,1,2688]{2,1,0:T(1,128)}), f32[32,1,2688]{2,1,0:T(1,128)S(1)}, u32[]{:S(2)}, u32[]{:S(2)}) async-start(f32[32,1,2688]{2,1,0:T(1,128)} %broadcast_in_dim.37), calls=%async_computation.4 | async-start | bytes 688128 | tf_op jit(solution)/shard_map/all_to_all | solution.py:25
  285.8 0.8 copy.74
  286.6 14.7 %all-to-all-done.4 = f32[32,1,2688]{2,1,0:T(1,128)S(1)} async-done(((f32[32,1,2688]{2,1,0:T(1,128)}), f32[32,1,2688]{2,1,0:T(1,128)S(1)}, u32[]{:S(2)}, u32[]{:S(2)}) %all-to-all-start.4) | async-done | bytes 344096 | tf_op jit(solution)/shard_map/all_to_all | solution.py:25
  301.4 0.2 reduce_sum.39
  301.6 0.2 reshape.154
  301.8 0.2 multiply_select_fusion
  301.9 0.7 copy.75
  (36 shorter events, 0.7 us)
Async XLA Ops:
  7.2 267.1 %copy-start = (f32[256,6]{0,1:T(8,128)S(1)}, f32[256,6]{0,1:T(8,128)}, u32[]{:S(2)}) copy-start(f32[256,6]{0,1:T(8,128)} %param.19) | copy-start | bytes 18436
  7.2 102.8 %all-gather.4.cloned.1.call-start = ((), (), s32[]{:S(2)}) async-start(), calls=%async_computation.5 | async-start | bytes 7077888 | tf_op jit(solution)/shard_map/all_gather | solution.py:19
  29.6 9.2 %copy-start.6 = (f32[256]{0:T(256)S(1)}, f32[256]{0:T(256)}, u32[]{:S(2)}) copy-start(f32[256]{0:T(256)} %param.13) | copy-start | bytes 3076
  29.6 54.9 %copy-start.7 = (s32[2]{0:T(128)S(1)}, s32[2]{0:T(128)}, u32[]{:S(2)}) copy-start(s32[2]{0:T(128)} %param.12) | copy-start | bytes 28
  33.7 51.0 %all-to-all-start = ((bf16[8,512,160]{1,2,0:T(8,128)(2,1)}), bf16[8,512,160]{1,2,0:T(8,128)(2,1)S(1)}, u32[]{:S(2)}, u32[]{:S(2)}) async-start(bf16[8,512,160]{1,2,0:T(8,128)(2,1)} %broadcast_in_dim.31), calls=%async_computation | async-start | bytes 2621440 | tf_op jit(solution)/shard_map/all_to_all | solution.py:25
  38.8 232.2 %all-gather.6.cloned.1.call-start = ((), (), s32[]{:S(2)}) async-start(), calls=%async_computation.6 | async-start | bytes 3538944 | tf_op jit(solution)/shard_map/all_gather | solution.py:19
  110.0 4.6 %copy-start.1 = (bf16[384,8192]{1,0:T(8,128)(2,1)S(1)}, bf16[384,8192]{1,0:T(8,128)(2,1)}, u32[]{:S(2)}) copy-start(bf16[384,8192]{1,0:T(8,128)(2,1)} %all-gather.4.cloned.1.call-done) | copy-start | bytes 18874372
  114.6 2.1 copy-start.2
  208.9 18.1 %copy-start.4 = (bf16[256,256]{1,0:T(8,128)(2,1)S(1)}, bf16[256,256]{1,0:T(8,128)(2,1)}, u32[]{:S(2)}) copy-start(bf16[256,256]{1,0:T(8,128)(2,1)} %param.17) | copy-start | bytes 393220
  210.1 22.4 %copy-start.3 = (bf16[384,256]{1,0:T(8,128)(2,1)S(1)}, bf16[384,256]{1,0:T(8,128)(2,1)}, u32[]{:S(2)}) copy-start(bf16[384,256]{1,0:T(8,128)(2,1)} %param.11) | copy-start | bytes 589828
  228.0 13.8 %all-to-all-start.2 = ((bf16[8,256,256]{2,1,0:T(8,128)(2,1)}), bf16[8,256,256]{2,1,0:T(8,128)(2,1)S(1)}, u32[]{:S(2)}, u32[]{:S(2)}) async-start(bf16[8,256,256]{2,1,0:T(8,128)(2,1)} %broadcast_in_dim.34), calls=%async_computation.2 | async-start | bytes 2097152 | tf_op jit(solution)/shard_map/all_to_all | solution.py:25
  271.0 3.3 %copy-start.5 = (f32[256]{0:T(256)S(1)}, f32[256]{0:T(256)}, u32[]{:S(2)}) copy-start(f32[256]{0:T(256)} %param.18) | copy-start | bytes 3076
  276.3 25.1 %all-to-all-start.4 = ((f32[32,1,2688]{2,1,0:T(1,128)}), f32[32,1,2688]{2,1,0:T(1,128)S(1)}, u32[]{:S(2)}, u32[]{:S(2)}) async-start(f32[32,1,2688]{2,1,0:T(1,128)} %broadcast_in_dim.37), calls=%async_computation.4 | async-start | bytes 688128 | tf_op jit(solution)/shard_map/all_to_all | solution.py:25
Sparse Core Ops, SparseCore 0:
  29.8 80.1 all-gather.3
  227.1 43.9 all-gather.5
where the time goes:
time: 310 us; the launch traced here: 309 us
  blocking collectives  182 us (59%)
  waiting for transfers between devices  58.2 us (19%)
  starting transfers between devices  19.1 us (6%)
  local copies, waits for them, and re-layouts  17.5 us (6%)
  between operations  14.3 us (5%)
  matrix products  10.2 us (3%)
  other arithmetic  7.93 us (3%)
    all_gather x1, blocking collectives, turned_gather(): whole = lax.all_gather(both, axis, axis=0, tiled=True)  86.5 us
    all_gather x4, blocking collectives, whole_of(): nearer = lax.all_gather(x, axes[-1], axis=dim, tiled=True)  84.4 us
    all_gather x2, waiting for transfers between devices, whole_of(): nearer = lax.all_gather(x, axes[-1], axis=dim, tiled=True)  34.3 us
    all_to_all x3, waiting for transfers between devices, copy_for_each(): lax.all_to_all(jnp.broadcast_to(x[None], (count, *x.shape)), axis, 0, 0,...  23.8 us
    all_to_all x3, starting transfers between devices, copy_for_each(): lax.all_to_all(jnp.broadcast_to(x[None], (count, *x.shape)), axis, 0, 0,...  19 us
    all_to_all x2, blocking collectives, copy_for_each(): lax.all_to_all(jnp.broadcast_to(x[None], (count, *x.shape)), axis, 0, 0,...  11.3 us
  transfers between devices with their start and end apart: 5, of which 4 were waited for; matrix products, arithmetic and copies ran while one was open for 5% of the time, Pallas kernels for 0%

commit v1 on v0

v1 whole, which is shorter than its diff:
```python
import jax
import jax.numpy as jnp
from jax import lax
from jax.experimental import pallas as pl
from jax.experimental.pallas import tpu as pltpu
from jax.sharding import Mesh
from jax.sharding import PartitionSpec as P

HEAD = 128
EPS = 1e-05
WIDTH = 8192
NZ, NYH, NYL, NX, NC = 8, 4, 2, 4, 2
TP = ("z", "yh")
REP = ("yl", "x", "c")
VMEM = 48 * 1024 * 1024
F32 = jnp.float32
BF16 = jnp.bfloat16


def copies(x, axis, count):
    return lax.all_to_all(jnp.broadcast_to(x[None], (count, *x.shape)), axis, 0, 0)


def head_perm(k):
    pairs = []
    for yh in range(NYH):
        for c in range(NC):
            b = (yh // 2 + k) % 2
            pairs.append((yh * NC + c, (2 * c + b) * NC + yh % 2))
    return pairs


def kv_perm(k):
    pairs = []
    for z in range(NZ):
        for yh in range(NYH):
            for c in range(NC):
                zn, yn = (z % 2) * 4 + yh, z // 2
                b = (yn // 2 + k) % 2
                dest = (zn * NYH + 2 * c + b) * NC + yn % 2
                pairs.append(((z * NYH + yh) * NC + c, dest))
    return pairs


def split_sum(total):
    high = total.astype(BF16)
    low = (total - high.astype(F32)).astype(BF16)
    return high, low


def project_kernel(core_ref, x_ref, own_ref, other_ref, q_ref, kv_ref, qacc, kvacc):
    step = pl.program_id(0)

    @pl.when(step == 0)
    def _():
        qacc[...] = jnp.zeros_like(qacc)
        kvacc[...] = jnp.zeros_like(kvacc)

    x = x_ref[0]
    for side, w_ref in enumerate((own_ref, other_ref)):
        q = jnp.concatenate(
            [
                jnp.concatenate([w_ref[0, 0:128, 0:128], w_ref[0, 0:128, 128:256]], axis=0),
                jnp.concatenate([w_ref[0, 128:256, 0:128], w_ref[0, 128:256, 128:256]], axis=0),
            ],
            axis=1,
        )
        qacc[side] += jnp.dot(x, q, preferred_element_type=F32)
        kvacc[side] += lax.dot_general(
            w_ref[0, 256:320, :], x, (((1,), (1,)), ((), ())), preferred_element_type=F32
        )

    @pl.when(step == NZ - 1)
    def _():
        core = core_ref[0]
        for side in range(2):
            d = core if side == 0 else 1 - core
            for hi in range(2):
                q_ref[2 * hi + d] = qacc[side, :, hi * 128 : (hi + 1) * 128].astype(BF16)
                kv_ref[2 * hi + d] = kvacc[side, hi * 32 : (hi + 1) * 32, :].astype(BF16)


def project(core, x, own, other):
    rows = x.shape[1]
    return pl.pallas_call(
        project_kernel,
        grid=(NZ,),
        in_specs=[
            pl.BlockSpec(memory_space=pltpu.SMEM),
            pl.BlockSpec((1, rows, 256), lambda i: (i, 0, 0)),
            pl.BlockSpec((1, 320, 256), lambda i: (i, 0, 0)),
            pl.BlockSpec((1, 320, 256), lambda i: (i, 0, 0)),
        ],
        out_specs=[
            pl.BlockSpec((4, rows, 128), lambda i: (0, 0, 0)),
            pl.BlockSpec((4, 32, rows), lambda i: (0, 0, 0)),
        ],
        out_shape=[
            jax.ShapeDtypeStruct((4, rows, 128), BF16),
            jax.ShapeDtypeStruct((4, 32, rows), BF16),
        ],
        scratch_shapes=[pltpu.VMEM((2, rows, 256), F32), pltpu.VMEM((2, 64, rows), F32)],
        compiler_params=pltpu.CompilerParams(vmem_limit_bytes=VMEM),
        cost_estimate=pl.CostEstimate(flops=2 * rows * 2048 * 640, bytes_accessed=5_000_000, transcendentals=0),
    )(core, x, own, other)


def attention_kernel(len_ref, q_ref, kv_ref, out_ref):
    rows = q_ref.shape[1]
    half = rows // 2
    kv = kv_ref[...]
    stats = jnp.sum(kv[:, 32:48, :].astype(F32), axis=0)
    scale = lax.rsqrt((stats[0:1] + stats[1:2]) * (1.0 / WIDTH) + EPS)
    wide = jnp.broadcast_to(scale, (HEAD, rows))
    key = (kv[:, 0:16, :].reshape(HEAD, rows).astype(F32) * wide).astype(BF16)
    value = (kv[:, 16:32, :].reshape(HEAD, rows).astype(F32) * wide).astype(BF16)
    q = jnp.sum(q_ref[...].astype(F32), axis=0)
    q = (q * wide.T).astype(BF16)
    scores = jnp.dot(q, key, preferred_element_type=F32) * (1.0 / HEAD**0.5)
    i = lax.broadcasted_iota(jnp.int32, (rows, rows), 0)
    j = lax.broadcasted_iota(jnp.int32, (rows, rows), 1)
    limit = jnp.where(j < half, len_ref[0], half + len_ref[1])
    allowed = (j <= i) & (j < limit) & ((i < half) | (j >= half))
    scores = jnp.where(allowed, scores, F32(-1e30))
    scores = scores - jnp.max(scores, axis=1, keepdims=True)
    expo = jnp.exp(scores)
    probs = (expo / jnp.sum(expo, axis=1, keepdims=True)).astype(BF16)
    out = lax.dot_general(probs, value, (((1,), (1,)), ((), ())), preferred_element_type=F32)
    out_ref[...] = out.astype(BF16)


def attention(lengths, q, kv):
    rows = q.shape[1]
    return pl.pallas_call(
        attention_kernel,
        in_specs=[
            pl.BlockSpec(memory_space=pltpu.SMEM),
            pl.BlockSpec(memory_space=pltpu.VMEM),
            pl.BlockSpec(memory_space=pltpu.VMEM),
        ],
        out_specs=pl.BlockSpec(memory_space=pltpu.VMEM),
        out_shape=jax.ShapeDtypeStruct((rows, HEAD), BF16),
        compiler_params=pltpu.CompilerParams(vmem_limit_bytes=VMEM),
        cost_estimate=pl.CostEstimate(flops=4 * rows * rows * 128, bytes_accessed=800_000, transcendentals=rows * rows),
    )(lengths, q, kv)


def output_kernel(core_ref, a_ref, own_ref, other_ref, out_ref, acc):
    step = pl.program_id(0)

    @pl.when(step == 0)
    def _():
        acc[...] = jnp.zeros_like(acc)

    a = jnp.concatenate([a_ref[0], a_ref[1]], axis=1)
    for side, w_ref in enumerate((own_ref, other_ref)):
        for hi in range(2):
            w = jnp.concatenate(
                [w_ref[0, hi * 128 : (hi + 1) * 128], w_ref[1, hi * 128 : (hi + 1) * 128]], axis=0
            )
            acc[side, hi] += jnp.dot(a, w, preferred_element_type=F32)

    @pl.when(step == NZ // 2 - 1)
    def _():
        core = core_ref[0]
        for side in range(2):
            d = core if side == 0 else 1 - core
            for hi in range(2):
                out_ref[2 * hi + d] = acc[side, hi].astype(BF16)


def output_products(core, attended, own, other):
    rows = attended.shape[1]
    return pl.pallas_call(
        output_kernel,
        grid=(NZ // 2,),
        in_specs=[
            pl.BlockSpec(memory_space=pltpu.SMEM),
            pl.BlockSpec((2, rows, 128), lambda i: (i, 0, 0)),
            pl.BlockSpec((2, 256, 256), lambda i: (i, 0, 0)),
            pl.BlockSpec((2, 256, 256), lambda i: (i, 0, 0)),
        ],
        out_specs=pl.BlockSpec((4, rows, 256), lambda i: (0, 0, 0)),
        out_shape=jax.ShapeDtypeStruct((4, rows, 256), BF16),
        scratch_shapes=[pltpu.VMEM((2, 2, rows, 256), F32)],
        compiler_params=pltpu.CompilerParams(vmem_limit_bytes=VMEM),
        cost_estimate=pl.CostEstimate(flops=2 * rows * 1024 * 1024, bytes_accessed=4_000_000, transcendentals=0),
    )(core, attended, own, other)


def resid_kernel(p_ref, x_ref, head_ref, resid_ref, stat_ref):
    update = jnp.sum(p_ref[...].astype(F32), axis=0)
    resid = (x_ref[...].astype(F32) + update).astype(BF16)
    resid_ref[...] = resid
    r = resid.astype(F32)
    nt = (((1,), (1,)), ((), ()))
    scores = lax.dot_general(
        head_ref[...], r, nt, precision=lax.Precision.HIGHEST, preferred_element_type=F32
    )
    ones = jnp.ones((8, r.shape[1]), F32)
    squares = lax.dot_general(
        ones, r * r, nt, precision=lax.Precision.HIGHEST, preferred_element_type=F32
    )
    row = lax.broadcasted_iota(jnp.int32, scores.shape, 0)
    stat_ref[...] = jnp.where(row < 6, scores, squares)


def resid_and_stats(parts, tokens, heads):
    rows, cols = tokens.shape
    return pl.pallas_call(
        resid_kernel,
        in_specs=[pl.BlockSpec(memory_space=pltpu.VMEM)] * 3,
        out_specs=[pl.BlockSpec(memory_space=pltpu.VMEM)] * 2,
        out_shape=[
            jax.ShapeDtypeStruct((rows, cols), BF16),
            jax.ShapeDtypeStruct((8, rows), F32),
        ],
        compiler_params=pltpu.CompilerParams(vmem_limit_bytes=VMEM),
        cost_estimate=pl.CostEstimate(flops=2 * rows * cols * 96, bytes_accessed=1_200_000, transcendentals=0),
    )(parts, tokens, heads)


def local(
    tokens,
    row_lengths,
    attn_gain,
    query_weight,
    key_weight,
    value_matrix,
    output_weight,
    final_gain,
    value_head,
):
    rows = tokens.shape[0]
    z, yh, c = lax.axis_index("z"), lax.axis_index("yh"), lax.axis_index("c")
    core = c.astype(jnp.int32)[None]

    xf = tokens.astype(F32)
    gained = (xf * attn_gain[None, :]).astype(BF16)
    squares = jnp.sum(xf * xf, axis=1)

    with jax.named_scope("weights_out"):
        blocks = []
        for b in range(2):
            q = query_weight[256 * b : 256 * (b + 1)]
            q = jnp.concatenate([q[:128], q[128:]], axis=1)
            blocks.append(jnp.concatenate([q, output_weight[128 * b : 128 * (b + 1)]], axis=0))
        kv_t = jnp.concatenate([key_weight.T, value_matrix.T], axis=0)
        kv_blocks = [kv_t[:, :256], kv_t[:, 256:]]
        first = (yh // 2) == 0
        kv_first = (z // 4) == 0
        came = [
            lax.ppermute(
                jnp.where(first, blocks[k], blocks[1 - k]), ("yh", "c"), head_perm(k)
            )
            for k in range(2)
        ]
        kv_came = [
            lax.ppermute(
                jnp.where(kv_first, kv_blocks[k], kv_blocks[1 - k]), ("z", "yh", "c"), kv_perm(k)
            )
            for k in range(2)
        ]
        even = (yh % 2) == 0
        w = [jnp.where(even, came[k], came[1 - k]) for k in range(2)]
        kvw = [jnp.where(even, kv_came[k], kv_came[1 - k]) for k in range(2)]
        qkv_part = jnp.concatenate([w[0][:128], w[1][:128], kvw[0], kvw[1]], axis=0)
        out_part = jnp.concatenate([w[0][128:], w[1][128:]], axis=0)

    swap = [(0, 1), (1, 0)]
    with jax.named_scope("tokens_z"):
        x_all = copies(gained, "z", NZ)
    with jax.named_scope("qkv_rep"):
        qkv_own = copies(qkv_part, ("yl", "x"), NYL * NX)
        qkv_other = lax.ppermute(qkv_own, "c", swap)
    with jax.named_scope("out_rep"):
        out_own = copies(out_part, ("yl", "x"), NYL * NX)
        out_other = lax.ppermute(out_own, "c", swap)

    q_parts, kv_parts = project(core, x_all, qkv_own, qkv_other)

    with jax.named_scope("kv_sum"):
        high, low = split_sum(squares)
        stat = jnp.concatenate([high[None], low[None], jnp.zeros((14, rows), BF16)], axis=0)
        kv_send = jnp.concatenate([kv_parts, jnp.broadcast_to(stat[None], (NYH, 16, rows))], axis=1)
        kv_sum = lax.all_to_all(kv_send, "yh", 0, 0).astype(F32).sum(axis=0)
        high, low = split_sum(kv_sum[32] + kv_sum[33])
        stat = jnp.concatenate([high[None], low[None], jnp.zeros((14, rows), BF16)], axis=0)
        kv_mine = jnp.concatenate([kv_sum[:32].astype(BF16), stat], axis=0)
    with jax.named_scope("kv_z"):
        kv_all = copies(kv_mine, "z", NZ)
    with jax.named_scope("q_sum"):
        q_all = lax.all_to_all(q_parts, "yh", 0, 0)

    attended = attention(row_lengths, q_all, kv_all)

    with jax.named_scope("attended_z"):
        attended_all = copies(attended, "z", NZ)
    parts = output_products(core, attended_all, out_own, out_other)
    with jax.named_scope("out_sum"):
        parts = lax.all_to_all(parts, "yh", 0, 0)

    heads = jnp.concatenate([(final_gain[:, None] * value_head).T, jnp.zeros((2, tokens.shape[1]), F32)], axis=0)
    resid_out, stat = resid_and_stats(parts, tokens, heads)

    with jax.named_scope("stat_yh"):
        stat = copies(stat, "yh", NYH).sum(axis=0)
    with jax.named_scope("stat_z"):
        stat = copies(stat, "z", NZ).sum(axis=0)
    logits = stat[:6] * lax.rsqrt(stat[6] / WIDTH + EPS)[None, :]
    position = jnp.arange(rows // row_lengths.shape[0], dtype=jnp.int32)
    live = (position[None, :] < row_lengths[:, None]).reshape(1, rows)
    scores = jnp.where(live, logits, F32(0.0)).T
    return resid_out, scores


def solution(mesh):
    split = Mesh(mesh.devices.reshape(NZ, NYH, NYL, NX, NC), TP + REP)
    in_specs = (
        P(REP, TP),
        P(REP),
        P(TP),
        P(REP, TP),
        P(REP, TP),
        P(REP, TP),
        P(REP, TP),
        P(TP),
        P(TP, None),
    )
    out_specs = (P(REP, TP), P(REP, None))
    return jax.shard_map(local, mesh=split, in_specs=in_specs, out_specs=out_specs, check_vma=False)
```

time: 310 us -> 251 us (0.81)
  blocking collectives: 182 us -> 22.9 us
  waiting for transfers between devices: 58.2 us -> 138 us
  starting transfers between devices: 19.1 us -> 66.6 us
  between operations: 14.3 us -> 0.93 us
  Pallas kernels: 0 us -> 11.1 us
  matrix products: 10.2 us -> 0 us
  local copies, waits for them, and re-layouts: 17.5 us -> 7.71 us
  other arithmetic: 7.93 us -> 1.87 us
    all_gather x5 -> x0, blocking collectives: 171 us -> none  [the longest x1 86.5 us: turned_gather(): whole = lax.all_gather(both, axis, axis=0, tiled=True)]
    all_to_all x3 -> x8, waiting for transfers between devices: 23.8 us -> 127 us  [the longest x6 94.8 us: copies(): lax.all_to_all(jnp.broadcast_to(x[None], (count, *x.shape)), axis, 0, 0)]
    all_gather x2 -> x0, waiting for transfers between devices: 34.3 us -> none  [whole_of(): nearer = lax.all_gather(x, axes[-1], axis=dim, tiled=True)]
    ppermute x0 -> x6, starting transfers between devices: none -> 24.3 us  [the longest x2 11.9 us: local(): lax.ppermute(jnp.where(first, blocks[k], blocks[1 - k]), ('yh', 'c'), hea...]
    all_to_all x3 -> x8, starting transfers between devices: 19 us -> 42.2 us  [the longest x6 30.9 us: copies(): lax.all_to_all(jnp.broadcast_to(x[None], (count, *x.shape)), axis, 0, 0)]
    ppermute x0 -> x6, waiting for transfers between devices: none -> 11.9 us  [the longest x2 9.24 us: local(): lax.ppermute(jnp.where(first, blocks[k], blocks[1 - k]), ('yh', 'c'), hea...]
    all_to_all x2, blocking collectives: 11.3 us -> 22.9 us  [the longest x1 11.6 us: copies(): lax.all_to_all(jnp.broadcast_to(x[None], (count, *x.shape)), axis, 0, 0)]
    pallas_call x0 -> x4, Pallas kernels: none -> 11.1 us  [the longest x1 6.49 us: project(): pl.pallas_call(project_kernel, grid=(NZ,), in_specs=[pl.BlockSpec(memory_...]
  transfers between devices with their start and end apart: 5 -> 14, of which waited for: 4 -> 10; matrix products, arithmetic and copies ran while one was open for 5% -> 1% of each run, Pallas kernels for 0% -> 0%
where the time goes in v1:
time: 251 us; the launch traced here: 250 us
  waiting for transfers between devices  138 us (55%)
  starting transfers between devices  66.6 us (27%)
  blocking collectives  22.9 us (9%)
  Pallas kernels  11.1 us (4%)
  local copies, waits for them, and re-layouts  7.71 us (3%)
    all_to_all x6, waiting for transfers between devices, copies(): lax.all_to_all(jnp.broadcast_to(x[None], (count, *x.shape)), axis, 0, 0)  94.8 us
    all_to_all x6, starting transfers between devices, copies(): lax.all_to_all(jnp.broadcast_to(x[None], (count, *x.shape)), axis, 0, 0)  30.9 us
    all_to_all x1, waiting for transfers between devices, local(): parts = lax.all_to_all(parts, 'yh', 0, 0)  21.4 us
    ppermute x2, starting transfers between devices, local(): lax.ppermute(jnp.where(first, blocks[k], blocks[1 - k]), ('yh', 'c'), hea...  11.9 us
    all_to_all x1, blocking collectives, copies(): lax.all_to_all(jnp.broadcast_to(x[None], (count, *x.shape)), axis, 0, 0)  11.6 us
    all_to_all x1, blocking collectives, local(): kv_sum = lax.all_to_all(kv_send, 'yh', 0, 0).astype(F32).sum(axis=0)  11.3 us
    all_to_all x1, waiting for transfers between devices, local(): q_all = lax.all_to_all(q_parts, 'yh', 0, 0)  10.3 us
    ppermute x2, waiting for transfers between devices, local(): lax.ppermute(jnp.where(first, blocks[k], blocks[1 - k]), ('yh', 'c'), hea...  9.24 us
  transfers between devices with their start and end apart: 14, of which 10 were waited for; matrix products, arithmetic and copies ran while one was open for 1% of the time, Pallas kernels for 0%

profile of v1, /device:TPU:6, one launch (start us, length us, event | category | flops | bytes accessed | tf_op | source)
XLA Modules:
  0.0 249.6 jit_solution(7624196351648324783)
XLA Ops:
  0.6 0.8 broadcast_select_fusion.5
  1.4 0.7 collective-permute-start.2
  2.1 7.9 %collective-permute-start.3 = (bf16[32,256]{1,0:T(8,128)(2,1)S(1)}, bf16[32,256]{1,0:T(8,128)(2,1)S(1)}, u32[]{:S(2)}, u32[]{:S(2)}) collective-permute-start(bf16[32,256]{1,0:T(8,128)(2,1)S(1)} %get-tuple-element.31), channel_id=1, source_target_pairs={{0,16},{1,48},{16,80},{17,112},{32,144},{33,176},{48,208},{49,240}... | collective-permute-start | bytes 49160 | tf_op jit(solution)/shard_map/weights_out/ppermute | solution.py:259
  10.0 0.9 fusion.12
  10.9 0.8 fusion.11
  11.7 0.1 broadcast_select_fusion.1
  11.8 0.7 collective-permute-start
  12.5 11.3 %collective-permute-start.1 = (bf16[256,256]{1,0:T(8,128)(2,1)S(1)}, bf16[256,256]{1,0:T(8,128)(2,1)S(1)}, u32[]{:S(2)}, u32[]{:S(2)}) collective-permute-start(bf16[256,256]{1,0:T(8,128)(2,1)S(1)} %get-tuple-element.13), channel_id=1, source_target_pairs={{0,16},{1,48},{16,17},{17,49},{32,0},{33,32},{48,1},{49,33},{2,18}... | collective-permute-start | bytes 393224 | tf_op jit(solution)/shard_map/weights_out/ppermute | solution.py:253
  23.8 0.0 collective-permute-done.2
  23.8 0.0 collective-permute-done.3
  23.8 0.0 collective-permute-done
  23.8 9.2 %collective-permute-done.1 = bf16[256,256]{1,0:T(8,128)(2,1)S(1)} collective-permute-done((bf16[256,256]{1,0:T(8,128)(2,1)S(1)}, bf16[256,256]{1,0:T(8,128)(2,1)S(1)}, u32[]{:S(2)}, u32[]{:S(2)}) %collective-permute-start.1) | collective-permute-done | bytes 131104 | tf_op jit(solution)/shard_map/weights_out/ppermute | solution.py:253
  33.1 1.2 broadcast_in_dim.28
  34.3 4.9 %all-to-all-start.1 = ((bf16[8,320,256]{2,1,0:T(8,128)(2,1)}), bf16[8,320,256]{2,1,0:T(8,128)(2,1)S(1)}, u32[]{:S(2)}, u32[]{:S(2)}) async-start(bf16[8,320,256]{2,1,0:T(8,128)(2,1)} %broadcast_in_dim.28), calls=%async_computation.1 | async-start | bytes 2621440 | tf_op jit(solution)/shard_map/qkv_rep/all_to_all | solution.py:21
  39.2 0.1 fusion.1
  39.4 16.0 %all-to-all-done.1.own_ref = bf16[8,320,256]{2,1,0:T(8,128)(2,1)S(1)} async-done(((bf16[8,320,256]{2,1,0:T(8,128)(2,1)}), bf16[8,320,256]{2,1,0:T(8,128)(2,1)S(1)}, u32[]{:S(2)}, u32[]{:S(2)}) %all-to-all-start.1) | async-done | bytes 1310752 | tf_op jit(solution)/shard_map/qkv_rep/all_to_all | solution.py:21
  55.4 1.3 broadcast_in_dim.27
  56.6 8.9 %all-to-all-start = ((bf16[8,384,256]{2,1,0:T(8,128)(2,1)}), bf16[8,384,256]{2,1,0:T(8,128)(2,1)S(1)}, u32[]{:S(2)}, u32[]{:S(2)}) async-start(bf16[8,384,256]{2,1,0:T(8,128)(2,1)} %broadcast_in_dim.27), calls=%async_computation | async-start | bytes 3145728 | tf_op jit(solution)/shard_map/tokens_z/all_to_all | solution.py:21
  65.5 1.9 collective-permute-start.4
  67.5 37.2 %all-to-all-done.x_ref = bf16[8,384,256]{2,1,0:T(8,128)(2,1)S(1)} async-done(((bf16[8,384,256]{2,1,0:T(8,128)(2,1)}), bf16[8,384,256]{2,1,0:T(8,128)(2,1)S(1)}, u32[]{:S(2)}, u32[]{:S(2)}) %all-to-all-start) | async-done | bytes 1572896 | tf_op jit(solution)/shard_map/tokens_z/all_to_all | solution.py:21
  104.7 0.0 collective-permute-done.4.other_ref
  104.7 6.5 %shard_map.104 = (bf16[4,384,128]{2,1,0:T(8,128)(2,1)}, bf16[4,32,384]{2,1,0:T(8,128)(2,1)S(1)}) custom-call(s32[1]{0:T(128)} %bitcast.core_ref, bf16[8,384,256]{2,1,0:T(8,128)(2,1)S(1)} %all-to-all-done.x_ref, bf16[8,320,256]{2,1,0:T(8,128)(2,1)S(1)} %all-to-all-done.1.own_ref, bf16[8,320,256]{2,1,0:T(8,128)(2,1)} %collective-permute-done.4.other_ref), custom_call_target="tpu_custom_call" | custom-call | flops 1006632960 | bytes 5000000 | tf_op jit(solution)/shard_map/pallas_call | solution.py:85
  111.2 11.3 %all_to_all.50 = bf16[4,48,384]{2,1,0:T(8,128)(2,1)S(1)} all-to-all(bf16[4,48,384]{2,1,0:T(8,128)(2,1)S(1)} %pad_maximum_fusion.1), channel_id=1, replica_groups=mesh['z'=8,'yh'=4,'yl'=2,'x'=4,'c'=2] {'yh'}, dimensions={0} | all-to-all | bytes 294912 | tf_op jit(solution)/shard_map/kv_sum/all_to_all | solution.py:286
  122.5 3.5 %all-to-all-start.2 = ((bf16[4,384,128]{2,1,0:T(8,128)(2,1)}), bf16[4,384,128]{2,1,0:T(8,128)(2,1)S(1)}, u32[]{:S(2)}, u32[]{:S(2)}) async-start(bf16[4,384,128]{2,1,0:T(8,128)(2,1)} %get-tuple-element.6), calls=%async_computation.2 | async-start | bytes 786432 | tf_op jit(solution)/shard_map/q_sum/all_to_all | solution.py:293
  126.1 10.3 %all-to-all-done.2.q_ref = bf16[4,384,128]{2,1,0:T(8,128)(2,1)S(1)} async-done(((bf16[4,384,128]{2,1,0:T(8,128)(2,1)}), bf16[4,384,128]{2,1,0:T(8,128)(2,1)S(1)}, u32[]{:S(2)}, u32[]{:S(2)}) %all-to-all-start.2) | async-done | bytes 393248 | tf_op jit(solution)/shard_map/q_sum/all_to_all | solution.py:293
  136.4 0.7 broadcast_in_dim.30
  137.2 3.7 %all-to-all-start.4 = ((bf16[8,48,384]{2,1,0:T(8,128)(2,1)}), bf16[8,48,384]{2,1,0:T(8,128)(2,1)S(1)}, u32[]{:S(2)}, u32[]{:S(2)}) async-start(bf16[8,48,384]{2,1,0:T(8,128)(2,1)} %broadcast_in_dim.30), calls=%async_computation.4 | async-start | bytes 589824 | tf_op jit(solution)/shard_map/kv_z/all_to_all | solution.py:21
  140.8 10.8 %all-to-all-done.4.kv_ref = bf16[8,48,384]{2,1,0:T(8,128)(2,1)S(1)} async-done(((bf16[8,48,384]{2,1,0:T(8,128)(2,1)}), bf16[8,48,384]{2,1,0:T(8,128)(2,1)S(1)}, u32[]{:S(2)}, u32[]{:S(2)}) %all-to-all-start.4) | async-done | bytes 294944 | tf_op jit(solution)/shard_map/kv_z/all_to_all | solution.py:21
  151.7 1.1 broadcast_in_dim.32
  152.7 6.6 %all-to-all-start.6 = ((bf16[8,256,256]{2,1,0:T(8,128)(2,1)}), bf16[8,256,256]{2,1,0:T(8,128)(2,1)S(1)}, u32[]{:S(2)}, u32[]{:S(2)}) async-start(bf16[8,256,256]{2,1,0:T(8,128)(2,1)} %broadcast_in_dim.32), calls=%async_computation.6 | async-start | bytes 2097152 | tf_op jit(solution)/shard_map/out_rep/all_to_all | solution.py:21
  159.3 1.2 shard_map.105
  160.5 8.3 %all-to-all-done.6.own_ref = bf16[8,256,256]{2,1,0:T(8,128)(2,1)S(1)} async-done(((bf16[8,256,256]{2,1,0:T(8,128)(2,1)}), bf16[8,256,256]{2,1,0:T(8,128)(2,1)S(1)}, u32[]{:S(2)}, u32[]{:S(2)}) %all-to-all-start.6) | async-done | bytes 1048608 | tf_op jit(solution)/shard_map/out_rep/all_to_all | solution.py:21
  168.8 1.0 broadcast_in_dim.31
  169.8 3.5 %all-to-all-start.5 = ((bf16[8,384,128]{2,1,0:T(8,128)(2,1)}), bf16[8,384,128]{2,1,0:T(8,128)(2,1)S(1)}, u32[]{:S(2)}, u32[]{:S(2)}) async-start(bf16[8,384,128]{2,1,0:T(8,128)(2,1)} %broadcast_in_dim.31), calls=%async_computation.5 | async-start | bytes 1572864 | tf_op jit(solution)/shard_map/attended_z/all_to_all | solution.py:21
  173.4 1.9 collective-permute-start.5
  175.3 2.6 %collective-permute-done.5.other_ref = bf16[8,256,256]{2,1,0:T(8,128)(2,1)S(1)} collective-permute-done((bf16[8,256,256]{2,1,0:T(8,128)(2,1)S(1)}, bf16[8,256,256]{2,1,0:T(8,128)(2,1)S(1)}, u32[]{:S(2)}, u32[]{:S(2)}) %collective-permute-start.5) | collective-permute-done | bytes 1048608 | tf_op jit(solution)/shard_map/out_rep/ppermute | solution.py:278
  177.9 14.0 %all-to-all-done.5.a_ref = bf16[8,384,128]{2,1,0:T(8,128)(2,1)S(1)} async-done(((bf16[8,384,128]{2,1,0:T(8,128)(2,1)}), bf16[8,384,128]{2,1,0:T(8,128)(2,1)S(1)}, u32[]{:S(2)}, u32[]{:S(2)}) %all-to-all-start.5) | async-done | bytes 786464 | tf_op jit(solution)/shard_map/attended_z/all_to_all | solution.py:21
  191.9 2.6 %shard_map.106 = bf16[4,384,256]{2,1,0:T(8,128)(2,1)} custom-call(s32[1]{0:T(128)} %bitcast.core_ref, bf16[8,384,128]{2,1,0:T(8,128)(2,1)S(1)} %all-to-all-done.5.a_ref, bf16[8,256,256]{2,1,0:T(8,128)(2,1)S(1)} %all-to-all-done.6.own_ref, bf16[8,256,256]{2,1,0:T(8,128)(2,1)S(1)} %collective-permute-done.5.other_ref), custom_call_target="tpu_custom_call" | custom-call | flops 805306368 | bytes 4000000 | tf_op jit(solution)/shard_map/pallas_call | solution.py:174
  194.5 7.8 %all-to-all-start.7 = ((bf16[4,384,256]{2,1,0:T(8,128)(2,1)}), bf16[4,384,256]{2,1,0:T(8,128)(2,1)S(1)}, u32[]{:S(2)}, u32[]{:S(2)}) async-start(bf16[4,384,256]{2,1,0:T(8,128)(2,1)} %shard_map.106), calls=%async_computation.7 | async-start | bytes 1572864 | tf_op jit(solution)/shard_map/out_sum/all_to_all | solution.py:301
  202.4 21.4 %all-to-all-done.7.p_ref = bf16[4,384,256]{2,1,0:T(8,128)(2,1)S(1)} async-done(((bf16[4,384,256]{2,1,0:T(8,128)(2,1)}), bf16[4,384,256]{2,1,0:T(8,128)(2,1)S(1)}, u32[]{:S(2)}, u32[]{:S(2)}) %all-to-all-start.7) | async-done | bytes 786464 | tf_op jit(solution)/shard_map/out_sum/all_to_all | solution.py:301
  223.8 0.8 shard_map.107
  224.7 11.6 %all_to_all.51 = f32[4,8,384]{2,1,0:T(8,128)S(1)} all-to-all(f32[4,8,384]{2,1,0:T(8,128)S(1)} %broadcast_in_dim.34), channel_id=1, replica_groups=mesh['z'=8,'yh'=4,'yl'=2,'x'=4,'c'=2] {'yh'}, dimensions={0} | all-to-all | bytes 98304 | tf_op jit(solution)/shard_map/stat_yh/all_to_all | solution.py:21
  236.3 0.6 broadcast_in_dim.35
  236.9 3.4 %all-to-all-start.9 = ((f32[8,8,384]{2,1,0:T(8,128)}), f32[8,8,384]{2,1,0:T(8,128)S(1)}, u32[]{:S(2)}, u32[]{:S(2)}) async-start(f32[8,8,384]{2,1,0:T(8,128)} %broadcast_in_dim.35), calls=%async_computation.9 | async-start | bytes 196608 | tf_op jit(solution)/shard_map/stat_z/all_to_all | solution.py:21
  240.3 0.1 iota_compare_fusion
  240.4 0.1 lt.30
  240.5 8.5 %all-to-all-done.9 = f32[8,8,384]{2,1,0:T(8,128)S(1)} async-done(((f32[8,8,384]{2,1,0:T(8,128)}), f32[8,8,384]{2,1,0:T(8,128)S(1)}, u32[]{:S(2)}, u32[]{:S(2)}) %all-to-all-start.9) | async-done | bytes 98336 | tf_op jit(solution)/shard_map/stat_z/all_to_all | solution.py:21
  249.0 0.6 fusion.4
  (31 shorter events, 0.3 us)
Async XLA Ops:
  1.4 22.3 %collective-permute-start.2 = (bf16[32,256]{1,0:T(8,128)(2,1)S(1)}, bf16[32,256]{1,0:T(8,128)(2,1)S(1)}, u32[]{:S(2)}, u32[]{:S(2)}) collective-permute-start(bf16[32,256]{1,0:T(8,128)(2,1)S(1)} %get-tuple-element.30), channel_id=1, source_target_pairs={{0,0},{1,32},{16,64},{17,96},{32,128},{33,160},{48,192},{49,224},{... | collective-permute-start | bytes 49160 | tf_op jit(solution)/shard_map/weights_out/ppermute | solution.py:259
  2.1 21.7 %collective-permute-start.3 = (bf16[32,256]{1,0:T(8,128)(2,1)S(1)}, bf16[32,256]{1,0:T(8,128)(2,1)S(1)}, u32[]{:S(2)}, u32[]{:S(2)}) collective-permute-start(bf16[32,256]{1,0:T(8,128)(2,1)S(1)} %get-tuple-element.31), channel_id=1, source_target_pairs={{0,16},{1,48},{16,80},{17,112},{32,144},{33,176},{48,208},{49,240}... | collective-permute-start | bytes 49160 | tf_op jit(solution)/shard_map/weights_out/ppermute | solution.py:259
  11.8 12.0 %collective-permute-start = (bf16[256,256]{1,0:T(8,128)(2,1)S(1)}, bf16[256,256]{1,0:T(8,128)(2,1)S(1)}, u32[]{:S(2)}, u32[]{:S(2)}) collective-permute-start(bf16[256,256]{1,0:T(8,128)(2,1)S(1)} %get-tuple-element.12), channel_id=1, source_target_pairs={{0,0},{1,32},{16,1},{17,33},{32,16},{33,48},{48,17},{49,49},{2,2},... | collective-permute-start | bytes 393224 | tf_op jit(solution)/shard_map/weights_out/ppermute | solution.py:253
  12.5 20.6 %collective-permute-start.1 = (bf16[256,256]{1,0:T(8,128)(2,1)S(1)}, bf16[256,256]{1,0:T(8,128)(2,1)S(1)}, u32[]{:S(2)}, u32[]{:S(2)}) collective-permute-start(bf16[256,256]{1,0:T(8,128)(2,1)S(1)} %get-tuple-element.13), channel_id=1, source_target_pairs={{0,16},{1,48},{16,17},{17,49},{32,0},{33,32},{48,1},{49,33},{2,18}... | collective-permute-start | bytes 393224 | tf_op jit(solution)/shard_map/weights_out/ppermute | solution.py:253
  34.3 4.9 %copy-start = (bf16[384,256]{1,0:T(8,128)(2,1)S(1)}, bf16[384,256]{1,0:T(8,128)(2,1)}, u32[]{:S(2)}) copy-start(bf16[384,256]{1,0:T(8,128)(2,1)} %x_ref.1) | copy-start | bytes 589828
  34.3 4.9 %copy-start.3 = (f32[256]{0:T(256)S(1)}, f32[256]{0:T(256)}, u32[]{:S(2)}) copy-start(f32[256]{0:T(256)} %param.11) | copy-start | bytes 3076
  34.3 21.1 %all-to-all-start.1 = ((bf16[8,320,256]{2,1,0:T(8,128)(2,1)}), bf16[8,320,256]{2,1,0:T(8,128)(2,1)S(1)}, u32[]{:S(2)}, u32[]{:S(2)}) async-start(bf16[8,320,256]{2,1,0:T(8,128)(2,1)} %broadcast_in_dim.28), calls=%async_computation.1 | async-start | bytes 2621440 | tf_op jit(solution)/shard_map/qkv_rep/all_to_all | solution.py:21
  56.6 48.1 %all-to-all-start = ((bf16[8,384,256]{2,1,0:T(8,128)(2,1)}), bf16[8,384,256]{2,1,0:T(8,128)(2,1)S(1)}, u32[]{:S(2)}, u32[]{:S(2)}) async-start(bf16[8,384,256]{2,1,0:T(8,128)(2,1)} %broadcast_in_dim.27), calls=%async_computation | async-start | bytes 3145728 | tf_op jit(solution)/shard_map/tokens_z/all_to_all | solution.py:21
  65.5 39.2 %collective-permute-start.4 = (bf16[8,320,256]{2,1,0:T(8,128)(2,1)S(1)}, bf16[8,320,256]{2,1,0:T(8,128)(2,1)}, u32[]{:S(2)}, u32[]{:S(2)}) collective-permute-start(bf16[8,320,256]{2,1,0:T(8,128)(2,1)S(1)} %all-to-all-done.1.own_ref), channel_id=1, source_target_pairs={{0,1},{1,0},{2,3},{3,2},{4,5},{5,4},{6,7},{7,6},{8,9},{9,8},{10,11... | collective-permute-start | bytes 3932168 | tf_op jit(solution)/shard_map/qkv_rep/ppermute | solution.py:275
  122.5 13.9 %all-to-all-start.2 = ((bf16[4,384,128]{2,1,0:T(8,128)(2,1)}), bf16[4,384,128]{2,1,0:T(8,128)(2,1)S(1)}, u32[]{:S(2)}, u32[]{:S(2)}) async-start(bf16[4,384,128]{2,1,0:T(8,128)(2,1)} %get-tuple-element.6), calls=%async_computation.2 | async-start | bytes 786432 | tf_op jit(solution)/shard_map/q_sum/all_to_all | solution.py:293
  137.2 14.5 %all-to-all-start.4 = ((bf16[8,48,384]{2,1,0:T(8,128)(2,1)}), bf16[8,48,384]{2,1,0:T(8,128)(2,1)S(1)}, u32[]{:S(2)}, u32[]{:S(2)}) async-start(bf16[8,48,384]{2,1,0:T(8,128)(2,1)} %broadcast_in_dim.30), calls=%async_computation.4 | async-start | bytes 589824 | tf_op jit(solution)/shard_map/kv_z/all_to_all | solution.py:21
  152.7 6.6 %copy-start.1 = (s32[2]{0:T(128)S(1)}, s32[2]{0:T(128)}, u32[]{:S(2)}) copy-start(s32[2]{0:T(128)} %len_ref.1) | copy-start | bytes 28
  152.7 16.1 %all-to-all-start.6 = ((bf16[8,256,256]{2,1,0:T(8,128)(2,1)}), bf16[8,256,256]{2,1,0:T(8,128)(2,1)S(1)}, u32[]{:S(2)}, u32[]{:S(2)}) async-start(bf16[8,256,256]{2,1,0:T(8,128)(2,1)} %broadcast_in_dim.32), calls=%async_computation.6 | async-start | bytes 2097152 | tf_op jit(solution)/shard_map/out_rep/all_to_all | solution.py:21
  169.8 22.1 %all-to-all-start.5 = ((bf16[8,384,128]{2,1,0:T(8,128)(2,1)}), bf16[8,384,128]{2,1,0:T(8,128)(2,1)S(1)}, u32[]{:S(2)}, u32[]{:S(2)}) async-start(bf16[8,384,128]{2,1,0:T(8,128)(2,1)} %broadcast_in_dim.31), calls=%async_computation.5 | async-start | bytes 1572864 | tf_op jit(solution)/shard_map/attended_z/all_to_all | solution.py:21
  173.4 4.6 %collective-permute-start.5 = (bf16[8,256,256]{2,1,0:T(8,128)(2,1)S(1)}, bf16[8,256,256]{2,1,0:T(8,128)(2,1)S(1)}, u32[]{:S(2)}, u32[]{:S(2)}) collective-permute-start(bf16[8,256,256]{2,1,0:T(8,128)(2,1)S(1)} %all-to-all-done.6.own_ref), channel_id=1, source_target_pairs={{0,1},{1,0},{2,3},{3,2},{4,5},{5,4},{6,7},{7,6},{8,9},{9,8},{10,11... | collective-permute-start | bytes 3145736 | tf_op jit(solution)/shard_map/out_rep/ppermute | solution.py:278
  194.5 7.8 %copy-start.2 = (f32[256,6]{0,1:T(8,128)S(1)}, f32[256,6]{0,1:T(8,128)}, u32[]{:S(2)}) copy-start(f32[256,6]{0,1:T(8,128)} %param.17) | copy-start | bytes 18436
  194.5 7.8 %copy-start.4 = (f32[256]{0:T(256)S(1)}, f32[256]{0:T(256)}, u32[]{:S(2)}) copy-start(f32[256]{0:T(256)} %param.16) | copy-start | bytes 3076
  194.5 29.3 %all-to-all-start.7 = ((bf16[4,384,256]{2,1,0:T(8,128)(2,1)}), bf16[4,384,256]{2,1,0:T(8,128)(2,1)S(1)}, u32[]{:S(2)}, u32[]{:S(2)}) async-start(bf16[4,384,256]{2,1,0:T(8,128)(2,1)} %shard_map.106), calls=%async_computation.7 | async-start | bytes 1572864 | tf_op jit(solution)/shard_map/out_sum/all_to_all | solution.py:301
  236.9 12.0 %all-to-all-start.9 = ((f32[8,8,384]{2,1,0:T(8,128)}), f32[8,8,384]{2,1,0:T(8,128)S(1)}, u32[]{:S(2)}, u32[]{:S(2)}) async-start(f32[8,8,384]{2,1,0:T(8,128)} %broadcast_in_dim.35), calls=%async_computation.9 | async-start | bytes 196608 | tf_op jit(solution)/shard_map/stat_z/all_to_all | solution.py:21

commit v2 on v1

v2 whole, which is shorter than its diff:
```python
import jax
import jax.numpy as jnp
from jax import lax
from jax.experimental import pallas as pl
from jax.experimental.pallas import tpu as pltpu
from jax.sharding import Mesh
from jax.sharding import PartitionSpec as P

HEAD = 128
EPS = 1e-05
WIDTH = 8192
NZ, NYH, NYL, NX, NC = 8, 4, 2, 4, 2
TP = ("z", "yh")
REP = ("yl", "x", "c")
VMEM = 48 * 1024 * 1024
F32 = jnp.float32
BF16 = jnp.bfloat16
NT = (((1,), (1,)), ((), ()))
OWN_COST = 30_000_000_000


def copies(x, axis, count):
    return lax.all_to_all(jnp.broadcast_to(x[None], (count, *x.shape)), axis, 0, 0)


def head_perm(k):
    pairs = []
    for yh in range(NYH):
        for c in range(NC):
            b = (yh // 2 + k) % 2
            pairs.append((yh * NC + c, (2 * c + b) * NC + yh % 2))
    return pairs


def kv_perm(k):
    pairs = []
    for z in range(NZ):
        for yh in range(NYH):
            for c in range(NC):
                zn, yn = (z % 2) * 4 + yh, z // 2
                b = (yn // 2 + k) % 2
                dest = (zn * NYH + 2 * c + b) * NC + yn % 2
                pairs.append(((z * NYH + yh) * NC + c, dest))
    return pairs


def split_sum(total):
    high = total.astype(BF16)
    low = (total - high.astype(F32)).astype(BF16)
    return high, low


def columns(w_ref, hi):
    return jnp.concatenate(
        [
            w_ref[k, hi * 128 : (hi + 1) * 128, half * 128 : (half + 1) * 128]
            for k in range(NZ)
            for half in range(2)
        ],
        axis=0,
    )


def project_side(x_ref, w_ref, sq_ref, out_ref, d):
    rows = x_ref.shape[1]
    x = jnp.concatenate([x_ref[k] for k in range(NZ)], axis=1)
    high, low = split_sum(sq_ref[...])
    stat = jnp.concatenate([high, low, jnp.zeros((14, rows), BF16)], axis=0)
    w = jnp.concatenate([columns(w_ref, hi) for hi in range(2)], axis=1)
    q = jnp.dot(x, w, preferred_element_type=F32).astype(BF16)
    kvw = jnp.concatenate([w_ref[k, 256:320, :] for k in range(NZ)], axis=1)
    kv = lax.dot_general(kvw, x, NT, preferred_element_type=F32).astype(BF16)
    for hi in range(2):
        out_ref[2 * hi + d, 0:rows, :] = q[:, hi * 128 : (hi + 1) * 128]
        one = jnp.concatenate([kv[hi * 32 : (hi + 1) * 32, :], stat], axis=0)
        for p in range(3):
            at = rows + 48 * p
            out_ref[2 * hi + d, at : at + 48, :] = one[:, 128 * p : 128 * (p + 1)]


def own_kernel(core_ref, x_ref, w_ref, sq_ref, out_ref):
    project_side(x_ref, w_ref, sq_ref, out_ref, core_ref[0])


def other_kernel(core_ref, x_ref, w_ref, sq_ref, first_ref, out_ref):
    core = core_ref[0]
    for hi in range(2):
        out_ref[2 * hi + core] = first_ref[2 * hi + core]
    project_side(x_ref, w_ref, sq_ref, out_ref, 1 - core)


def project(core, x, own, other, squares):
    rows = x.shape[1]
    vmem = pl.BlockSpec(memory_space=pltpu.VMEM)
    smem = pl.BlockSpec(memory_space=pltpu.SMEM)

    def call(kernel, flops, *args):
        return pl.pallas_call(
            kernel,
            in_specs=[smem] + [vmem] * (len(args) - 1),
            out_specs=vmem,
            out_shape=jax.ShapeDtypeStruct((4, rows + 144, 128), BF16),
            compiler_params=pltpu.CompilerParams(vmem_limit_bytes=VMEM),
            cost_estimate=pl.CostEstimate(flops=flops, bytes_accessed=3_000_000, transcendentals=0),
        )(*args)

    first = call(own_kernel, OWN_COST, core, x, own, squares)
    return call(other_kernel, 2 * rows * 2048 * 320, core, x, other, squares, first)


def sum_kernel(p_ref, out_ref):
    rows = p_ref.shape[1] - 144
    total = jnp.sum(p_ref[...].astype(F32), axis=0)
    parts = [total[0:rows].astype(BF16)]
    for p in range(3):
        part = total[rows + 48 * p : rows + 48 * (p + 1)]
        high, low = split_sum(part[32:33] + part[33:34])
        parts += [part[0:32].astype(BF16), high, low, jnp.zeros((14, 128), BF16)]
    whole = jnp.concatenate(parts, axis=0)
    for k in range(NZ):
        out_ref[k] = whole


def summed_copies(parts):
    return pl.pallas_call(
        sum_kernel,
        in_specs=[pl.BlockSpec(memory_space=pltpu.VMEM)],
        out_specs=pl.BlockSpec(memory_space=pltpu.VMEM),
        out_shape=jax.ShapeDtypeStruct((NZ, *parts.shape[1:]), BF16),
        compiler_params=pltpu.CompilerParams(vmem_limit_bytes=VMEM),
    )(parts)


def attend_kernel(core_ref, len_ref, m_ref, own_ref, other_ref, out_ref, att):
    rows = m_ref.shape[1] - 144
    half = rows // 2
    at = [rows + 48 * p for p in range(3)]
    stats = jnp.concatenate(
        [jnp.sum(m_ref[:, a + 32 : a + 48, :].astype(F32), axis=0) for a in at], axis=1
    )
    scale = lax.rsqrt((stats[0:1] + stats[1:2]) * (1.0 / WIDTH) + EPS)
    wide = jnp.broadcast_to(scale, (HEAD, rows))
    key = jnp.concatenate([m_ref[:, a : a + 16, :].reshape(HEAD, 128) for a in at], axis=1)
    key = (key.astype(F32) * wide).astype(BF16)
    value = jnp.concatenate([m_ref[:, a + 16 : a + 32, :].reshape(HEAD, 128) for a in at], axis=1)
    value = (value.astype(F32) * wide).astype(BF16)
    column = wide.T[:, 0:1] * (1.0 / HEAD**0.5)
    for seq in range(2):
        first = seq * 128
        k = key[:, first : first + 256]
        v = value[:, first : first + 256]
        i = lax.broadcasted_iota(jnp.int32, (half, 256), 0)
        j = lax.broadcasted_iota(jnp.int32, (half, 256), 1) - (seq * half - first)
        allowed = (j >= 0) & (j <= i) & (j < len_ref[seq])
        c = column[seq * half : (seq + 1) * half]
        for head in range(NZ):
            q = m_ref[head, seq * half : (seq + 1) * half, :]
            scores = jnp.dot(q, k, preferred_element_type=F32) * c
            scores = jnp.where(allowed, scores, F32(-1e30))
            scores = scores - jnp.max(scores, axis=1, keepdims=True)
            expo = jnp.exp(scores)
            probs = (expo * (1.0 / jnp.sum(expo, axis=1, keepdims=True))).astype(BF16)
            o = lax.dot_general(probs, v, NT, preferred_element_type=F32)
            att[seq * half : (seq + 1) * half, head * 128 : (head + 1) * 128] = o.astype(BF16)
    core = core_ref[0]
    a = att[...]
    for side, w_ref in enumerate((own_ref, other_ref)):
        d = core if side == 0 else 1 - core
        for hi in range(2):
            w = jnp.concatenate([w_ref[k, hi * 128 : (hi + 1) * 128] for k in range(NZ)], axis=0)
            out_ref[2 * hi + d] = jnp.dot(a, w, preferred_element_type=F32).astype(BF16)


def attend(core, lengths, messages, own, other):
    rows = messages.shape[1] - 144
    vmem = pl.BlockSpec(memory_space=pltpu.VMEM)
    smem = pl.BlockSpec(memory_space=pltpu.SMEM)
    return pl.pallas_call(
        attend_kernel,
        in_specs=[smem, smem, vmem, vmem, vmem],
        out_specs=vmem,
        out_shape=jax.ShapeDtypeStruct((4, rows, 256), BF16),
        scratch_shapes=[pltpu.VMEM((rows, NZ * HEAD), BF16)],
        compiler_params=pltpu.CompilerParams(vmem_limit_bytes=VMEM),
        cost_estimate=pl.CostEstimate(flops=2 * rows * 1024 * 1300, bytes_accessed=4_000_000, transcendentals=1_000_000),
    )(core, lengths, messages, own, other)


def resid_kernel(p_ref, x_ref, head_ref, resid_ref, stat_ref):
    update = jnp.sum(p_ref[...].astype(F32), axis=0)
    resid = (x_ref[...].astype(F32) + update).astype(BF16)
    resid_ref[...] = resid
    r = resid.astype(F32)
    scores = lax.dot_general(
        head_ref[...], r, NT, precision=lax.Precision.HIGHEST, preferred_element_type=F32
    )
    ones = jnp.ones((8, r.shape[1]), F32)
    squares = lax.dot_general(
        ones, r * r, NT, precision=lax.Precision.HIGHEST, preferred_element_type=F32
    )
    row = lax.broadcasted_iota(jnp.int32, scores.shape, 0)
    stat = jnp.where(row < 6, scores, squares).astype(BF16)
    for k in range(NZ * NYH):
        stat_ref[k] = stat


def resid_and_stats(parts, tokens, heads):
    rows, cols = tokens.shape
    return pl.pallas_call(
        resid_kernel,
        in_specs=[pl.BlockSpec(memory_space=pltpu.VMEM)] * 3,
        out_specs=[pl.BlockSpec(memory_space=pltpu.VMEM)] * 2,
        out_shape=[
            jax.ShapeDtypeStruct((rows, cols), BF16),
            jax.ShapeDtypeStruct((NZ * NYH, 8, rows), BF16),
        ],
        compiler_params=pltpu.CompilerParams(vmem_limit_bytes=VMEM),
        cost_estimate=pl.CostEstimate(flops=2 * rows * cols * 96, bytes_accessed=1_200_000, transcendentals=0),
    )(parts, tokens, heads)


def local(
    tokens,
    row_lengths,
    attn_gain,
    query_weight,
    key_weight,
    value_matrix,
    output_weight,
    final_gain,
    value_head,
):
    rows = tokens.shape[0]
    z, yh, c = lax.axis_index("z"), lax.axis_index("yh"), lax.axis_index("c")
    core = c.astype(jnp.int32)[None]

    xf = tokens.astype(F32)
    gained = (xf * attn_gain[None, :]).astype(BF16)
    squares = jnp.sum(xf * xf, axis=1)[None, :]

    with jax.named_scope("weights_out"):
        blocks = []
        for b in range(2):
            q = query_weight[256 * b : 256 * (b + 1)]
            q = jnp.concatenate([q[:128], q[128:]], axis=1)
            blocks.append(jnp.concatenate([q, output_weight[128 * b : 128 * (b + 1)]], axis=0))
        kv_t = jnp.concatenate([key_weight.T, value_matrix.T], axis=0)
        kv_blocks = [kv_t[:, :256], kv_t[:, 256:]]
        first = (yh // 2) == 0
        kv_first = (z // 4) == 0
        came = [
            lax.ppermute(
                jnp.where(first, blocks[k], blocks[1 - k]), ("yh", "c"), head_perm(k)
            )
            for k in range(2)
        ]
        kv_came = [
            lax.ppermute(
                jnp.where(kv_first, kv_blocks[k], kv_blocks[1 - k]), ("z", "yh", "c"), kv_perm(k)
            )
            for k in range(2)
        ]
        even = (yh % 2) == 0
        w = [jnp.where(even, came[k], came[1 - k]) for k in range(2)]
        kvw = [jnp.where(even, kv_came[k], kv_came[1 - k]) for k in range(2)]
        qkv_part = jnp.concatenate([w[0][:128], w[1][:128], kvw[0], kvw[1]], axis=0)
        out_part = jnp.concatenate([w[0][128:], w[1][128:]], axis=0)

    swap = [(0, 1), (1, 0)]
    with jax.named_scope("tokens_z"):
        x_all = lax.all_gather(gained, "z", axis=0)
    with jax.named_scope("qkv_rep"):
        qkv_own = copies(qkv_part, ("yl", "x"), NYL * NX)
        qkv_other = lax.ppermute(qkv_own, "c", swap)
    with jax.named_scope("out_rep"):
        out_own = lax.all_gather(out_part, ("yl", "x"), axis=0)
        out_other = lax.ppermute(out_own, "c", swap)

    parts = project(core, x_all, qkv_own, qkv_other, squares)
    with jax.named_scope("qkv_sum"):
        parts = lax.all_to_all(parts, "yh", 0, 0)
    with jax.named_scope("qkv_z"):
        messages = lax.all_to_all(summed_copies(parts), "z", 0, 0)
    parts = attend(core, row_lengths, messages, out_own, out_other)
    with jax.named_scope("out_sum"):
        parts = lax.all_to_all(parts, "yh", 0, 0)

    heads = jnp.concatenate([(final_gain[:, None] * value_head).T, jnp.zeros((2, tokens.shape[1]), F32)], axis=0)
    resid_out, stat = resid_and_stats(parts, tokens, heads)

    with jax.named_scope("stat_tp"):
        stat = lax.all_to_all(stat, TP, 0, 0).astype(F32).sum(axis=0)
    logits = stat[:6] * lax.rsqrt(stat[6] / WIDTH + EPS)[None, :]
    position = jnp.arange(rows // row_lengths.shape[0], dtype=jnp.int32)
    live = (position[None, :] < row_lengths[:, None]).reshape(1, rows)
    scores = jnp.where(live, logits, F32(0.0)).T
    return resid_out, scores


def solution(mesh):
    split = Mesh(mesh.devices.reshape(NZ, NYH, NYL, NX, NC), TP + REP)
    in_specs = (
        P(REP, TP),
        P(REP),
        P(TP),
        P(REP, TP),
        P(REP, TP),
        P(REP, TP),
        P(REP, TP),
        P(TP),
        P(TP, None),
    )
    out_specs = (P(REP, TP), P(REP, None))
    return jax.shard_map(local, mesh=split, in_specs=in_specs, out_specs=out_specs, check_vma=False)
```

time: 251 us -> 191 us (0.76)
  waiting for transfers between devices: 138 us -> 91.6 us
  starting transfers between devices: 66.6 us -> 42.8 us
  between operations: 0.93 us -> 14.3 us
    all_to_all x6 -> x1, waiting for transfers between devices: 94.8 us -> 16.3 us  [copies(): lax.all_to_all(jnp.broadcast_to(x[None], (count, *x.shape)), axis, 0, 0)]
    all_gather x0 -> x2, waiting for transfers between devices: none -> 33.5 us  [the longest x1 20.2 us: local(): x_all = lax.all_gather(gained, 'z', axis=0)]
    all_to_all x6 -> x1, starting transfers between devices: 30.9 us -> 5.79 us  [copies(): lax.all_to_all(jnp.broadcast_to(x[None], (count, *x.shape)), axis, 0, 0)]
    all_to_all x1 -> x2, starting transfers between devices: 3.46 us -> 13 us  [the longest x1 9.35 us: local(): stat = lax.all_to_all(stat, TP, 0, 0).astype(F32).sum(axis=0)]
    ppermute x2, waiting for transfers between devices: 9.24 us -> 0.01 us  [local(): lax.ppermute(jnp.where(first, blocks[k], blocks[1 - k]), ('yh', 'c'), hea...]
    ppermute x2, starting transfers between devices: 11.9 us -> 6.42 us  [local(): lax.ppermute(jnp.where(first, blocks[k], blocks[1 - k]), ('yh', 'c'), hea...]
    all_to_all x1 -> x2, waiting for transfers between devices: 10.3 us -> 15.5 us  [the longest x1 12.4 us: local(): stat = lax.all_to_all(stat, TP, 0, 0).astype(F32).sum(axis=0)]
    broadcast_in_dim x7 -> x1, local copies, waits for them, and re-layouts: 5.86 us -> 1.16 us  [copies(): jnp.broadcast_to(x[None], (count, *x.shape))]
  transfers between devices with their start and end apart: 14 -> 12, of which waited for: 10 -> 8; matrix products, arithmetic and copies ran while one was open for 1% -> 2% of each run, Pallas kernels for 0% -> 2%
where the time goes in v2:
time: 191 us; the launch traced here: 189 us
  waiting for transfers between devices  91.6 us (48%)
  starting transfers between devices  42.8 us (22%)
  blocking collectives  22 us (12%)
  between operations  14.3 us (7%)
  Pallas kernels  8.8 us (5%)
  local copies, waits for them, and re-layouts  5.66 us (3%)
  other arithmetic  3.71 us (2%)
    all_to_all x1, blocking collectives, local(): parts = lax.all_to_all(parts, 'yh', 0, 0)  22 us
    all_gather x1, waiting for transfers between devices, local(): x_all = lax.all_gather(gained, 'z', axis=0)  20.2 us
    all_to_all x1, waiting for transfers between devices, local(): parts = lax.all_to_all(parts, 'yh', 0, 0)  18.9 us
    all_to_all x1, waiting for transfers between devices, copies(): lax.all_to_all(jnp.broadcast_to(x[None], (count, *x.shape)), axis, 0, 0)  16.3 us
    all_gather x1, waiting for transfers between devices, local(): out_own = lax.all_gather(out_part, ('yl', 'x'), axis=0)  13.3 us
    all_to_all x1, waiting for transfers between devices, local(): stat = lax.all_to_all(stat, TP, 0, 0).astype(F32).sum(axis=0)  12.4 us
    all_to_all x1, starting transfers between devices, local(): stat = lax.all_to_all(stat, TP, 0, 0).astype(F32).sum(axis=0)  9.35 us
    ppermute x2, starting transfers between devices, local(): lax.ppermute(jnp.where(kv_first, kv_blocks[k], kv_blocks[1 - k]), ('z', '...  8.55 us
  transfers between devices with their start and end apart: 12, of which 8 were waited for; matrix products, arithmetic and copies ran while one was open for 2% of the time, Pallas kernels for 2%

profile of v2, /device:TPU:6, one launch (start us, length us, event | category | flops | bytes accessed | tf_op | source)
XLA Modules:
  0.0 188.8 jit_solution(2387929933687933262)
XLA Ops:
  7.2 0.0 copy-start.2
  7.2 0.0 all-gather.5.cloned.1.call-start
  7.2 0.9 fusion.10
  8.1 0.9 fusion.11
  9.0 0.1 broadcast_select_fusion.1
  9.0 0.7 collective-permute-start
  9.7 5.7 %collective-permute-start.1 = (bf16[256,256]{1,0:T(8,128)(2,1)S(1)}, bf16[256,256]{1,0:T(8,128)(2,1)S(1)}, u32[]{:S(2)}, u32[]{:S(2)}) collective-permute-start(bf16[256,256]{1,0:T(8,128)(2,1)S(1)} %get-tuple-element.9), channel_id=1, source_target_pairs={{0,16},{1,48},{16,17},{17,49},{32,0},{33,32},{48,1},{49,33},{2,18}... | collective-permute-start | bytes 393224 | tf_op jit(solution)/shard_map/weights_out/ppermute | solution.py:252
  15.5 0.8 broadcast_select_fusion.5
  16.3 0.7 collective-permute-start.2
  17.0 7.9 %collective-permute-start.3 = (bf16[32,256]{1,0:T(8,128)(2,1)S(1)}, bf16[32,256]{1,0:T(8,128)(2,1)S(1)}, u32[]{:S(2)}, u32[]{:S(2)}) collective-permute-start(bf16[32,256]{1,0:T(8,128)(2,1)S(1)} %get-tuple-element.25), channel_id=1, source_target_pairs={{0,16},{1,48},{16,80},{17,112},{32,144},{33,176},{48,208},{49,240}... | collective-permute-start | bytes 49160 | tf_op jit(solution)/shard_map/weights_out/ppermute | solution.py:258
  24.9 0.0 copy-done.2
  24.9 1.4 fusion.1
  26.3 0.0 all-gather.5.cloned.1.call-update
  26.3 0.0 collective-permute-done.2
  26.3 4.5 %collective-permute-done.3 = bf16[32,256]{1,0:T(8,128)(2,1)S(1)} collective-permute-done((bf16[32,256]{1,0:T(8,128)(2,1)S(1)}, bf16[32,256]{1,0:T(8,128)(2,1)S(1)}, u32[]{:S(2)}, u32[]{:S(2)}) %collective-permute-start.3) | collective-permute-done | bytes 16416 | tf_op jit(solution)/shard_map/weights_out/ppermute | solution.py:258
  30.9 0.0 collective-permute-done
  30.9 0.0 collective-permute-done.1
  31.0 1.2 broadcast_in_dim.15
  32.1 5.8 %all-to-all-start = ((bf16[8,320,256]{2,1,0:T(8,128)(2,1)}), bf16[8,320,256]{2,1,0:T(8,128)(2,1)S(1)}, u32[]{:S(2)}, u32[]{:S(2)}) async-start(bf16[8,320,256]{2,1,0:T(8,128)(2,1)} %broadcast_in_dim.15), calls=%async_computation | async-start | bytes 2621440 | tf_op jit(solution)/shard_map/qkv_rep/all_to_all | solution.py:23
  37.9 0.0 all-gather.7.cloned.1.call-start
  37.9 0.6 pad_maximum_fusion.3
  38.6 0.1 all-gather.7.cloned.1.call-update
  38.6 16.3 %all-to-all-done.w_ref = bf16[8,320,256]{2,1,0:T(8,128)(2,1)S(1)} async-done(((bf16[8,320,256]{2,1,0:T(8,128)(2,1)}), bf16[8,320,256]{2,1,0:T(8,128)(2,1)S(1)}, u32[]{:S(2)}, u32[]{:S(2)}) %all-to-all-start) | async-done | bytes 1310752 | tf_op jit(solution)/shard_map/qkv_rep/all_to_all | solution.py:23
  54.9 1.9 %collective-permute-start.4 = (bf16[8,320,256]{2,1,0:T(8,128)(2,1)S(1)}, bf16[8,320,256]{2,1,0:T(8,128)(2,1)S(1)}, u32[]{:S(2)}, u32[]{:S(2)}) collective-permute-start(bf16[8,320,256]{2,1,0:T(8,128)(2,1)S(1)} %all-to-all-done.w_ref), channel_id=1, source_target_pairs={{0,1},{1,0},{2,3},{3,2},{4,5},{5,4},{6,7},{7,6},{8,9},{9,8},{10,11... | collective-permute-start | bytes 3932168 | tf_op jit(solution)/shard_map/qkv_rep/ppermute | solution.py:274
  56.8 20.2 %all-gather.5.cloned.1.call-done = bf16[3072,256]{1,0:T(8,128)(2,1)} async-done(((bf16[384,256]{1,0:T(8,128)(2,1)}), bf16[3072,256]{1,0:T(8,128)(2,1)}) %all-gather.5.cloned.1.call-update) | async-done | bytes 1572880 | tf_op jit(solution)/shard_map/tokens_z/all_gather | solution.py:271
  77.1 1.4 copy-done
  78.5 1.0 shard_map.104.first_ref
  79.5 0.0 collective-permute-done.4.w_ref
  79.5 1.0 shard_map.105
  80.5 22.0 %all_to_all.25.p_ref = bf16[4,528,128]{2,1,0:T(8,128)(2,1)S(1)} all-to-all(bf16[4,528,128]{2,1,0:T(8,128)(2,1)S(1)} %shard_map.105), channel_id=1, replica_groups=mesh['z'=8,'yh'=4,'yl'=2,'x'=4,'c'=2] {'yh'}, dimensions={0} | all-to-all | bytes 1081344 | tf_op jit(solution)/shard_map/qkv_sum/all_to_all | solution.py:281
  102.5 1.1 qkv_z.1
  103.6 3.7 %all-to-all-start.2 = ((bf16[8,528,128]{2,1,0:T(8,128)(2,1)}), bf16[8,528,128]{2,1,0:T(8,128)(2,1)S(1)}, u32[]{:S(2)}, u32[]{:S(2)}) async-start(bf16[8,528,128]{2,1,0:T(8,128)(2,1)} %qkv_z.1), calls=%async_computation.2 | async-start | bytes 2162688 | tf_op jit(solution)/shard_map/qkv_z/all_to_all | solution.py:283
  107.3 13.3 %all-gather.7.cloned.1.call-done = bf16[2048,256]{1,0:T(8,128)(2,1)} async-done(((bf16[256,256]{1,0:T(8,128)(2,1)}), bf16[2048,256]{1,0:T(8,128)(2,1)}) %all-gather.7.cloned.1.call-update) | async-done | bytes 1048592 | tf_op jit(solution)/shard_map/out_rep/all_gather | solution.py:276
  120.6 1.9 %collective-permute-start.5 = (bf16[8,256,256]{2,1,0:T(8,128)(2,1)}, bf16[8,256,256]{2,1,0:T(8,128)(2,1)S(1)}, u32[]{:S(2)}, u32[]{:S(2)}) collective-permute-start(bf16[8,256,256]{2,1,0:T(8,128)(2,1)} %bitcast.11), channel_id=1, source_target_pairs={{0,1},{1,0},{2,3},{3,2},{4,5},{5,4},{6,7},{7,6},{8,9},{9,8},{10,11... | collective-permute-start | bytes 3145736 | tf_op jit(solution)/shard_map/out_rep/ppermute | solution.py:277
  122.5 2.8 %collective-permute-done.5.other_ref = bf16[8,256,256]{2,1,0:T(8,128)(2,1)S(1)} collective-permute-done((bf16[8,256,256]{2,1,0:T(8,128)(2,1)}, bf16[8,256,256]{2,1,0:T(8,128)(2,1)S(1)}, u32[]{:S(2)}, u32[]{:S(2)}) %collective-permute-start.5) | collective-permute-done | bytes 1048608 | tf_op jit(solution)/shard_map/out_rep/ppermute | solution.py:277
  125.4 3.0 %all-to-all-done.2.m_ref = bf16[8,528,128]{2,1,0:T(8,128)(2,1)S(1)} async-done(((bf16[8,528,128]{2,1,0:T(8,128)(2,1)}), bf16[8,528,128]{2,1,0:T(8,128)(2,1)S(1)}, u32[]{:S(2)}, u32[]{:S(2)}) %all-to-all-start.2) | async-done | bytes 1081376 | tf_op jit(solution)/shard_map/qkv_z/all_to_all | solution.py:283
  128.4 0.0 copy-done.3
  128.4 1.2 copy-done.1
  129.6 4.2 %shard_map.106 = bf16[4,384,256]{2,1,0:T(8,128)(2,1)} custom-call(s32[1]{0:T(128)} %bitcast.core_ref, s32[2]{0:T(128)S(1)} %copy-done.3, bf16[8,528,128]{2,1,0:T(8,128)(2,1)S(1)} %all-to-all-done.2.m_ref, bf16[8,256,256]{2,1,0:T(8,128)(2,1)S(1)} %bitcast.12, bf16[8,256,256]{2,1,0:T(8,128)(2,1)S(1)} %collective-permute-done.5.other_ref), custom_call_target="tpu_custom_call" | custom-call | flops 1022361600 | bytes 4000000 | tf_op jit(solution)/shard_map/pallas_call | solution.py:178
  133.8 5.1 %all-to-all-start.3 = ((bf16[4,384,256]{2,1,0:T(8,128)(2,1)}), bf16[4,384,256]{2,1,0:T(8,128)(2,1)S(1)}, u32[]{:S(2)}, u32[]{:S(2)}) async-start(bf16[4,384,256]{2,1,0:T(8,128)(2,1)} %shard_map.106), calls=%async_computation.3 | async-start | bytes 1572864 | tf_op jit(solution)/shard_map/out_sum/all_to_all | solution.py:286
  138.9 0.0 copy-done.4
  138.9 18.9 %all-to-all-done.3.p_ref = bf16[4,384,256]{2,1,0:T(8,128)(2,1)S(1)} async-done(((bf16[4,384,256]{2,1,0:T(8,128)(2,1)}), bf16[4,384,256]{2,1,0:T(8,128)(2,1)S(1)}, u32[]{:S(2)}, u32[]{:S(2)}) %all-to-all-start.3) | async-done | bytes 786464 | tf_op jit(solution)/shard_map/out_sum/all_to_all | solution.py:286
  157.9 1.5 shard_map.107
  159.4 9.4 %all-to-all-start.4 = ((bf16[32,8,384]{2,1,0:T(8,128)(2,1)}), bf16[32,8,384]{2,1,0:T(8,128)(2,1)S(1)}, u32[]{:S(2)}, u32[]{:S(2)}) async-start(bf16[32,8,384]{2,1,0:T(8,128)(2,1)} %get-tuple-element.5), calls=%async_computation.4 | async-start | bytes 393216 | tf_op jit(solution)/shard_map/stat_tp/all_to_all | solution.py:292
  168.7 0.1 iota_compare_fusion
  168.8 0.1 lt.30
  168.9 12.4 %all-to-all-done.4 = bf16[32,8,384]{2,1,0:T(8,128)(2,1)S(1)} async-done(((bf16[32,8,384]{2,1,0:T(8,128)(2,1)}), bf16[32,8,384]{2,1,0:T(8,128)(2,1)S(1)}, u32[]{:S(2)}, u32[]{:S(2)}) %all-to-all-start.4) | async-done | bytes 196640 | tf_op jit(solution)/shard_map/stat_tp/all_to_all | solution.py:292
  181.4 0.6 fusion.4
  (15 shorter events, 0.2 us)
Async XLA Ops:
  7.2 17.7 %copy-start.2 = (bf16[384,256]{1,0:T(8,128)(2,1)S(1)}, bf16[384,256]{1,0:T(8,128)(2,1)}, u32[]{:S(2)}) copy-start(bf16[384,256]{1,0:T(8,128)(2,1)} %x_ref.1) | copy-start | bytes 589828
  7.2 69.9 %all-gather.5.cloned.1.call-start = ((), (), s32[]{:S(2)}) async-start(), calls=%async_computation.5 | async-start | bytes 1769472 | tf_op jit(solution)/shard_map/tokens_z/all_gather | solution.py:271
  9.0 21.8 %collective-permute-start = (bf16[256,256]{1,0:T(8,128)(2,1)S(1)}, bf16[256,256]{1,0:T(8,128)(2,1)S(1)}, u32[]{:S(2)}, u32[]{:S(2)}) collective-permute-start(bf16[256,256]{1,0:T(8,128)(2,1)S(1)} %get-tuple-element.8), channel_id=1, source_target_pairs={{0,0},{1,32},{16,1},{17,33},{32,16},{33,48},{48,17},{49,49},{2,2},... | collective-permute-start | bytes 393224 | tf_op jit(solution)/shard_map/weights_out/ppermute | solution.py:252
  9.7 21.2 %collective-permute-start.1 = (bf16[256,256]{1,0:T(8,128)(2,1)S(1)}, bf16[256,256]{1,0:T(8,128)(2,1)S(1)}, u32[]{:S(2)}, u32[]{:S(2)}) collective-permute-start(bf16[256,256]{1,0:T(8,128)(2,1)S(1)} %get-tuple-element.9), channel_id=1, source_target_pairs={{0,16},{1,48},{16,17},{17,49},{32,0},{33,32},{48,1},{49,33},{2,18}... | collective-permute-start | bytes 393224 | tf_op jit(solution)/shard_map/weights_out/ppermute | solution.py:252
  16.3 10.0 %collective-permute-start.2 = (bf16[32,256]{1,0:T(8,128)(2,1)S(1)}, bf16[32,256]{1,0:T(8,128)(2,1)S(1)}, u32[]{:S(2)}, u32[]{:S(2)}) collective-permute-start(bf16[32,256]{1,0:T(8,128)(2,1)S(1)} %get-tuple-element.24), channel_id=1, source_target_pairs={{0,0},{1,32},{16,64},{17,96},{32,128},{33,160},{48,192},{49,224},{... | collective-permute-start | bytes 49160 | tf_op jit(solution)/shard_map/weights_out/ppermute | solution.py:258
  17.0 13.9 %collective-permute-start.3 = (bf16[32,256]{1,0:T(8,128)(2,1)S(1)}, bf16[32,256]{1,0:T(8,128)(2,1)S(1)}, u32[]{:S(2)}, u32[]{:S(2)}) collective-permute-start(bf16[32,256]{1,0:T(8,128)(2,1)S(1)} %get-tuple-element.25), channel_id=1, source_target_pairs={{0,16},{1,48},{16,80},{17,112},{32,144},{33,176},{48,208},{49,240}... | collective-permute-start | bytes 49160 | tf_op jit(solution)/shard_map/weights_out/ppermute | solution.py:258
  32.1 22.8 %all-to-all-start = ((bf16[8,320,256]{2,1,0:T(8,128)(2,1)}), bf16[8,320,256]{2,1,0:T(8,128)(2,1)S(1)}, u32[]{:S(2)}, u32[]{:S(2)}) async-start(bf16[8,320,256]{2,1,0:T(8,128)(2,1)} %broadcast_in_dim.15), calls=%async_computation | async-start | bytes 2621440 | tf_op jit(solution)/shard_map/qkv_rep/all_to_all | solution.py:23
  37.9 82.7 %all-gather.7.cloned.1.call-start = ((), (), s32[]{:S(2)}) async-start(), calls=%async_computation.6 | async-start | bytes 1179648 | tf_op jit(solution)/shard_map/out_rep/all_gather | solution.py:276
  54.9 24.6 %collective-permute-start.4 = (bf16[8,320,256]{2,1,0:T(8,128)(2,1)S(1)}, bf16[8,320,256]{2,1,0:T(8,128)(2,1)S(1)}, u32[]{:S(2)}, u32[]{:S(2)}) collective-permute-start(bf16[8,320,256]{2,1,0:T(8,128)(2,1)S(1)} %all-to-all-done.w_ref), channel_id=1, source_target_pairs={{0,1},{1,0},{2,3},{3,2},{4,5},{5,4},{6,7},{7,6},{8,9},{9,8},{10,11... | collective-permute-start | bytes 3932168 | tf_op jit(solution)/shard_map/qkv_rep/ppermute | solution.py:274
  77.1 1.4 copy-start
  103.6 24.8 %copy-start.3 = (s32[2]{0:T(128)S(1)}, s32[2]{0:T(128)}, u32[]{:S(2)}) copy-start(s32[2]{0:T(128)} %len_ref.1) | copy-start | bytes 28
  103.6 24.8 %all-to-all-start.2 = ((bf16[8,528,128]{2,1,0:T(8,128)(2,1)}), bf16[8,528,128]{2,1,0:T(8,128)(2,1)S(1)}, u32[]{:S(2)}, u32[]{:S(2)}) async-start(bf16[8,528,128]{2,1,0:T(8,128)(2,1)} %qkv_z.1), calls=%async_computation.2 | async-start | bytes 2162688 | tf_op jit(solution)/shard_map/qkv_z/all_to_all | solution.py:283
  120.6 4.8 %collective-permute-start.5 = (bf16[8,256,256]{2,1,0:T(8,128)(2,1)}, bf16[8,256,256]{2,1,0:T(8,128)(2,1)S(1)}, u32[]{:S(2)}, u32[]{:S(2)}) collective-permute-start(bf16[8,256,256]{2,1,0:T(8,128)(2,1)} %bitcast.11), channel_id=1, source_target_pairs={{0,1},{1,0},{2,3},{3,2},{4,5},{5,4},{6,7},{7,6},{8,9},{9,8},{10,11... | collective-permute-start | bytes 3145736 | tf_op jit(solution)/shard_map/out_rep/ppermute | solution.py:277
  128.4 1.2 copy-start.1
  133.8 5.1 %copy-start.4 = (f32[256,6]{0,1:T(8,128)S(1)}, f32[256,6]{0,1:T(8,128)}, u32[]{:S(2)}) copy-start(f32[256,6]{0,1:T(8,128)} %param.17) | copy-start | bytes 18436
  133.8 5.1 %copy-start.5 = (f32[256]{0:T(256)S(1)}, f32[256]{0:T(256)}, u32[]{:S(2)}) copy-start(f32[256]{0:T(256)} %param.16) | copy-start | bytes 3076
  133.8 24.1 %all-to-all-start.3 = ((bf16[4,384,256]{2,1,0:T(8,128)(2,1)}), bf16[4,384,256]{2,1,0:T(8,128)(2,1)S(1)}, u32[]{:S(2)}, u32[]{:S(2)}) async-start(bf16[4,384,256]{2,1,0:T(8,128)(2,1)} %shard_map.106), calls=%async_computation.3 | async-start | bytes 1572864 | tf_op jit(solution)/shard_map/out_sum/all_to_all | solution.py:286
  159.4 21.9 %all-to-all-start.4 = ((bf16[32,8,384]{2,1,0:T(8,128)(2,1)}), bf16[32,8,384]{2,1,0:T(8,128)(2,1)S(1)}, u32[]{:S(2)}, u32[]{:S(2)}) async-start(bf16[32,8,384]{2,1,0:T(8,128)(2,1)} %get-tuple-element.5), calls=%async_computation.4 | async-start | bytes 393216 | tf_op jit(solution)/shard_map/stat_tp/all_to_all | solution.py:292
Sparse Core Ops, SparseCore 0:
  26.4 50.5 all-gather.4
  79.1 41.4 all-gather.6

commit v3 on v2

v3 whole, which is shorter than its diff:
```python
import jax
import jax.numpy as jnp
from jax import lax
from jax.experimental import pallas as pl
from jax.experimental.pallas import tpu as pltpu
from jax.sharding import Mesh
from jax.sharding import PartitionSpec as P

HEAD = 128
EPS = 1e-05
WIDTH = 8192
NZ, NYH, NYL, NX, NC = 8, 4, 2, 4, 2
TP = ("z", "yh")
REP = ("yl", "x", "c")
VMEM = 48 * 1024 * 1024
F32 = jnp.float32
BF16 = jnp.bfloat16
NT = (((1,), (1,)), ((), ()))
OWN_COST = 30_000_000_000
ATTEND_COST = 8_000_000_000


def copies(x, axis, count):
    return lax.all_to_all(jnp.broadcast_to(x[None], (count, *x.shape)), axis, 0, 0)


def head_perm(k):
    pairs = []
    for yh in range(NYH):
        for c in range(NC):
            b = (yh // 2 + k) % 2
            pairs.append((yh * NC + c, (2 * c + b) * NC + yh % 2))
    return pairs


def kv_perm():
    return [
        (z * NYH + yh, ((z % 2) * 4 + yh) * NYH + z // 2) for z in range(NZ) for yh in range(NYH)
    ]


def split_sum(total):
    high = total.astype(BF16)
    low = (total - high.astype(F32)).astype(BF16)
    return high, low


def pack_kernel(odd_ref, q0, q1, out_ref):
    even = odd_ref[0] == 0
    first, second = jnp.where(even, q0[...], q1[...]), jnp.where(even, q1[...], q0[...])
    whole = jnp.concatenate([first[:128], second[:128], first[128:], second[128:]], axis=0)
    for k in range(NYL * NX):
        out_ref[k] = whole


def packed_copies(odd, *parts):
    vmem = pl.BlockSpec(memory_space=pltpu.VMEM)
    return pl.pallas_call(
        pack_kernel,
        in_specs=[pl.BlockSpec(memory_space=pltpu.SMEM)] + [vmem] * 2,
        out_specs=vmem,
        out_shape=jax.ShapeDtypeStruct((NYL * NX, 320, 256), BF16),
        compiler_params=pltpu.CompilerParams(vmem_limit_bytes=VMEM),
        cost_estimate=pl.CostEstimate(flops=1000, bytes_accessed=1000, transcendentals=0),
    )(odd, *parts)


def columns(w_ref, hi):
    return jnp.concatenate(
        [
            w_ref[k, hi * 128 : (hi + 1) * 128, half * 128 : (half + 1) * 128]
            for k in range(NZ)
            for half in range(2)
        ],
        axis=0,
    )


def project_side(x_ref, w_ref, stat, out_ref, d):
    rows = x_ref.shape[1]
    x = jnp.concatenate([x_ref[k] for k in range(NZ)], axis=1)
    w = jnp.concatenate([columns(w_ref, hi) for hi in range(2)], axis=1)
    q = jnp.dot(x, w, preferred_element_type=F32).astype(BF16)
    kvw = jnp.concatenate([w_ref[k, 256:320, :] for k in range(NZ)], axis=1)
    kv = lax.dot_general(kvw, x, NT, preferred_element_type=F32).astype(BF16)
    for hi in range(2):
        out_ref[2 * hi + d, 0:rows, :] = q[:, hi * 128 : (hi + 1) * 128]
        for p in range(3):
            at = rows + 32 * p
            out_ref[2 * hi + d, at : at + 32, :] = kv[hi * 32 : (hi + 1) * 32, 128 * p : 128 * (p + 1)]
        out_ref[2 * hi + d, rows + 96 : rows + 112, :] = stat


def stat_rows(sums):
    pairs = [half for one in sums for half in split_sum(one)]
    return jnp.concatenate(pairs + [jnp.zeros((10, 128), BF16)], axis=0)


def own_kernel(core_ref, x_ref, w_ref, tokens_ref, out_ref):
    t = tokens_ref[...].astype(F32)
    ones = jnp.ones((8, t.shape[1]), F32)
    sq = lax.dot_general(
        ones, t * t, NT, precision=lax.Precision.HIGHEST, preferred_element_type=F32
    )
    stat = stat_rows([sq[0:1, 128 * p : 128 * (p + 1)] for p in range(3)])
    project_side(x_ref, w_ref, stat, out_ref, core_ref[0])


def other_kernel(core_ref, x_ref, w_ref, first_ref, out_ref):
    core = core_ref[0]
    rows = x_ref.shape[1]
    for hi in range(2):
        out_ref[2 * hi + core] = first_ref[2 * hi + core]
    project_side(x_ref, w_ref, first_ref[core, rows + 96 : rows + 112, :], out_ref, 1 - core)


def project(core, x, own, other, tokens):
    rows = x.shape[1]
    vmem = pl.BlockSpec(memory_space=pltpu.VMEM)
    smem = pl.BlockSpec(memory_space=pltpu.SMEM)

    def call(kernel, flops, *args):
        return pl.pallas_call(
            kernel,
            in_specs=[smem] + [vmem] * (len(args) - 1),
            out_specs=vmem,
            out_shape=jax.ShapeDtypeStruct((4, rows + 112, 128), BF16),
            compiler_params=pltpu.CompilerParams(vmem_limit_bytes=VMEM),
            cost_estimate=pl.CostEstimate(flops=flops, bytes_accessed=3_000_000, transcendentals=0),
        )(*args)

    first = call(own_kernel, OWN_COST, core, x, own, tokens)
    return call(other_kernel, 2 * rows * 2048 * 320, core, x, other, first)


def sum_kernel(p_ref, out_ref):
    rows = p_ref.shape[1] - 112
    total = jnp.sum(p_ref[...].astype(F32), axis=0)
    out_ref[0 : rows + 96, :] = total[0 : rows + 96].astype(BF16)
    at = rows + 96
    sums = [total[at + 2 * p : at + 2 * p + 1] + total[at + 2 * p + 1 : at + 2 * p + 2] for p in range(3)]
    out_ref[at : at + 16, :] = stat_rows(sums)


def summed(parts):
    return pl.pallas_call(
        sum_kernel,
        in_specs=[pl.BlockSpec(memory_space=pltpu.VMEM)],
        out_specs=pl.BlockSpec(memory_space=pltpu.VMEM),
        out_shape=jax.ShapeDtypeStruct(parts.shape[1:], BF16),
        compiler_params=pltpu.CompilerParams(vmem_limit_bytes=VMEM),
    )(parts)


def attend_kernel(len_ref, m_ref, att_ref):
    rows = m_ref.shape[1] - 112
    half = rows // 2
    at = [rows + 32 * p for p in range(3)]
    stats = jnp.sum(m_ref[:, rows + 96 : rows + 112, :].astype(F32), axis=0)
    stats = jnp.concatenate(
        [stats[2 * p : 2 * p + 1] + stats[2 * p + 1 : 2 * p + 2] for p in range(3)], axis=1
    )
    scale = lax.rsqrt(stats * (1.0 / WIDTH) + EPS)
    wide = jnp.broadcast_to(scale, (HEAD, rows))
    key = jnp.concatenate([m_ref[:, a : a + 16, :].reshape(HEAD, 128) for a in at], axis=1)
    key = (key.astype(F32) * wide).astype(BF16)
    value = jnp.concatenate([m_ref[:, a + 16 : a + 32, :].reshape(HEAD, 128) for a in at], axis=1)
    value = (value.astype(F32) * wide).astype(BF16)
    column = wide.T[:, 0:1] * (1.0 / HEAD**0.5)
    for seq in range(2):
        first = seq * 128
        k = key[:, first : first + 256]
        v = value[:, first : first + 256]
        i = lax.broadcasted_iota(jnp.int32, (half, 256), 0)
        j = lax.broadcasted_iota(jnp.int32, (half, 256), 1) - (seq * half - first)
        allowed = (j >= 0) & (j <= i) & (j < len_ref[seq])
        c = column[seq * half : (seq + 1) * half]
        for head in range(NZ):
            q = m_ref[head, seq * half : (seq + 1) * half, :]
            scores = jnp.dot(q, k, preferred_element_type=F32) * c
            scores = jnp.where(allowed, scores, F32(-1e30))
            scores = scores - jnp.max(scores, axis=1, keepdims=True)
            expo = jnp.exp(scores)
            probs = (expo * (1.0 / jnp.sum(expo, axis=1, keepdims=True))).astype(BF16)
            o = lax.dot_general(probs, v, NT, preferred_element_type=F32)
            att_ref[seq * half : (seq + 1) * half, head * 128 : (head + 1) * 128] = o.astype(BF16)


def output_side(a, w_ref, out_ref, d):
    for hi in range(2):
        w = jnp.concatenate([w_ref[k, hi * 128 : (hi + 1) * 128] for k in range(NZ)], axis=0)
        out_ref[2 * hi + d] = jnp.dot(a, w, preferred_element_type=F32).astype(BF16)


def output_kernel(core_ref, att_ref, own_ref, other_ref, out_ref):
    core = core_ref[0]
    output_side(att_ref[...], own_ref, out_ref, core)
    output_side(att_ref[...], other_ref, out_ref, 1 - core)


def attend(lengths, messages):
    rows = messages.shape[1] - 112
    vmem = pl.BlockSpec(memory_space=pltpu.VMEM)
    smem = pl.BlockSpec(memory_space=pltpu.SMEM)
    return pl.pallas_call(
        attend_kernel,
        in_specs=[smem, vmem],
        out_specs=vmem,
        out_shape=jax.ShapeDtypeStruct((rows, NZ * HEAD), BF16),
        compiler_params=pltpu.CompilerParams(vmem_limit_bytes=VMEM),
        cost_estimate=pl.CostEstimate(flops=ATTEND_COST, bytes_accessed=2_000_000, transcendentals=1_000_000),
    )(lengths, messages)


def output_products(core, attended, own, other):
    rows = attended.shape[0]
    vmem = pl.BlockSpec(memory_space=pltpu.VMEM)
    smem = pl.BlockSpec(memory_space=pltpu.SMEM)
    return pl.pallas_call(
        output_kernel,
        in_specs=[smem, vmem, vmem, vmem],
        out_specs=vmem,
        out_shape=jax.ShapeDtypeStruct((4, rows, 256), BF16),
        compiler_params=pltpu.CompilerParams(vmem_limit_bytes=VMEM),
        cost_estimate=pl.CostEstimate(flops=2 * rows * 1024 * 1024, bytes_accessed=5_000_000, transcendentals=0),
    )(core, attended, own, other)


def resid_kernel(p_ref, x_ref, head_ref, resid_ref, stat_ref):
    update = jnp.sum(p_ref[...].astype(F32), axis=0)
    resid = (x_ref[...].astype(F32) + update).astype(BF16)
    resid_ref[...] = resid
    r = resid.astype(F32)
    scores = lax.dot_general(
        head_ref[...], r, NT, precision=lax.Precision.HIGHEST, preferred_element_type=F32
    )
    ones = jnp.ones((8, r.shape[1]), F32)
    squares = lax.dot_general(
        ones, r * r, NT, precision=lax.Precision.HIGHEST, preferred_element_type=F32
    )
    row = lax.broadcasted_iota(jnp.int32, scores.shape, 0)
    stat = jnp.where(row < 6, scores, squares).astype(BF16)
    for k in range(NZ * NYH):
        stat_ref[k] = stat


def resid_and_stats(parts, tokens, heads):
    rows, cols = tokens.shape
    return pl.pallas_call(
        resid_kernel,
        in_specs=[pl.BlockSpec(memory_space=pltpu.VMEM)] * 3,
        out_specs=[pl.BlockSpec(memory_space=pltpu.VMEM)] * 2,
        out_shape=[
            jax.ShapeDtypeStruct((rows, cols), BF16),
            jax.ShapeDtypeStruct((NZ * NYH, 8, rows), BF16),
        ],
        compiler_params=pltpu.CompilerParams(vmem_limit_bytes=VMEM),
        cost_estimate=pl.CostEstimate(flops=2 * rows * cols * 96, bytes_accessed=1_200_000, transcendentals=0),
    )(parts, tokens, heads)


def local(
    tokens,
    row_lengths,
    attn_gain,
    query_weight,
    key_weight,
    value_matrix,
    output_weight,
    final_gain,
    value_head,
):
    rows = tokens.shape[0]
    z, yh, c = lax.axis_index("z"), lax.axis_index("yh"), lax.axis_index("c")
    core = c.astype(jnp.int32)[None]

    xf = tokens.astype(F32)
    gained = (xf * attn_gain[None, :]).astype(BF16)

    first, even = (yh // 2) == 0, (yh % 2) == 0
    with jax.named_scope("weights_yh"):
        kv = lax.ppermute(jnp.concatenate([key_weight.T, value_matrix.T], axis=0), TP, kv_perm())
        q = [query_weight[256 * b : 256 * (b + 1)] for b in range(2)]
        q = [
            jnp.concatenate(
                [q[b][:128], q[b][128:]], axis=1
            )
            for b in range(2)
        ]
        q = [jnp.concatenate([q[b], kv[:, 256 * b : 256 * (b + 1)]], axis=0) for b in range(2)]
        q = [
            lax.ppermute(jnp.where(first, q[k], q[1 - k]), ("yh", "c"), head_perm(k))
            for k in range(2)
        ]
        odd = (yh % 2).astype(jnp.int32)[None]
        qkv_send = packed_copies(odd, *q)
    with jax.named_scope("out_yh"):
        o = [output_weight[:128], output_weight[128:]]
        o = [jnp.where(first, o[k], o[1 - k]) for k in range(2)]
        o, qkv_send = lax.optimization_barrier((o, qkv_send))
        o = [lax.ppermute(o[k], ("yh", "c"), head_perm(k)) for k in range(2)]


    swap = [(0, 1), (1, 0)]
    with jax.named_scope("tokens_z"):
        x_all = lax.all_gather(gained, "z", axis=0)
    with jax.named_scope("qkv_rep"):
        qkv_own = lax.all_to_all(qkv_send, ("yl", "x"), 0, 0)
        qkv_other = lax.ppermute(qkv_own, "c", swap)
    with jax.named_scope("out_rep"):
        o, x_all = lax.optimization_barrier((o, x_all))
        out_part = jnp.concatenate([jnp.where(even, o[k], o[1 - k]) for k in range(2)], axis=0)
        out_own = lax.all_gather(out_part, ("yl", "x"), axis=0)
    parts = project(core, x_all, qkv_own, qkv_other, tokens)
    with jax.named_scope("qkv_sum"):
        parts = lax.all_to_all(parts, "yh", 0, 0)
    with jax.named_scope("qkv_z"):
        messages = lax.all_gather(summed(parts), "z", axis=0)
    out_own, messages = lax.optimization_barrier((out_own, messages))
    out_other = lax.ppermute(out_own, "c", swap)
    attended = attend(row_lengths, messages)
    parts = output_products(core, attended, out_own, out_other)
    with jax.named_scope("out_sum"):
        parts = lax.all_to_all(parts, "yh", 0, 0)

    heads = jnp.concatenate([(final_gain[:, None] * value_head).T, jnp.zeros((2, tokens.shape[1]), F32)], axis=0)
    resid_out, stat = resid_and_stats(parts, tokens, heads)

    with jax.named_scope("stat_tp"):
        stat = lax.all_to_all(stat, TP, 0, 0).astype(F32).sum(axis=0)
    logits = stat[:6] * lax.rsqrt(stat[6] / WIDTH + EPS)[None, :]
    position = jnp.arange(rows // row_lengths.shape[0], dtype=jnp.int32)
    live = (position[None, :] < row_lengths[:, None]).reshape(1, rows)
    scores = jnp.where(live, logits, F32(0.0)).T
    return resid_out, scores


def solution(mesh):
    split = Mesh(mesh.devices.reshape(NZ, NYH, NYL, NX, NC), TP + REP)
    in_specs = (
        P(REP, TP),
        P(REP),
        P(TP),
        P(REP, TP),
        P(REP, TP),
        P(REP, TP),
        P(REP, TP),
        P(TP),
        P(TP, None),
    )
    out_specs = (P(REP, TP), P(REP, None))
    return jax.shard_map(local, mesh=split, in_specs=in_specs, out_specs=out_specs, check_vma=False)
```

time: 191 us -> 184 us (0.963)
  waiting for transfers between devices: 91.6 us -> 53.9 us
  blocking collectives: 22 us -> 55.2 us
  local copies, waits for them, and re-layouts: 5.66 us -> 2.35 us
    all_gather x0 -> x1, blocking collectives: none -> 33.1 us  [local(): messages = lax.all_gather(summed(parts), 'z', axis=0)]
    all_gather x1, waiting for transfers between devices: 20.2 us -> 0.38 us  [local(): x_all = lax.all_gather(gained, 'z', axis=0)]
    all_gather x1, waiting for transfers between devices: 13.3 us -> 0.01 us  [local(): out_own = lax.all_gather(out_part, ('yl', 'x'), axis=0)]
    all_to_all x2 -> x1, waiting for transfers between devices: 19.3 us -> 8.33 us  [local(): qkv_own = lax.all_to_all(qkv_send, ('yl', 'x'), 0, 0)]
    ppermute x4 -> x5, waiting for transfers between devices: 4.54 us -> 11.8 us  [the longest x2 11.7 us: local(): lax.ppermute(jnp.where(first, q[k], q[1 - k]), ('yh', 'c'), head_perm(k))]
    ppermute x4 -> x5, starting transfers between devices: 15 us -> 21.1 us  [the longest x2 11.7 us: local(): lax.ppermute(jnp.where(first, q[k], q[1 - k]), ('yh', 'c'), head_perm(k))]
    all_to_all x2 -> x1, starting transfers between devices: 9.48 us -> 5.72 us  [local(): qkv_own = lax.all_to_all(qkv_send, ('yl', 'x'), 0, 0)]
    ppermute x1, waiting for transfers between devices: 2.84 us -> 0.48 us  [local(): out_other = lax.ppermute(out_own, 'c', swap)]
  transfers between devices with their start and end apart: 12 -> 12, of which waited for: 8 -> 6; matrix products, arithmetic and copies ran while one was open for 2% -> 2% of each run, Pallas kernels for 2% -> 3%
where the time goes in v3:
time: 184 us; the launch traced here: 183 us
  blocking collectives  55.2 us (30%)
  waiting for transfers between devices  53.9 us (29%)
  starting transfers between devices  43.9 us (24%)
  between operations  14.3 us (8%)
  Pallas kernels  9.32 us (5%)
  other arithmetic  3.89 us (2%)
  local copies, waits for them, and re-layouts  2.35 us (1%)
    all_gather x1, blocking collectives, local(): messages = lax.all_gather(summed(parts), 'z', axis=0)  33.1 us
    all_to_all x1, blocking collectives, local(): parts = lax.all_to_all(parts, 'yh', 0, 0)  22.2 us
    all_to_all x1, waiting for transfers between devices, local(): parts = lax.all_to_all(parts, 'yh', 0, 0)  20.5 us
    all_to_all x1, waiting for transfers between devices, local(): stat = lax.all_to_all(stat, TP, 0, 0).astype(F32).sum(axis=0)  12.4 us
    ppermute x2, waiting for transfers between devices, local(): lax.ppermute(jnp.where(first, q[k], q[1 - k]), ('yh', 'c'), head_perm(k))  11.7 us
    ppermute x2, starting transfers between devices, local(): lax.ppermute(jnp.where(first, q[k], q[1 - k]), ('yh', 'c'), head_perm(k))  11.7 us
    ppermute x2, starting transfers between devices, local(): o = [lax.ppermute(o[k], ('yh', 'c'), head_perm(k)) for k in range(2)]  8.67 us
    all_to_all x1, waiting for transfers between devices, local(): qkv_own = lax.all_to_all(qkv_send, ('yl', 'x'), 0, 0)  8.33 us
  transfers between devices with their start and end apart: 12, of which 6 were waited for; matrix products, arithmetic and copies ran while one was open for 2% of the time, Pallas kernels for 3%

profile of v3, /device:TPU:6, one launch (start us, length us, event | category | flops | bytes accessed | tf_op | source)
XLA Modules:
  0.0 182.9 jit_solution(9876932178314751664)
XLA Ops:
  7.2 0.0 copy-start.4
  7.2 0.0 all-gather.6.cloned.1.call-start
  7.2 0.8 pad_maximum_fusion.3
  8.0 0.7 collective-permute-start
  8.6 1.6 multiply_convert_fusion
  10.3 0.0 all-gather.6.cloned.1.call-update
  10.3 0.8 fusion.5
  11.2 0.0 collective-permute-done
  11.2 0.7 collective-permute-start.1
  11.9 11.1 %collective-permute-start.2 = (bf16[160,256]{1,0:T(8,128)(2,1)S(1)}, bf16[160,256]{1,0:T(8,128)(2,1)S(1)}, u32[]{:S(2)}, u32[]{:S(2)}) collective-permute-start(bf16[160,256]{1,0:T(8,128)(2,1)S(1)} %get-tuple-element.22), channel_id=1, source_target_pairs={{0,16},{1,48},{16,17},{17,49},{32,0},{33,32},{48,1},{49,33},{2,18}... | collective-permute-start | bytes 245768 | tf_op jit(solution)/shard_map/weights_yh/ppermute | solution.py:292
  23.0 0.0 copy-done.4
  23.0 0.0 collective-permute-done.1.q0
  23.0 11.7 %collective-permute-done.2.q1 = bf16[160,256]{1,0:T(8,128)(2,1)S(1)} collective-permute-done((bf16[160,256]{1,0:T(8,128)(2,1)S(1)}, bf16[160,256]{1,0:T(8,128)(2,1)S(1)}, u32[]{:S(2)}, u32[]{:S(2)}) %collective-permute-start.2) | collective-permute-done | bytes 81952 | tf_op jit(solution)/shard_map/weights_yh/ppermute | solution.py:292
  34.8 1.2 weights_yh.1
  36.0 5.7 %all-to-all-start = ((bf16[8,320,256]{2,1,0:T(8,128)(2,1)}), bf16[8,320,256]{2,1,0:T(8,128)(2,1)S(1)}, u32[]{:S(2)}, u32[]{:S(2)}) async-start(bf16[8,320,256]{2,1,0:T(8,128)(2,1)} %weights_yh.1), calls=%async_computation | async-start | bytes 2621440 | tf_op jit(solution)/shard_map/qkv_rep/all_to_all | solution.py:308
  41.7 0.0 all-gather.8.cloned.1.call-start
  41.7 0.7 collective-permute-start.3
  42.3 8.0 %collective-permute-start.4 = (bf16[128,256]{1,0:T(8,128)(2,1)S(1)}, bf16[128,256]{1,0:T(8,128)(2,1)S(1)}, u32[]{:S(2)}, u32[]{:S(2)}) collective-permute-start(bf16[128,256]{1,0:T(8,128)(2,1)S(1)} %get-tuple-element.13), channel_id=1, source_target_pairs={{0,16},{1,48},{16,17},{17,49},{32,0},{33,32},{48,1},{49,33},{2,18}... | collective-permute-start | bytes 196616 | tf_op jit(solution)/shard_map/out_yh/ppermute | solution.py:301
  50.4 8.3 %all-to-all-done.w_ref = bf16[8,320,256]{2,1,0:T(8,128)(2,1)S(1)} async-done(((bf16[8,320,256]{2,1,0:T(8,128)(2,1)}), bf16[8,320,256]{2,1,0:T(8,128)(2,1)S(1)}, u32[]{:S(2)}, u32[]{:S(2)}) %all-to-all-start) | async-done | bytes 1310752 | tf_op jit(solution)/shard_map/qkv_rep/all_to_all | solution.py:308
  58.7 3.8 %collective-permute-start.5 = (bf16[8,320,256]{2,1,0:T(8,128)(2,1)S(1)}, bf16[8,320,256]{2,1,0:T(8,128)(2,1)S(1)}, u32[]{:S(2)}, u32[]{:S(2)}) collective-permute-start(bf16[8,320,256]{2,1,0:T(8,128)(2,1)S(1)} %all-to-all-done.w_ref), channel_id=1, source_target_pairs={{0,1},{1,0},{2,3},{3,2},{4,5},{5,4},{6,7},{7,6},{8,9},{9,8},{10,11... | collective-permute-start | bytes 3932168 | tf_op jit(solution)/shard_map/qkv_rep/ppermute | solution.py:309
  62.5 0.0 collective-permute-done.3
  62.5 0.0 collective-permute-done.4
  62.5 0.4 all-gather.6.cloned.1.call-done
  62.9 0.7 pad_maximum_fusion
  63.6 0.0 all-gather.8.cloned.1.call-update
  63.6 1.4 copy-done
  65.0 1.3 shard_map.104.first_ref
  66.4 0.0 collective-permute-done.5.w_ref
  66.4 1.0 shard_map.105
  67.4 0.0 copy-start.3
  67.4 22.2 %all_to_all.20.p_ref = bf16[4,496,128]{2,1,0:T(8,128)(2,1)S(1)} all-to-all(bf16[4,496,128]{2,1,0:T(8,128)(2,1)S(1)} %shard_map.105), channel_id=1, replica_groups=mesh['z'=8,'yh'=4,'yl'=2,'x'=4,'c'=2] {'yh'}, dimensions={0} | all-to-all | bytes 1015808 | tf_op jit(solution)/shard_map/qkv_sum/all_to_all | solution.py:316
  89.6 0.1 qkv_z.1
  89.6 33.1 %all-gather.2 = bf16[3968,128]{1,0:T(8,128)(2,1)S(1)} all-gather(bf16[496,128]{1,0:T(8,128)(2,1)S(1)} %qkv_z.1), channel_id=4, replica_groups=mesh['z'=8,'yh'=4,'yl'=2,'x'=4,'c'=2] {'z'}, dimensions={0}, use_global_device_ids=true | all-gather | bytes 1142784 | tf_op jit(solution)/shard_map/qkv_z/all_gather | solution.py:318
  122.7 2.0 %collective-permute-start.6 = (bf16[8,256,256]{2,1,0:T(8,128)(2,1)}, bf16[8,256,256]{2,1,0:T(8,128)(2,1)S(1)}, u32[]{:S(2)}, u32[]{:S(2)}) collective-permute-start(bf16[8,256,256]{2,1,0:T(8,128)(2,1)} %bitcast.13), channel_id=1, source_target_pairs={{0,1},{1,0},{2,3},{3,2},{4,5},{5,4},{6,7},{7,6},{8,9},{9,8},{10,11... | collective-permute-start | bytes 3145736 | tf_op jit(solution)/shard_map/ppermute | solution.py:320
  124.8 0.0 copy-done.3
  124.8 2.3 %shard_map.106.att_ref = bf16[384,1024]{1,0:T(8,128)(2,1)S(1)} custom-call(s32[2]{0:T(128)S(1)} %copy-done.3, bf16[8,496,128]{2,1,0:T(8,128)(2,1)S(1)} %bitcast.15), custom_call_target="tpu_custom_call" | custom-call | flops 8000000000 | bytes 2000000 | tf_op jit(solution)/shard_map/pallas_call | solution.py:205
  127.1 0.5 collective-permute-done.6.other_ref
  127.6 0.0 copy-done.1
  127.6 1.9 %shard_map.107 = bf16[4,384,256]{2,1,0:T(8,128)(2,1)} custom-call(s32[1]{0:T(128)} %bitcast.core_ref, bf16[384,1024]{1,0:T(8,128)(2,1)S(1)} %shard_map.106.att_ref, bf16[8,256,256]{2,1,0:T(8,128)(2,1)S(1)} %bitcast.14, bf16[8,256,256]{2,1,0:T(8,128)(2,1)S(1)} %collective-permute-done.6.other_ref), custom_call_target="tpu_custom_call" | custom-call | flops 805306368 | bytes 5000000 | tf_op jit(solution)/shard_map/pallas_call | solution.py:219
  129.5 4.1 %all-to-all-start.2 = ((bf16[4,384,256]{2,1,0:T(8,128)(2,1)}), bf16[4,384,256]{2,1,0:T(8,128)(2,1)S(1)}, u32[]{:S(2)}, u32[]{:S(2)}) async-start(bf16[4,384,256]{2,1,0:T(8,128)(2,1)} %shard_map.107), calls=%async_computation.2 | async-start | bytes 1572864 | tf_op jit(solution)/shard_map/out_sum/all_to_all | solution.py:324
  133.6 0.0 copy-done.6
  133.7 20.5 %all-to-all-done.2.p_ref = bf16[4,384,256]{2,1,0:T(8,128)(2,1)S(1)} async-done(((bf16[4,384,256]{2,1,0:T(8,128)(2,1)}), bf16[4,384,256]{2,1,0:T(8,128)(2,1)S(1)}, u32[]{:S(2)}, u32[]{:S(2)}) %all-to-all-start.2) | async-done | bytes 786464 | tf_op jit(solution)/shard_map/out_sum/all_to_all | solution.py:324
  154.2 1.5 shard_map.108
  155.7 7.1 %all-to-all-start.3 = ((bf16[32,8,384]{2,1,0:T(8,128)(2,1)}), bf16[32,8,384]{2,1,0:T(8,128)(2,1)S(1)}, u32[]{:S(2)}, u32[]{:S(2)}) async-start(bf16[32,8,384]{2,1,0:T(8,128)(2,1)} %get-tuple-element.21), calls=%async_computation.3 | async-start | bytes 393216 | tf_op jit(solution)/shard_map/stat_tp/all_to_all | solution.py:330
  162.8 0.1 iota_compare_fusion
  162.9 0.1 lt.32
  163.0 12.4 %all-to-all-done.3 = bf16[32,8,384]{2,1,0:T(8,128)(2,1)S(1)} async-done(((bf16[32,8,384]{2,1,0:T(8,128)(2,1)}), bf16[32,8,384]{2,1,0:T(8,128)(2,1)S(1)}, u32[]{:S(2)}, u32[]{:S(2)}) %all-to-all-start.3) | async-done | bytes 196640 | tf_op jit(solution)/shard_map/stat_tp/all_to_all | solution.py:330
  175.4 0.6 fusion.1
  (16 shorter events, 0.2 us)
Async XLA Ops:
  7.2 15.8 %copy-start.4 = (bf16[256,256]{1,0:T(8,128)(2,1)S(1)}, bf16[256,256]{1,0:T(8,128)(2,1)}, u32[]{:S(2)}) copy-start(bf16[256,256]{1,0:T(8,128)(2,1)} %param.15) | copy-start | bytes 393220
  7.2 55.7 %all-gather.6.cloned.1.call-start = ((), (), s32[]{:S(2)}) async-start(), calls=%async_computation.4 | async-start | bytes 1769472 | tf_op jit(solution)/shard_map/tokens_z/all_gather | solution.py:306
  8.0 3.2 %collective-permute-start = (bf16[32,512]{1,0:T(8,128)(2,1)S(1)}, bf16[32,512]{1,0:T(8,128)(2,1)S(1)}, u32[]{:S(2)}, u32[]{:S(2)}) collective-permute-start(bf16[32,512]{1,0:T(8,128)(2,1)S(1)} %pad_maximum_fusion.3), channel_id=1, source_target_pairs={{0,0},{16,64},{32,128},{48,192},{64,256},{80,320},{96,384},{112,44... | collective-permute-start | bytes 98312 | tf_op jit(solution)/shard_map/weights_yh/ppermute | solution.py:282
  11.2 11.8 %collective-permute-start.1 = (bf16[160,256]{1,0:T(8,128)(2,1)S(1)}, bf16[160,256]{1,0:T(8,128)(2,1)S(1)}, u32[]{:S(2)}, u32[]{:S(2)}) collective-permute-start(bf16[160,256]{1,0:T(8,128)(2,1)S(1)} %get-tuple-element.23), channel_id=1, source_target_pairs={{0,0},{1,32},{16,1},{17,33},{32,16},{33,48},{48,17},{49,49},{2,2},... | collective-permute-start | bytes 245768 | tf_op jit(solution)/shard_map/weights_yh/ppermute | solution.py:292
  11.9 22.9 %collective-permute-start.2 = (bf16[160,256]{1,0:T(8,128)(2,1)S(1)}, bf16[160,256]{1,0:T(8,128)(2,1)S(1)}, u32[]{:S(2)}, u32[]{:S(2)}) collective-permute-start(bf16[160,256]{1,0:T(8,128)(2,1)S(1)} %get-tuple-element.22), channel_id=1, source_target_pairs={{0,16},{1,48},{16,17},{17,49},{32,0},{33,32},{48,1},{49,33},{2,18}... | collective-permute-start | bytes 245768 | tf_op jit(solution)/shard_map/weights_yh/ppermute | solution.py:292
  36.0 27.7 %copy-start.2 = (bf16[384,256]{1,0:T(8,128)(2,1)S(1)}, bf16[384,256]{1,0:T(8,128)(2,1)}, u32[]{:S(2)}) copy-start(bf16[384,256]{1,0:T(8,128)(2,1)} %x_ref.1) | copy-start | bytes 589828
  36.0 22.8 %all-to-all-start = ((bf16[8,320,256]{2,1,0:T(8,128)(2,1)}), bf16[8,320,256]{2,1,0:T(8,128)(2,1)S(1)}, u32[]{:S(2)}, u32[]{:S(2)}) async-start(bf16[8,320,256]{2,1,0:T(8,128)(2,1)} %weights_yh.1), calls=%async_computation | async-start | bytes 2621440 | tf_op jit(solution)/shard_map/qkv_rep/all_to_all | solution.py:308
  41.7 81.0 %all-gather.8.cloned.1.call-start = ((), (), s32[]{:S(2)}) async-start(), calls=%async_computation.5 | async-start | bytes 1179648 | tf_op jit(solution)/shard_map/out_rep/all_gather | solution.py:313
  41.7 20.8 %collective-permute-start.3 = (bf16[128,256]{1,0:T(8,128)(2,1)S(1)}, bf16[128,256]{1,0:T(8,128)(2,1)S(1)}, u32[]{:S(2)}, u32[]{:S(2)}) collective-permute-start(bf16[128,256]{1,0:T(8,128)(2,1)S(1)} %get-tuple-element.12), channel_id=1, source_target_pairs={{0,0},{1,32},{16,1},{17,33},{32,16},{33,48},{48,17},{49,49},{2,2},... | collective-permute-start | bytes 196616 | tf_op jit(solution)/shard_map/out_yh/ppermute | solution.py:301
  42.3 20.2 %collective-permute-start.4 = (bf16[128,256]{1,0:T(8,128)(2,1)S(1)}, bf16[128,256]{1,0:T(8,128)(2,1)S(1)}, u32[]{:S(2)}, u32[]{:S(2)}) collective-permute-start(bf16[128,256]{1,0:T(8,128)(2,1)S(1)} %get-tuple-element.13), channel_id=1, source_target_pairs={{0,16},{1,48},{16,17},{17,49},{32,0},{33,32},{48,1},{49,33},{2,18}... | collective-permute-start | bytes 196616 | tf_op jit(solution)/shard_map/out_yh/ppermute | solution.py:301
  58.7 7.7 %collective-permute-start.5 = (bf16[8,320,256]{2,1,0:T(8,128)(2,1)S(1)}, bf16[8,320,256]{2,1,0:T(8,128)(2,1)S(1)}, u32[]{:S(2)}, u32[]{:S(2)}) collective-permute-start(bf16[8,320,256]{2,1,0:T(8,128)(2,1)S(1)} %all-to-all-done.w_ref), channel_id=1, source_target_pairs={{0,1},{1,0},{2,3},{3,2},{4,5},{5,4},{6,7},{7,6},{8,9},{9,8},{10,11... | collective-permute-start | bytes 3932168 | tf_op jit(solution)/shard_map/qkv_rep/ppermute | solution.py:309
  63.6 1.4 copy-start
  67.4 57.4 %copy-start.3 = (s32[2]{0:T(128)S(1)}, s32[2]{0:T(128)}, u32[]{:S(2)}) copy-start(s32[2]{0:T(128)} %len_ref.1) | copy-start | bytes 28
  122.7 4.9 %copy-start.1 = (bf16[2048,256]{1,0:T(8,128)(2,1)S(1)}, bf16[2048,256]{1,0:T(8,128)(2,1)}, u32[]{:S(2)}) copy-start(bf16[2048,256]{1,0:T(8,128)(2,1)} %all-gather.8.cloned.1.call-done) | copy-start | bytes 3145732
  122.7 4.9 %collective-permute-start.6 = (bf16[8,256,256]{2,1,0:T(8,128)(2,1)}, bf16[8,256,256]{2,1,0:T(8,128)(2,1)S(1)}, u32[]{:S(2)}, u32[]{:S(2)}) collective-permute-start(bf16[8,256,256]{2,1,0:T(8,128)(2,1)} %bitcast.13), channel_id=1, source_target_pairs={{0,1},{1,0},{2,3},{3,2},{4,5},{5,4},{6,7},{7,6},{8,9},{9,8},{10,11... | collective-permute-start | bytes 3145736 | tf_op jit(solution)/shard_map/ppermute | solution.py:320
  129.5 4.1 %copy-start.5 = (f32[256,6]{0,1:T(8,128)S(1)}, f32[256,6]{0,1:T(8,128)}, u32[]{:S(2)}) copy-start(f32[256,6]{0,1:T(8,128)} %param.17) | copy-start | bytes 18436
  129.5 4.1 %copy-start.6 = (f32[256]{0:T(256)S(1)}, f32[256]{0:T(256)}, u32[]{:S(2)}) copy-start(f32[256]{0:T(256)} %param.16) | copy-start | bytes 3076
  129.5 24.7 %all-to-all-start.2 = ((bf16[4,384,256]{2,1,0:T(8,128)(2,1)}), bf16[4,384,256]{2,1,0:T(8,128)(2,1)S(1)}, u32[]{:S(2)}, u32[]{:S(2)}) async-start(bf16[4,384,256]{2,1,0:T(8,128)(2,1)} %shard_map.107), calls=%async_computation.2 | async-start | bytes 1572864 | tf_op jit(solution)/shard_map/out_sum/all_to_all | solution.py:324
  155.7 19.7 %all-to-all-start.3 = ((bf16[32,8,384]{2,1,0:T(8,128)(2,1)}), bf16[32,8,384]{2,1,0:T(8,128)(2,1)S(1)}, u32[]{:S(2)}, u32[]{:S(2)}) async-start(bf16[32,8,384]{2,1,0:T(8,128)(2,1)} %get-tuple-element.21), calls=%async_computation.3 | async-start | bytes 393216 | tf_op jit(solution)/shard_map/stat_tp/all_to_all | solution.py:330
Sparse Core Ops, SparseCore 0:
  10.7 52.2 all-gather.5
  65.6 42.0 all-gather.7

commit v4 on v3

--- a/solution.py
+++ b/solution.py
@@ -186,16 +186,14 @@
             att_ref[seq * half : (seq + 1) * half, head * 128 : (head + 1) * 128] = o.astype(BF16)
 
 
-def output_side(a, w_ref, out_ref, d):
-    for hi in range(2):
-        w = jnp.concatenate([w_ref[k, hi * 128 : (hi + 1) * 128] for k in range(NZ)], axis=0)
-        out_ref[2 * hi + d] = jnp.dot(a, w, preferred_element_type=F32).astype(BF16)
-
-
-def output_kernel(core_ref, att_ref, own_ref, other_ref, out_ref):
-    core = core_ref[0]
-    output_side(att_ref[...], own_ref, out_ref, core)
-    output_side(att_ref[...], other_ref, out_ref, 1 - core)
+def output_kernel(att_ref, w_ref, out_ref):
+    a = att_ref[...]
+    for d in range(2):
+        for hi in range(2):
+            w = jnp.concatenate(
+                [w_ref[2 * k + d, hi * 128 : (hi + 1) * 128] for k in range(NZ)], axis=0
+            )
+            out_ref[2 * hi + d] = jnp.dot(a, w, preferred_element_type=F32).astype(BF16)
 
 
 def attend(lengths, messages):
@@ -212,18 +210,17 @@
     )(lengths, messages)
 
 
-def output_products(core, attended, own, other):
+def output_products(attended, weights):
     rows = attended.shape[0]
     vmem = pl.BlockSpec(memory_space=pltpu.VMEM)
-    smem = pl.BlockSpec(memory_space=pltpu.SMEM)
     return pl.pallas_call(
         output_kernel,
-        in_specs=[smem, vmem, vmem, vmem],
+        in_specs=[vmem, vmem],
         out_specs=vmem,
         out_shape=jax.ShapeDtypeStruct((4, rows, 256), BF16),
         compiler_params=pltpu.CompilerParams(vmem_limit_bytes=VMEM),
         cost_estimate=pl.CostEstimate(flops=2 * rows * 1024 * 1024, bytes_accessed=5_000_000, transcendentals=0),
-    )(core, attended, own, other)
+    )(attended, weights)
 
 
 def resid_kernel(p_ref, x_ref, head_ref, resid_ref, stat_ref):
@@ -281,12 +278,7 @@
     with jax.named_scope("weights_yh"):
         kv = lax.ppermute(jnp.concatenate([key_weight.T, value_matrix.T], axis=0), TP, kv_perm())
         q = [query_weight[256 * b : 256 * (b + 1)] for b in range(2)]
-        q = [
-            jnp.concatenate(
-                [q[b][:128], q[b][128:]], axis=1
-            )
-            for b in range(2)
-        ]
+        q = [jnp.concatenate([one[:128], one[128:]], axis=1) for one in q]
         q = [jnp.concatenate([q[b], kv[:, 256 * b : 256 * (b + 1)]], axis=0) for b in range(2)]
         q = [
             lax.ppermute(jnp.where(first, q[k], q[1 - k]), ("yh", "c"), head_perm(k))
@@ -310,16 +302,15 @@
     with jax.named_scope("out_rep"):
         o, x_all = lax.optimization_barrier((o, x_all))
         out_part = jnp.concatenate([jnp.where(even, o[k], o[1 - k]) for k in range(2)], axis=0)
-        out_own = lax.all_gather(out_part, ("yl", "x"), axis=0)
+        out_all = lax.all_gather(out_part, REP, axis=0)
     parts = project(core, x_all, qkv_own, qkv_other, tokens)
     with jax.named_scope("qkv_sum"):
         parts = lax.all_to_all(parts, "yh", 0, 0)
     with jax.named_scope("qkv_z"):
         messages = lax.all_gather(summed(parts), "z", axis=0)
-    out_own, messages = lax.optimization_barrier((out_own, messages))
-    out_other = lax.ppermute(out_own, "c", swap)
+    out_all, messages = lax.optimization_barrier((out_all, messages))
     attended = attend(row_lengths, messages)
-    parts = output_products(core, attended, out_own, out_other)
+    parts = output_products(attended, out_all)
     with jax.named_scope("out_sum"):
         parts = lax.all_to_all(parts, "yh", 0, 0)
 

time: 184 us -> 175 us (0.951)
  waiting for transfers between devices: 53.9 us -> 45.8 us
    all_to_all x1, waiting for transfers between devices: 20.5 us -> 13 us  [local(): parts = lax.all_to_all(parts, 'yh', 0, 0)]
    ppermute x1 -> x0, starting transfers between devices: 2.04 us -> none  [local(): out_other = lax.ppermute(out_own, 'c', swap)]
  transfers between devices with their start and end apart: 12 -> 11, of which waited for: 6 -> 5; matrix products, arithmetic and copies ran while one was open for 2% -> 2% of each run, Pallas kernels for 3% -> 2%
where the time goes in v4:
time: 175 us; the launch traced here: 174 us
  blocking collectives  56 us (32%)
  waiting for transfers between devices  45.8 us (26%)
  starting transfers between devices  42.7 us (24%)
  between operations  14.3 us (8%)
  Pallas kernels  9.28 us (5%)
  other arithmetic  3.89 us (2%)
  local copies, waits for them, and re-layouts  2.35 us (1%)
    all_gather x1, blocking collectives, local(): messages = lax.all_gather(summed(parts), 'z', axis=0)  34.1 us
    all_to_all x1, blocking collectives, local(): parts = lax.all_to_all(parts, 'yh', 0, 0)  21.9 us
    all_to_all x1, waiting for transfers between devices, local(): parts = lax.all_to_all(parts, 'yh', 0, 0)  13 us
    all_to_all x1, waiting for transfers between devices, local(): stat = lax.all_to_all(stat, TP, 0, 0).astype(F32).sum(axis=0)  12.4 us
    ppermute x2, waiting for transfers between devices, local(): lax.ppermute(jnp.where(first, q[k], q[1 - k]), ('yh', 'c'), head_perm(k))  11.7 us
    ppermute x2, starting transfers between devices, local(): lax.ppermute(jnp.where(first, q[k], q[1 - k]), ('yh', 'c'), head_perm(k))  11.7 us
    ppermute x2, starting transfers between devices, local(): o = [lax.ppermute(o[k], ('yh', 'c'), head_perm(k)) for k in range(2)]  8.67 us
    all_to_all x1, waiting for transfers between devices, local(): qkv_own = lax.all_to_all(qkv_send, ('yl', 'x'), 0, 0)  8.33 us
  transfers between devices with their start and end apart: 11, of which 5 were waited for; matrix products, arithmetic and copies ran while one was open for 2% of the time, Pallas kernels for 2%

profile of v4, /device:TPU:6, one launch (start us, length us, event | category | flops | bytes accessed | tf_op | source)
XLA Modules:
  0.0 174.3 jit_solution(15024716368175786713)
XLA Ops:
  7.2 0.0 copy-start.4
  7.2 0.0 all-gather.6.cloned.1.call-start
  7.2 0.8 pad_maximum_fusion.3
  8.0 0.7 collective-permute-start
  8.6 1.6 multiply_convert_fusion
  10.3 0.0 all-gather.6.cloned.1.call-update
  10.3 0.8 fusion.5
  11.2 0.0 collective-permute-done
  11.2 0.7 collective-permute-start.1
  11.9 11.1 %collective-permute-start.2 = (bf16[160,256]{1,0:T(8,128)(2,1)S(1)}, bf16[160,256]{1,0:T(8,128)(2,1)S(1)}, u32[]{:S(2)}, u32[]{:S(2)}) collective-permute-start(bf16[160,256]{1,0:T(8,128)(2,1)S(1)} %get-tuple-element.22), channel_id=1, source_target_pairs={{0,16},{1,48},{16,17},{17,49},{32,0},{33,32},{48,1},{49,33},{2,18}... | collective-permute-start | bytes 245768 | tf_op jit(solution)/shard_map/weights_yh/ppermute | solution.py:284
  23.0 0.0 copy-done.4
  23.0 0.0 collective-permute-done.1.q0
  23.0 11.7 %collective-permute-done.2.q1 = bf16[160,256]{1,0:T(8,128)(2,1)S(1)} collective-permute-done((bf16[160,256]{1,0:T(8,128)(2,1)S(1)}, bf16[160,256]{1,0:T(8,128)(2,1)S(1)}, u32[]{:S(2)}, u32[]{:S(2)}) %collective-permute-start.2) | collective-permute-done | bytes 81952 | tf_op jit(solution)/shard_map/weights_yh/ppermute | solution.py:284
  34.8 1.2 weights_yh.1
  36.0 5.7 %all-to-all-start = ((bf16[8,320,256]{2,1,0:T(8,128)(2,1)}), bf16[8,320,256]{2,1,0:T(8,128)(2,1)S(1)}, u32[]{:S(2)}, u32[]{:S(2)}) async-start(bf16[8,320,256]{2,1,0:T(8,128)(2,1)} %weights_yh.1), calls=%async_computation | async-start | bytes 2621440 | tf_op jit(solution)/shard_map/qkv_rep/all_to_all | solution.py:300
  41.7 0.0 all-gather.8.cloned.1.call-start
  41.7 0.7 collective-permute-start.3
  42.3 8.0 %collective-permute-start.4 = (bf16[128,256]{1,0:T(8,128)(2,1)S(1)}, bf16[128,256]{1,0:T(8,128)(2,1)S(1)}, u32[]{:S(2)}, u32[]{:S(2)}) collective-permute-start(bf16[128,256]{1,0:T(8,128)(2,1)S(1)} %get-tuple-element.13), channel_id=1, source_target_pairs={{0,16},{1,48},{16,17},{17,49},{32,0},{33,32},{48,1},{49,33},{2,18}... | collective-permute-start | bytes 196616 | tf_op jit(solution)/shard_map/out_yh/ppermute | solution.py:293
  50.4 8.3 %all-to-all-done.w_ref = bf16[8,320,256]{2,1,0:T(8,128)(2,1)S(1)} async-done(((bf16[8,320,256]{2,1,0:T(8,128)(2,1)}), bf16[8,320,256]{2,1,0:T(8,128)(2,1)S(1)}, u32[]{:S(2)}, u32[]{:S(2)}) %all-to-all-start) | async-done | bytes 1310752 | tf_op jit(solution)/shard_map/qkv_rep/all_to_all | solution.py:300
  58.7 3.8 %collective-permute-start.5 = (bf16[8,320,256]{2,1,0:T(8,128)(2,1)S(1)}, bf16[8,320,256]{2,1,0:T(8,128)(2,1)S(1)}, u32[]{:S(2)}, u32[]{:S(2)}) collective-permute-start(bf16[8,320,256]{2,1,0:T(8,128)(2,1)S(1)} %all-to-all-done.w_ref), channel_id=1, source_target_pairs={{0,1},{1,0},{2,3},{3,2},{4,5},{5,4},{6,7},{7,6},{8,9},{9,8},{10,11... | collective-permute-start | bytes 3932168 | tf_op jit(solution)/shard_map/qkv_rep/ppermute | solution.py:301
  62.5 0.0 collective-permute-done.3
  62.5 0.0 collective-permute-done.4
  62.5 0.4 all-gather.6.cloned.1.call-done
  62.9 0.7 pad_maximum_fusion
  63.6 0.0 all-gather.8.cloned.1.call-update
  63.6 0.0 copy-done.2
  63.6 0.0 copy-start.1
  63.6 1.4 copy-done.1
  65.0 1.3 shard_map.104.first_ref
  66.4 0.0 collective-permute-done.5.w_ref
  66.4 1.0 shard_map.105
  67.4 0.0 copy-start.3
  67.4 21.9 %all_to_all.20.p_ref = bf16[4,496,128]{2,1,0:T(8,128)(2,1)S(1)} all-to-all(bf16[4,496,128]{2,1,0:T(8,128)(2,1)S(1)} %shard_map.105), channel_id=1, replica_groups=mesh['z'=8,'yh'=4,'yl'=2,'x'=4,'c'=2] {'yh'}, dimensions={0} | all-to-all | bytes 1015808 | tf_op jit(solution)/shard_map/qkv_sum/all_to_all | solution.py:308
  89.3 0.1 qkv_z.1
  89.4 34.1 %all-gather.2 = bf16[3968,128]{1,0:T(8,128)(2,1)S(1)} all-gather(bf16[496,128]{1,0:T(8,128)(2,1)S(1)} %qkv_z.1), channel_id=4, replica_groups=mesh['z'=8,'yh'=4,'yl'=2,'x'=4,'c'=2] {'z'}, dimensions={0}, use_global_device_ids=true | all-gather | bytes 1142784 | tf_op jit(solution)/shard_map/qkv_z/all_gather | solution.py:310
  123.5 0.0 copy-done.3
  123.5 2.3 %shard_map.106.att_ref = bf16[384,1024]{1,0:T(8,128)(2,1)S(1)} custom-call(s32[2]{0:T(128)S(1)} %copy-done.3, bf16[8,496,128]{2,1,0:T(8,128)(2,1)S(1)} %bitcast.14), custom_call_target="tpu_custom_call" | custom-call | flops 8000000000 | bytes 2000000 | tf_op jit(solution)/shard_map/pallas_call | solution.py:203
  125.8 0.0 copy-done
  125.8 1.9 %shard_map.107 = bf16[4,384,256]{2,1,0:T(8,128)(2,1)} custom-call(bf16[384,1024]{1,0:T(8,128)(2,1)S(1)} %shard_map.106.att_ref, bf16[16,256,256]{2,1,0:T(8,128)(2,1)S(1)} %bitcast.11), custom_call_target="tpu_custom_call" | custom-call | flops 805306368 | bytes 5000000 | tf_op jit(solution)/shard_map/pallas_call | solution.py:216
  127.7 4.2 %all-to-all-start.2 = ((bf16[4,384,256]{2,1,0:T(8,128)(2,1)}), bf16[4,384,256]{2,1,0:T(8,128)(2,1)S(1)}, u32[]{:S(2)}, u32[]{:S(2)}) async-start(bf16[4,384,256]{2,1,0:T(8,128)(2,1)} %shard_map.107), calls=%async_computation.2 | async-start | bytes 1572864 | tf_op jit(solution)/shard_map/out_sum/all_to_all | solution.py:315
  131.8 0.0 copy-done.5
  131.9 13.0 %all-to-all-done.2.p_ref = bf16[4,384,256]{2,1,0:T(8,128)(2,1)S(1)} async-done(((bf16[4,384,256]{2,1,0:T(8,128)(2,1)}), bf16[4,384,256]{2,1,0:T(8,128)(2,1)S(1)}, u32[]{:S(2)}, u32[]{:S(2)}) %all-to-all-start.2) | async-done | bytes 786464 | tf_op jit(solution)/shard_map/out_sum/all_to_all | solution.py:315
  144.8 1.5 shard_map.108
  146.3 7.9 %all-to-all-start.3 = ((bf16[32,8,384]{2,1,0:T(8,128)(2,1)}), bf16[32,8,384]{2,1,0:T(8,128)(2,1)S(1)}, u32[]{:S(2)}, u32[]{:S(2)}) async-start(bf16[32,8,384]{2,1,0:T(8,128)(2,1)} %get-tuple-element.21), calls=%async_computation.3 | async-start | bytes 393216 | tf_op jit(solution)/shard_map/stat_tp/all_to_all | solution.py:321
  154.3 0.1 iota_compare_fusion
  154.3 0.1 lt.32
  154.4 12.4 %all-to-all-done.3 = bf16[32,8,384]{2,1,0:T(8,128)(2,1)S(1)} async-done(((bf16[32,8,384]{2,1,0:T(8,128)(2,1)}), bf16[32,8,384]{2,1,0:T(8,128)(2,1)S(1)}, u32[]{:S(2)}, u32[]{:S(2)}) %all-to-all-start.3) | async-done | bytes 196640 | tf_op jit(solution)/shard_map/stat_tp/all_to_all | solution.py:321
  166.9 0.6 fusion.1
  (14 shorter events, 0.2 us)
Async XLA Ops:
  7.2 15.8 %copy-start.4 = (bf16[256,256]{1,0:T(8,128)(2,1)S(1)}, bf16[256,256]{1,0:T(8,128)(2,1)}, u32[]{:S(2)}) copy-start(bf16[256,256]{1,0:T(8,128)(2,1)} %param.15) | copy-start | bytes 393220
  7.2 55.7 %all-gather.6.cloned.1.call-start = ((), (), s32[]{:S(2)}) async-start(), calls=%async_computation.4 | async-start | bytes 1769472 | tf_op jit(solution)/shard_map/tokens_z/all_gather | solution.py:298
  8.0 3.2 %collective-permute-start = (bf16[32,512]{1,0:T(8,128)(2,1)S(1)}, bf16[32,512]{1,0:T(8,128)(2,1)S(1)}, u32[]{:S(2)}, u32[]{:S(2)}) collective-permute-start(bf16[32,512]{1,0:T(8,128)(2,1)S(1)} %pad_maximum_fusion.3), channel_id=1, source_target_pairs={{0,0},{16,64},{32,128},{48,192},{64,256},{80,320},{96,384},{112,44... | collective-permute-start | bytes 98312 | tf_op jit(solution)/shard_map/weights_yh/ppermute | solution.py:279
  11.2 11.8 %collective-permute-start.1 = (bf16[160,256]{1,0:T(8,128)(2,1)S(1)}, bf16[160,256]{1,0:T(8,128)(2,1)S(1)}, u32[]{:S(2)}, u32[]{:S(2)}) collective-permute-start(bf16[160,256]{1,0:T(8,128)(2,1)S(1)} %get-tuple-element.23), channel_id=1, source_target_pairs={{0,0},{1,32},{16,1},{17,33},{32,16},{33,48},{48,17},{49,49},{2,2},... | collective-permute-start | bytes 245768 | tf_op jit(solution)/shard_map/weights_yh/ppermute | solution.py:284
  11.9 22.9 %collective-permute-start.2 = (bf16[160,256]{1,0:T(8,128)(2,1)S(1)}, bf16[160,256]{1,0:T(8,128)(2,1)S(1)}, u32[]{:S(2)}, u32[]{:S(2)}) collective-permute-start(bf16[160,256]{1,0:T(8,128)(2,1)S(1)} %get-tuple-element.22), channel_id=1, source_target_pairs={{0,16},{1,48},{16,17},{17,49},{32,0},{33,32},{48,1},{49,33},{2,18}... | collective-permute-start | bytes 245768 | tf_op jit(solution)/shard_map/weights_yh/ppermute | solution.py:284
  35.9 27.7 %copy-start.2 = (bf16[384,256]{1,0:T(8,128)(2,1)S(1)}, bf16[384,256]{1,0:T(8,128)(2,1)}, u32[]{:S(2)}) copy-start(bf16[384,256]{1,0:T(8,128)(2,1)} %x_ref.1) | copy-start | bytes 589828
  36.0 22.8 %all-to-all-start = ((bf16[8,320,256]{2,1,0:T(8,128)(2,1)}), bf16[8,320,256]{2,1,0:T(8,128)(2,1)S(1)}, u32[]{:S(2)}, u32[]{:S(2)}) async-start(bf16[8,320,256]{2,1,0:T(8,128)(2,1)} %weights_yh.1), calls=%async_computation | async-start | bytes 2621440 | tf_op jit(solution)/shard_map/qkv_rep/all_to_all | solution.py:300
  41.7 81.8 %all-gather.8.cloned.1.call-start = ((), (), s32[]{:S(2)}) async-start(), calls=%async_computation.5 | async-start | bytes 2228224 | tf_op jit(solution)/shard_map/out_rep/all_gather | solution.py:305
  41.7 20.8 %collective-permute-start.3 = (bf16[128,256]{1,0:T(8,128)(2,1)S(1)}, bf16[128,256]{1,0:T(8,128)(2,1)S(1)}, u32[]{:S(2)}, u32[]{:S(2)}) collective-permute-start(bf16[128,256]{1,0:T(8,128)(2,1)S(1)} %get-tuple-element.12), channel_id=1, source_target_pairs={{0,0},{1,32},{16,1},{17,33},{32,16},{33,48},{48,17},{49,49},{2,2},... | collective-permute-start | bytes 196616 | tf_op jit(solution)/shard_map/out_yh/ppermute | solution.py:293
  42.3 20.2 %collective-permute-start.4 = (bf16[128,256]{1,0:T(8,128)(2,1)S(1)}, bf16[128,256]{1,0:T(8,128)(2,1)S(1)}, u32[]{:S(2)}, u32[]{:S(2)}) collective-permute-start(bf16[128,256]{1,0:T(8,128)(2,1)S(1)} %get-tuple-element.13), channel_id=1, source_target_pairs={{0,16},{1,48},{16,17},{17,49},{32,0},{33,32},{48,1},{49,33},{2,18}... | collective-permute-start | bytes 196616 | tf_op jit(solution)/shard_map/out_yh/ppermute | solution.py:293
  58.7 7.7 %collective-permute-start.5 = (bf16[8,320,256]{2,1,0:T(8,128)(2,1)S(1)}, bf16[8,320,256]{2,1,0:T(8,128)(2,1)S(1)}, u32[]{:S(2)}, u32[]{:S(2)}) collective-permute-start(bf16[8,320,256]{2,1,0:T(8,128)(2,1)S(1)} %all-to-all-done.w_ref), channel_id=1, source_target_pairs={{0,1},{1,0},{2,3},{3,2},{4,5},{5,4},{6,7},{7,6},{8,9},{9,8},{10,11... | collective-permute-start | bytes 3932168 | tf_op jit(solution)/shard_map/qkv_rep/ppermute | solution.py:301
  63.6 1.4 copy-start.1
  67.4 56.1 %copy-start.3 = (s32[2]{0:T(128)S(1)}, s32[2]{0:T(128)}, u32[]{:S(2)}) copy-start(s32[2]{0:T(128)} %len_ref.1) | copy-start | bytes 28
  123.5 2.3 %copy-start = (bf16[4096,256]{1,0:T(8,128)(2,1)S(1)}, bf16[4096,256]{1,0:T(8,128)(2,1)}, u32[]{:S(2)}) copy-start(bf16[4096,256]{1,0:T(8,128)(2,1)} %all-gather.8.cloned.1.call-done) | copy-start | bytes 6291460
  127.7 4.2 %copy-start.5 = (f32[256,6]{0,1:T(8,128)S(1)}, f32[256,6]{0,1:T(8,128)}, u32[]{:S(2)}) copy-start(f32[256,6]{0,1:T(8,128)} %param.17) | copy-start | bytes 18436
  127.7 4.2 %copy-start.6 = (f32[256]{0:T(256)S(1)}, f32[256]{0:T(256)}, u32[]{:S(2)}) copy-start(f32[256]{0:T(256)} %param.16) | copy-start | bytes 3076
  127.7 17.1 %all-to-all-start.2 = ((bf16[4,384,256]{2,1,0:T(8,128)(2,1)}), bf16[4,384,256]{2,1,0:T(8,128)(2,1)S(1)}, u32[]{:S(2)}, u32[]{:S(2)}) async-start(bf16[4,384,256]{2,1,0:T(8,128)(2,1)} %shard_map.107), calls=%async_computation.2 | async-start | bytes 1572864 | tf_op jit(solution)/shard_map/out_sum/all_to_all | solution.py:315
  146.3 20.4 %all-to-all-start.3 = ((bf16[32,8,384]{2,1,0:T(8,128)(2,1)}), bf16[32,8,384]{2,1,0:T(8,128)(2,1)S(1)}, u32[]{:S(2)}, u32[]{:S(2)}) async-start(bf16[32,8,384]{2,1,0:T(8,128)(2,1)} %get-tuple-element.21), calls=%async_computation.3 | async-start | bytes 393216 | tf_op jit(solution)/shard_map/stat_tp/all_to_all | solution.py:321
Sparse Core Ops, SparseCore 0:
  10.7 52.2 all-gather.5
  65.6 38.1 all-gather.7

commit v5 on v4

--- a/solution.py
+++ b/solution.py
@@ -91,17 +91,21 @@
         out_ref[2 * hi + d, rows + 96 : rows + 112, :] = stat
 
 
+def row_squares(t):
+    sq = t.astype(F32) * t.astype(F32)
+    high, low = split_sum(sq)
+    ones = jnp.ones((16, t.shape[1]), BF16)
+    total = lax.dot_general(ones, high, NT, preferred_element_type=F32)
+    return total + lax.dot_general(ones, low, NT, preferred_element_type=F32)
+
+
 def stat_rows(sums):
     pairs = [half for one in sums for half in split_sum(one)]
     return jnp.concatenate(pairs + [jnp.zeros((10, 128), BF16)], axis=0)
 
 
 def own_kernel(core_ref, x_ref, w_ref, tokens_ref, out_ref):
-    t = tokens_ref[...].astype(F32)
-    ones = jnp.ones((8, t.shape[1]), F32)
-    sq = lax.dot_general(
-        ones, t * t, NT, precision=lax.Precision.HIGHEST, preferred_element_type=F32
-    )
+    sq = row_squares(tokens_ref[...])
     stat = stat_rows([sq[0:1, 128 * p : 128 * (p + 1)] for p in range(3)])
     project_side(x_ref, w_ref, stat, out_ref, core_ref[0])
 
@@ -227,16 +231,15 @@
     update = jnp.sum(p_ref[...].astype(F32), axis=0)
     resid = (x_ref[...].astype(F32) + update).astype(BF16)
     resid_ref[...] = resid
-    r = resid.astype(F32)
-    scores = lax.dot_general(
-        head_ref[...], r, NT, precision=lax.Precision.HIGHEST, preferred_element_type=F32
-    )
-    ones = jnp.ones((8, r.shape[1]), F32)
-    squares = lax.dot_general(
-        ones, r * r, NT, precision=lax.Precision.HIGHEST, preferred_element_type=F32
+    head = head_ref[...]
+    h1 = head.astype(BF16)
+    h2 = (head - h1.astype(F32)).astype(BF16)
+    h3 = (head - h1.astype(F32) - h2.astype(F32)).astype(BF16)
+    scores = sum(
+        lax.dot_general(h, resid, NT, preferred_element_type=F32) for h in (h3, h2, h1)
     )
     row = lax.broadcasted_iota(jnp.int32, scores.shape, 0)
-    stat = jnp.where(row < 6, scores, squares).astype(BF16)
+    stat = jnp.where(row < 6, scores, row_squares(resid)[0:8]).astype(BF16)
     for k in range(NZ * NYH):
         stat_ref[k] = stat
 

time: 175 us -> 174 us (level)
  no operation moved by 1% of the time
where the time goes in v5:
time: 174 us
  blocking collectives  55.5 us (32%)
  waiting for transfers between devices  46 us (26%)
  starting transfers between devices  43.1 us (25%)
  between operations  14.3 us (8%)
  Pallas kernels  8.72 us (5%)
  other arithmetic  3.89 us (2%)
  local copies, waits for them, and re-layouts  2.35 us (1%)
    all_gather x1, blocking collectives, local(): messages = lax.all_gather(summed(parts), 'z', axis=0)  34 us
    all_to_all x1, blocking collectives, local(): parts = lax.all_to_all(parts, 'yh', 0, 0)  21.5 us
    all_to_all x1, waiting for transfers between devices, local(): parts = lax.all_to_all(parts, 'yh', 0, 0)  13.1 us
    all_to_all x1, waiting for transfers between devices, local(): stat = lax.all_to_all(stat, TP, 0, 0).astype(F32).sum(axis=0)  12.4 us
    ppermute x2, waiting for transfers between devices, local(): lax.ppermute(jnp.where(first, q[k], q[1 - k]), ('yh', 'c'), head_perm(k))  11.7 us
    ppermute x2, starting transfers between devices, local(): lax.ppermute(jnp.where(first, q[k], q[1 - k]), ('yh', 'c'), head_perm(k))  11.7 us
    ppermute x2, starting transfers between devices, local(): o = [lax.ppermute(o[k], ('yh', 'c'), head_perm(k)) for k in range(2)]  8.67 us
    all_to_all x1, waiting for transfers between devices, local(): qkv_own = lax.all_to_all(qkv_send, ('yl', 'x'), 0, 0)  8.33 us
  transfers between devices with their start and end apart: 11, of which 5 were waited for; matrix products, arithmetic and copies ran while one was open for 2% of the time, Pallas kernels for 2%

profile of v5, /device:TPU:6, one launch (start us, length us, event | category | flops | bytes accessed | tf_op | source)
XLA Modules:
  0.0 173.8 jit_solution(12868941389844328770)
XLA Ops:
  7.2 0.0 copy-start.4
  7.2 0.0 all-gather.6.cloned.1.call-start
  7.2 0.8 pad_maximum_fusion.3
  8.0 0.7 collective-permute-start
  8.6 1.6 multiply_convert_fusion
  10.3 0.0 all-gather.6.cloned.1.call-update
  10.3 0.8 fusion.5
  11.2 0.0 collective-permute-done
  11.2 0.7 collective-permute-start.1
  11.9 11.1 %collective-permute-start.2 = (bf16[160,256]{1,0:T(8,128)(2,1)S(1)}, bf16[160,256]{1,0:T(8,128)(2,1)S(1)}, u32[]{:S(2)}, u32[]{:S(2)}) collective-permute-start(bf16[160,256]{1,0:T(8,128)(2,1)S(1)} %get-tuple-element.22), channel_id=1, source_target_pairs={{0,16},{1,48},{16,17},{17,49},{32,0},{33,32},{48,1},{49,33},{2,18}... | collective-permute-start | bytes 245768 | tf_op jit(solution)/shard_map/weights_yh/ppermute | solution.py:287
  23.0 0.0 copy-done.4
  23.0 0.0 collective-permute-done.1.q0
  23.0 11.7 %collective-permute-done.2.q1 = bf16[160,256]{1,0:T(8,128)(2,1)S(1)} collective-permute-done((bf16[160,256]{1,0:T(8,128)(2,1)S(1)}, bf16[160,256]{1,0:T(8,128)(2,1)S(1)}, u32[]{:S(2)}, u32[]{:S(2)}) %collective-permute-start.2) | collective-permute-done | bytes 81952 | tf_op jit(solution)/shard_map/weights_yh/ppermute | solution.py:287
  34.8 1.2 weights_yh.1
  36.0 5.7 %all-to-all-start = ((bf16[8,320,256]{2,1,0:T(8,128)(2,1)}), bf16[8,320,256]{2,1,0:T(8,128)(2,1)S(1)}, u32[]{:S(2)}, u32[]{:S(2)}) async-start(bf16[8,320,256]{2,1,0:T(8,128)(2,1)} %weights_yh.1), calls=%async_computation | async-start | bytes 2621440 | tf_op jit(solution)/shard_map/qkv_rep/all_to_all | solution.py:303
  41.7 0.0 all-gather.8.cloned.1.call-start
  41.7 0.7 collective-permute-start.3
  42.3 8.0 %collective-permute-start.4 = (bf16[128,256]{1,0:T(8,128)(2,1)S(1)}, bf16[128,256]{1,0:T(8,128)(2,1)S(1)}, u32[]{:S(2)}, u32[]{:S(2)}) collective-permute-start(bf16[128,256]{1,0:T(8,128)(2,1)S(1)} %get-tuple-element.13), channel_id=1, source_target_pairs={{0,16},{1,48},{16,17},{17,49},{32,0},{33,32},{48,1},{49,33},{2,18}... | collective-permute-start | bytes 196616 | tf_op jit(solution)/shard_map/out_yh/ppermute | solution.py:296
  50.4 8.3 %all-to-all-done.w_ref = bf16[8,320,256]{2,1,0:T(8,128)(2,1)S(1)} async-done(((bf16[8,320,256]{2,1,0:T(8,128)(2,1)}), bf16[8,320,256]{2,1,0:T(8,128)(2,1)S(1)}, u32[]{:S(2)}, u32[]{:S(2)}) %all-to-all-start) | async-done | bytes 1310752 | tf_op jit(solution)/shard_map/qkv_rep/all_to_all | solution.py:303
  58.7 3.8 %collective-permute-start.5 = (bf16[8,320,256]{2,1,0:T(8,128)(2,1)S(1)}, bf16[8,320,256]{2,1,0:T(8,128)(2,1)S(1)}, u32[]{:S(2)}, u32[]{:S(2)}) collective-permute-start(bf16[8,320,256]{2,1,0:T(8,128)(2,1)S(1)} %all-to-all-done.w_ref), channel_id=1, source_target_pairs={{0,1},{1,0},{2,3},{3,2},{4,5},{5,4},{6,7},{7,6},{8,9},{9,8},{10,11... | collective-permute-start | bytes 3932168 | tf_op jit(solution)/shard_map/qkv_rep/ppermute | solution.py:304
  62.5 0.0 collective-permute-done.3
  62.5 0.0 collective-permute-done.4
  62.5 0.4 all-gather.6.cloned.1.call-done
  62.9 0.7 pad_maximum_fusion
  63.6 0.0 all-gather.8.cloned.1.call-update
  63.6 0.0 copy-done.2
  63.6 0.0 copy-start.1
  63.6 1.4 copy-done.1
  65.0 1.1 shard_map.104.first_ref
  66.2 0.0 collective-permute-done.5.w_ref
  66.2 1.0 shard_map.105
  67.2 0.0 copy-start.3
  67.2 21.5 %all_to_all.20.p_ref = bf16[4,496,128]{2,1,0:T(8,128)(2,1)S(1)} all-to-all(bf16[4,496,128]{2,1,0:T(8,128)(2,1)S(1)} %shard_map.105), channel_id=1, replica_groups=mesh['z'=8,'yh'=4,'yl'=2,'x'=4,'c'=2] {'yh'}, dimensions={0} | all-to-all | bytes 1015808 | tf_op jit(solution)/shard_map/qkv_sum/all_to_all | solution.py:311
  88.8 0.1 qkv_z.1
  88.8 34.0 %all-gather.2 = bf16[3968,128]{1,0:T(8,128)(2,1)S(1)} all-gather(bf16[496,128]{1,0:T(8,128)(2,1)S(1)} %qkv_z.1), channel_id=4, replica_groups=mesh['z'=8,'yh'=4,'yl'=2,'x'=4,'c'=2] {'z'}, dimensions={0}, use_global_device_ids=true | all-gather | bytes 1142784 | tf_op jit(solution)/shard_map/qkv_z/all_gather | solution.py:313
  122.8 0.0 copy-done.3
  122.8 2.3 %shard_map.106.att_ref = bf16[384,1024]{1,0:T(8,128)(2,1)S(1)} custom-call(s32[2]{0:T(128)S(1)} %copy-done.3, bf16[8,496,128]{2,1,0:T(8,128)(2,1)S(1)} %bitcast.14), custom_call_target="tpu_custom_call" | custom-call | flops 8000000000 | bytes 2000000 | tf_op jit(solution)/shard_map/pallas_call | solution.py:207
  125.2 0.0 copy-done
  125.2 1.9 %shard_map.107 = bf16[4,384,256]{2,1,0:T(8,128)(2,1)} custom-call(bf16[384,1024]{1,0:T(8,128)(2,1)S(1)} %shard_map.106.att_ref, bf16[16,256,256]{2,1,0:T(8,128)(2,1)S(1)} %bitcast.11), custom_call_target="tpu_custom_call" | custom-call | flops 805306368 | bytes 5000000 | tf_op jit(solution)/shard_map/pallas_call | solution.py:220
  127.0 4.6 %all-to-all-start.2 = ((bf16[4,384,256]{2,1,0:T(8,128)(2,1)}), bf16[4,384,256]{2,1,0:T(8,128)(2,1)S(1)}, u32[]{:S(2)}, u32[]{:S(2)}) async-start(bf16[4,384,256]{2,1,0:T(8,128)(2,1)} %shard_map.107), calls=%async_computation.2 | async-start | bytes 1572864 | tf_op jit(solution)/shard_map/out_sum/all_to_all | solution.py:318
  131.6 0.0 copy-done.5
  131.7 13.1 %all-to-all-done.2.p_ref = bf16[4,384,256]{2,1,0:T(8,128)(2,1)S(1)} async-done(((bf16[4,384,256]{2,1,0:T(8,128)(2,1)}), bf16[4,384,256]{2,1,0:T(8,128)(2,1)S(1)}, u32[]{:S(2)}, u32[]{:S(2)}) %all-to-all-start.2) | async-done | bytes 786464 | tf_op jit(solution)/shard_map/out_sum/all_to_all | solution.py:318
  144.8 1.1 shard_map.108
  145.9 7.9 %all-to-all-start.3 = ((bf16[32,8,384]{2,1,0:T(8,128)(2,1)}), bf16[32,8,384]{2,1,0:T(8,128)(2,1)S(1)}, u32[]{:S(2)}, u32[]{:S(2)}) async-start(bf16[32,8,384]{2,1,0:T(8,128)(2,1)} %get-tuple-element.21), calls=%async_computation.3 | async-start | bytes 393216 | tf_op jit(solution)/shard_map/stat_tp/all_to_all | solution.py:324
  153.8 0.1 iota_compare_fusion
  153.9 0.1 lt.32
  154.0 12.4 %all-to-all-done.3 = bf16[32,8,384]{2,1,0:T(8,128)(2,1)S(1)} async-done(((bf16[32,8,384]{2,1,0:T(8,128)(2,1)}), bf16[32,8,384]{2,1,0:T(8,128)(2,1)S(1)}, u32[]{:S(2)}, u32[]{:S(2)}) %all-to-all-start.3) | async-done | bytes 196640 | tf_op jit(solution)/shard_map/stat_tp/all_to_all | solution.py:324
  166.4 0.6 fusion.1
  (14 shorter events, 0.2 us)
Async XLA Ops:
  7.2 15.8 %copy-start.4 = (bf16[256,256]{1,0:T(8,128)(2,1)S(1)}, bf16[256,256]{1,0:T(8,128)(2,1)}, u32[]{:S(2)}) copy-start(bf16[256,256]{1,0:T(8,128)(2,1)} %param.15) | copy-start | bytes 393220
  7.2 55.7 %all-gather.6.cloned.1.call-start = ((), (), s32[]{:S(2)}) async-start(), calls=%async_computation.4 | async-start | bytes 1769472 | tf_op jit(solution)/shard_map/tokens_z/all_gather | solution.py:301
  8.0 3.2 %collective-permute-start = (bf16[32,512]{1,0:T(8,128)(2,1)S(1)}, bf16[32,512]{1,0:T(8,128)(2,1)S(1)}, u32[]{:S(2)}, u32[]{:S(2)}) collective-permute-start(bf16[32,512]{1,0:T(8,128)(2,1)S(1)} %pad_maximum_fusion.3), channel_id=1, source_target_pairs={{0,0},{16,64},{32,128},{48,192},{64,256},{80,320},{96,384},{112,44... | collective-permute-start | bytes 98312 | tf_op jit(solution)/shard_map/weights_yh/ppermute | solution.py:282
  11.2 11.8 %collective-permute-start.1 = (bf16[160,256]{1,0:T(8,128)(2,1)S(1)}, bf16[160,256]{1,0:T(8,128)(2,1)S(1)}, u32[]{:S(2)}, u32[]{:S(2)}) collective-permute-start(bf16[160,256]{1,0:T(8,128)(2,1)S(1)} %get-tuple-element.23), channel_id=1, source_target_pairs={{0,0},{1,32},{16,1},{17,33},{32,16},{33,48},{48,17},{49,49},{2,2},... | collective-permute-start | bytes 245768 | tf_op jit(solution)/shard_map/weights_yh/ppermute | solution.py:287
  11.9 22.9 %collective-permute-start.2 = (bf16[160,256]{1,0:T(8,128)(2,1)S(1)}, bf16[160,256]{1,0:T(8,128)(2,1)S(1)}, u32[]{:S(2)}, u32[]{:S(2)}) collective-permute-start(bf16[160,256]{1,0:T(8,128)(2,1)S(1)} %get-tuple-element.22), channel_id=1, source_target_pairs={{0,16},{1,48},{16,17},{17,49},{32,0},{33,32},{48,1},{49,33},{2,18}... | collective-permute-start | bytes 245768 | tf_op jit(solution)/shard_map/weights_yh/ppermute | solution.py:287
  35.9 27.7 %copy-start.2 = (bf16[384,256]{1,0:T(8,128)(2,1)S(1)}, bf16[384,256]{1,0:T(8,128)(2,1)}, u32[]{:S(2)}) copy-start(bf16[384,256]{1,0:T(8,128)(2,1)} %x_ref.1) | copy-start | bytes 589828
  36.0 22.8 %all-to-all-start = ((bf16[8,320,256]{2,1,0:T(8,128)(2,1)}), bf16[8,320,256]{2,1,0:T(8,128)(2,1)S(1)}, u32[]{:S(2)}, u32[]{:S(2)}) async-start(bf16[8,320,256]{2,1,0:T(8,128)(2,1)} %weights_yh.1), calls=%async_computation | async-start | bytes 2621440 | tf_op jit(solution)/shard_map/qkv_rep/all_to_all | solution.py:303
  41.7 81.1 %all-gather.8.cloned.1.call-start = ((), (), s32[]{:S(2)}) async-start(), calls=%async_computation.5 | async-start | bytes 2228224 | tf_op jit(solution)/shard_map/out_rep/all_gather | solution.py:308
  41.7 20.8 %collective-permute-start.3 = (bf16[128,256]{1,0:T(8,128)(2,1)S(1)}, bf16[128,256]{1,0:T(8,128)(2,1)S(1)}, u32[]{:S(2)}, u32[]{:S(2)}) collective-permute-start(bf16[128,256]{1,0:T(8,128)(2,1)S(1)} %get-tuple-element.12), channel_id=1, source_target_pairs={{0,0},{1,32},{16,1},{17,33},{32,16},{33,48},{48,17},{49,49},{2,2},... | collective-permute-start | bytes 196616 | tf_op jit(solution)/shard_map/out_yh/ppermute | solution.py:296
  42.3 20.2 %collective-permute-start.4 = (bf16[128,256]{1,0:T(8,128)(2,1)S(1)}, bf16[128,256]{1,0:T(8,128)(2,1)S(1)}, u32[]{:S(2)}, u32[]{:S(2)}) collective-permute-start(bf16[128,256]{1,0:T(8,128)(2,1)S(1)} %get-tuple-element.13), channel_id=1, source_target_pairs={{0,16},{1,48},{16,17},{17,49},{32,0},{33,32},{48,1},{49,33},{2,18}... | collective-permute-start | bytes 196616 | tf_op jit(solution)/shard_map/out_yh/ppermute | solution.py:296
  58.7 7.5 %collective-permute-start.5 = (bf16[8,320,256]{2,1,0:T(8,128)(2,1)S(1)}, bf16[8,320,256]{2,1,0:T(8,128)(2,1)S(1)}, u32[]{:S(2)}, u32[]{:S(2)}) collective-permute-start(bf16[8,320,256]{2,1,0:T(8,128)(2,1)S(1)} %all-to-all-done.w_ref), channel_id=1, source_target_pairs={{0,1},{1,0},{2,3},{3,2},{4,5},{5,4},{6,7},{7,6},{8,9},{9,8},{10,11... | collective-permute-start | bytes 3932168 | tf_op jit(solution)/shard_map/qkv_rep/ppermute | solution.py:304
  63.6 1.4 copy-start.1
  67.2 55.6 %copy-start.3 = (s32[2]{0:T(128)S(1)}, s32[2]{0:T(128)}, u32[]{:S(2)}) copy-start(s32[2]{0:T(128)} %len_ref.1) | copy-start | bytes 28
  122.8 2.4 %copy-start = (bf16[4096,256]{1,0:T(8,128)(2,1)S(1)}, bf16[4096,256]{1,0:T(8,128)(2,1)}, u32[]{:S(2)}) copy-start(bf16[4096,256]{1,0:T(8,128)(2,1)} %all-gather.8.cloned.1.call-done) | copy-start | bytes 6291460
  127.0 4.6 %copy-start.5 = (f32[256,6]{0,1:T(8,128)S(1)}, f32[256,6]{0,1:T(8,128)}, u32[]{:S(2)}) copy-start(f32[256,6]{0,1:T(8,128)} %param.17) | copy-start | bytes 18436
  127.0 4.6 %copy-start.6 = (f32[256]{0:T(256)S(1)}, f32[256]{0:T(256)}, u32[]{:S(2)}) copy-start(f32[256]{0:T(256)} %param.16) | copy-start | bytes 3076
  127.0 17.7 %all-to-all-start.2 = ((bf16[4,384,256]{2,1,0:T(8,128)(2,1)}), bf16[4,384,256]{2,1,0:T(8,128)(2,1)S(1)}, u32[]{:S(2)}, u32[]{:S(2)}) async-start(bf16[4,384,256]{2,1,0:T(8,128)(2,1)} %shard_map.107), calls=%async_computation.2 | async-start | bytes 1572864 | tf_op jit(solution)/shard_map/out_sum/all_to_all | solution.py:318
  145.9 20.4 %all-to-all-start.3 = ((bf16[32,8,384]{2,1,0:T(8,128)(2,1)}), bf16[32,8,384]{2,1,0:T(8,128)(2,1)S(1)}, u32[]{:S(2)}, u32[]{:S(2)}) async-start(bf16[32,8,384]{2,1,0:T(8,128)(2,1)} %get-tuple-element.21), calls=%async_computation.3 | async-start | bytes 393216 | tf_op jit(solution)/shard_map/stat_tp/all_to_all | solution.py:324
Sparse Core Ops, SparseCore 0:
  10.7 52.2 all-gather.5
  65.6 37.8 all-gather.7

commit v6 on v5

--- a/solution.py
+++ b/solution.py
@@ -45,10 +45,12 @@
     return high, low
 
 
-def pack_kernel(odd_ref, q0, q1, out_ref):
+def pack_kernel(odd_ref, q0, q1, kv0, kv1, out_ref):
     even = odd_ref[0] == 0
-    first, second = jnp.where(even, q0[...], q1[...]), jnp.where(even, q1[...], q0[...])
-    whole = jnp.concatenate([first[:128], second[:128], first[128:], second[128:]], axis=0)
+    q, kv = (q0[...], q1[...]), (kv0[...], kv1[...])
+    whole = jnp.concatenate(
+        [jnp.where(even, a[k], a[1 - k]) for a in (q, kv) for k in range(2)], axis=0
+    )
     for k in range(NYL * NX):
         out_ref[k] = whole
 
@@ -57,7 +59,7 @@
     vmem = pl.BlockSpec(memory_space=pltpu.VMEM)
     return pl.pallas_call(
         pack_kernel,
-        in_specs=[pl.BlockSpec(memory_space=pltpu.SMEM)] + [vmem] * 2,
+        in_specs=[pl.BlockSpec(memory_space=pltpu.SMEM)] + [vmem] * 4,
         out_specs=vmem,
         out_shape=jax.ShapeDtypeStruct((NYL * NX, 320, 256), BF16),
         compiler_params=pltpu.CompilerParams(vmem_limit_bytes=VMEM),
@@ -110,7 +112,10 @@
     project_side(x_ref, w_ref, stat, out_ref, core_ref[0])
 
 
-def other_kernel(core_ref, x_ref, w_ref, first_ref, out_ref):
+def other_kernel(core_ref, x_ref, w_ref, first_ref, o0_ref, o1_ref, out_ref, o_ref):
+    even = core_ref[1] == 0
+    o_ref[0:128, :] = jnp.where(even, o0_ref[...], o1_ref[...])
+    o_ref[128:256, :] = jnp.where(even, o1_ref[...], o0_ref[...])
     core = core_ref[0]
     rows = x_ref.shape[1]
     for hi in range(2):
@@ -118,23 +123,25 @@
     project_side(x_ref, w_ref, first_ref[core, rows + 96 : rows + 112, :], out_ref, 1 - core)
 
 
-def project(core, x, own, other, tokens):
+def project(core, x, own, other, tokens, out_blocks):
     rows = x.shape[1]
     vmem = pl.BlockSpec(memory_space=pltpu.VMEM)
     smem = pl.BlockSpec(memory_space=pltpu.SMEM)
 
-    def call(kernel, flops, *args):
+    def call(kernel, flops, more, *args):
         return pl.pallas_call(
             kernel,
             in_specs=[smem] + [vmem] * (len(args) - 1),
-            out_specs=vmem,
-            out_shape=jax.ShapeDtypeStruct((4, rows + 112, 128), BF16),
+            out_specs=[vmem] * (1 + len(more)),
+            out_shape=[jax.ShapeDtypeStruct((4, rows + 112, 128), BF16)] + more,
             compiler_params=pltpu.CompilerParams(vmem_limit_bytes=VMEM),
             cost_estimate=pl.CostEstimate(flops=flops, bytes_accessed=3_000_000, transcendentals=0),
         )(*args)
 
-    first = call(own_kernel, OWN_COST, core, x, own, tokens)
-    return call(other_kernel, 2 * rows * 2048 * 320, core, x, other, first)
+    (first,) = call(own_kernel, OWN_COST, [], core, x, own, tokens)
+    joined = jax.ShapeDtypeStruct((256, 256), BF16)
+    cost = 2 * rows * 2048 * 320
+    return call(other_kernel, cost, [joined], core, x, other, first, *out_blocks)
 
 
 def sum_kernel(p_ref, out_ref):
@@ -272,7 +279,7 @@
 ):
     rows = tokens.shape[0]
     z, yh, c = lax.axis_index("z"), lax.axis_index("yh"), lax.axis_index("c")
-    core = c.astype(jnp.int32)[None]
+    core = jnp.stack([c, yh % 2]).astype(jnp.int32)
 
     xf = tokens.astype(F32)
     gained = (xf * attn_gain[None, :]).astype(BF16)
@@ -282,13 +289,17 @@
         kv = lax.ppermute(jnp.concatenate([key_weight.T, value_matrix.T], axis=0), TP, kv_perm())
         q = [query_weight[256 * b : 256 * (b + 1)] for b in range(2)]
         q = [jnp.concatenate([one[:128], one[128:]], axis=1) for one in q]
-        q = [jnp.concatenate([q[b], kv[:, 256 * b : 256 * (b + 1)]], axis=0) for b in range(2)]
         q = [
             lax.ppermute(jnp.where(first, q[k], q[1 - k]), ("yh", "c"), head_perm(k))
             for k in range(2)
         ]
+        kv = [kv[:, :256], kv[:, 256:]]
+        kv = [
+            lax.ppermute(jnp.where(first, kv[k], kv[1 - k]), ("yh", "c"), head_perm(k))
+            for k in range(2)
+        ]
         odd = (yh % 2).astype(jnp.int32)[None]
-        qkv_send = packed_copies(odd, *q)
+        qkv_send = packed_copies(odd, *q, *kv)
     with jax.named_scope("out_yh"):
         o = [output_weight[:128], output_weight[128:]]
         o = [jnp.where(first, o[k], o[1 - k]) for k in range(2)]
@@ -302,11 +313,9 @@
     with jax.named_scope("qkv_rep"):
         qkv_own = lax.all_to_all(qkv_send, ("yl", "x"), 0, 0)
         qkv_other = lax.ppermute(qkv_own, "c", swap)
+    parts, out_part = project(core, x_all, qkv_own, qkv_other, tokens, o)
     with jax.named_scope("out_rep"):
-        o, x_all = lax.optimization_barrier((o, x_all))
-        out_part = jnp.concatenate([jnp.where(even, o[k], o[1 - k]) for k in range(2)], axis=0)
         out_all = lax.all_gather(out_part, REP, axis=0)
-    parts = project(core, x_all, qkv_own, qkv_other, tokens)
     with jax.named_scope("qkv_sum"):
         parts = lax.all_to_all(parts, "yh", 0, 0)
     with jax.named_scope("qkv_z"):

time: 174 us -> 173 us (level)
  waiting for transfers between devices: 46 us -> 39.8 us
  starting transfers between devices: 43.1 us -> 49.2 us
  blocking collectives: 55.5 us -> 52.8 us
    ppermute x2, waiting for transfers between devices: 11.7 us -> 0.01 us  [local(): lax.ppermute(jnp.where(first, q[k], q[1 - k]), ('yh', 'c'), head_perm(k))]
    ppermute x0 -> x2, starting transfers between devices: none -> 11.3 us  [local(): lax.ppermute(jnp.where(first, kv[k], kv[1 - k]), ('yh', 'c'), head_perm(k))]
    all_to_all x1, blocking collectives: 21.5 us -> 18.7 us  [local(): parts = lax.all_to_all(parts, 'yh', 0, 0)]
    ppermute x0 -> x2, waiting for transfers between devices: none -> 2.51 us  [local(): lax.ppermute(jnp.where(first, kv[k], kv[1 - k]), ('yh', 'c'), head_perm(k))]
    all_to_all x1, waiting for transfers between devices: 8.33 us -> 10.7 us  [local(): qkv_own = lax.all_to_all(qkv_send, ('yl', 'x'), 0, 0)]
    ppermute x2, starting transfers between devices: 11.7 us -> 9.81 us  [local(): lax.ppermute(jnp.where(first, q[k], q[1 - k]), ('yh', 'c'), head_perm(k))]
  transfers between devices with their start and end apart: 11 -> 13, of which waited for: 5 -> 4; matrix products, arithmetic and copies ran while one was open for 2% -> 2% of each run, Pallas kernels for 2% -> 2%
where the time goes in v6:
time: 173 us; the launch traced here: 172 us
  blocking collectives  52.8 us (31%)
  starting transfers between devices  49.2 us (28%)
  waiting for transfers between devices  39.8 us (23%)
  between operations  14.3 us (8%)
  Pallas kernels  10.4 us (6%)
  other arithmetic  3.29 us (2%)
  local copies, waits for them, and re-layouts  2.34 us (1%)
    all_gather x1, blocking collectives, local(): messages = lax.all_gather(summed(parts), 'z', axis=0)  34.1 us
    all_to_all x1, blocking collectives, local(): parts = lax.all_to_all(parts, 'yh', 0, 0)  18.7 us
    all_to_all x1, waiting for transfers between devices, local(): parts = lax.all_to_all(parts, 'yh', 0, 0)  14.2 us
    all_to_all x1, waiting for transfers between devices, local(): stat = lax.all_to_all(stat, TP, 0, 0).astype(F32).sum(axis=0)  12.4 us
    ppermute x2, starting transfers between devices, local(): lax.ppermute(jnp.where(first, kv[k], kv[1 - k]), ('yh', 'c'), head_perm(k))  11.3 us
    all_to_all x1, waiting for transfers between devices, local(): qkv_own = lax.all_to_all(qkv_send, ('yl', 'x'), 0, 0)  10.7 us
    ppermute x2, starting transfers between devices, local(): lax.ppermute(jnp.where(first, q[k], q[1 - k]), ('yh', 'c'), head_perm(k))  9.81 us
    ppermute x2, starting transfers between devices, local(): o = [lax.ppermute(o[k], ('yh', 'c'), head_perm(k)) for k in range(2)]  7.7 us
  transfers between devices with their start and end apart: 13, of which 4 were waited for; matrix products, arithmetic and copies ran while one was open for 2% of the time, Pallas kernels for 2%

profile of v6, /device:TPU:6, one launch (start us, length us, event | category | flops | bytes accessed | tf_op | source)
XLA Modules:
  0.0 172.1 jit_solution(8513586436340838330)
XLA Ops:
  7.2 0.0 copy-start.4
  7.2 0.0 all-gather.6.cloned.1.call-start
  7.2 0.8 pad_maximum_fusion.2
  8.0 0.7 collective-permute-start.2
  8.6 1.6 multiply_convert_fusion
  10.3 0.0 all-gather.6.cloned.1.call-update
  10.3 0.8 fusion.5
  11.2 0.7 collective-permute-start
  11.9 9.1 %collective-permute-start.1 = (bf16[128,256]{1,0:T(8,128)(2,1)S(1)}, bf16[128,256]{1,0:T(8,128)(2,1)S(1)}, u32[]{:S(2)}, u32[]{:S(2)}) collective-permute-start(bf16[128,256]{1,0:T(8,128)(2,1)S(1)} %get-tuple-element.20), channel_id=1, source_target_pairs={{0,16},{1,48},{16,17},{17,49},{32,0},{33,32},{48,1},{49,33},{2,18}... | collective-permute-start | bytes 196616 | tf_op jit(solution)/shard_map/weights_yh/ppermute | solution.py:293
  21.0 0.0 collective-permute-done.2
  21.0 0.7 collective-permute-start.3
  21.7 10.6 %collective-permute-start.4 = (bf16[32,256]{1,0:T(8,128)(2,1)S(1)}, bf16[32,256]{1,0:T(8,128)(2,1)S(1)}, u32[]{:S(2)}, u32[]{:S(2)}) collective-permute-start(bf16[32,256]{1,0:T(8,128)(2,1)S(1)} %get-tuple-element.28), channel_id=1, source_target_pairs={{0,16},{1,48},{16,17},{17,49},{32,0},{33,32},{48,1},{49,33},{2,18}... | collective-permute-start | bytes 49160 | tf_op jit(solution)/shard_map/weights_yh/ppermute | solution.py:298
  32.4 0.0 collective-permute-done.3.kv0
  32.4 2.5 %collective-permute-done.4.kv1 = bf16[32,256]{1,0:T(8,128)(2,1)S(1)} collective-permute-done((bf16[32,256]{1,0:T(8,128)(2,1)S(1)}, bf16[32,256]{1,0:T(8,128)(2,1)S(1)}, u32[]{:S(2)}, u32[]{:S(2)}) %collective-permute-start.4) | collective-permute-done | bytes 16416 | tf_op jit(solution)/shard_map/weights_yh/ppermute | solution.py:298
  34.9 0.0 collective-permute-done.q0
  34.9 0.0 collective-permute-done.1.q1
  34.9 1.2 weights_yh.1
  36.1 5.8 %all-to-all-start = ((bf16[8,320,256]{2,1,0:T(8,128)(2,1)}), bf16[8,320,256]{2,1,0:T(8,128)(2,1)S(1)}, u32[]{:S(2)}, u32[]{:S(2)}) async-start(bf16[8,320,256]{2,1,0:T(8,128)(2,1)} %weights_yh.1), calls=%async_computation | async-start | bytes 2621440 | tf_op jit(solution)/shard_map/qkv_rep/all_to_all | solution.py:314
  41.9 0.1 pad_add_fusion.core_ref
  42.0 0.7 collective-permute-start.6
  42.6 7.0 %collective-permute-start.7 = (bf16[128,256]{1,0:T(8,128)(2,1)S(1)}, bf16[128,256]{1,0:T(8,128)(2,1)S(1)}, u32[]{:S(2)}, u32[]{:S(2)}) collective-permute-start(bf16[128,256]{1,0:T(8,128)(2,1)S(1)} %get-tuple-element.13), channel_id=1, source_target_pairs={{0,16},{1,48},{16,17},{17,49},{32,0},{33,32},{48,1},{49,33},{2,18}... | collective-permute-start | bytes 196616 | tf_op jit(solution)/shard_map/out_yh/ppermute | solution.py:307
  49.7 10.7 %all-to-all-done.w_ref = bf16[8,320,256]{2,1,0:T(8,128)(2,1)S(1)} async-done(((bf16[8,320,256]{2,1,0:T(8,128)(2,1)}), bf16[8,320,256]{2,1,0:T(8,128)(2,1)S(1)}, u32[]{:S(2)}, u32[]{:S(2)}) %all-to-all-start) | async-done | bytes 1310752 | tf_op jit(solution)/shard_map/qkv_rep/all_to_all | solution.py:314
  60.4 2.7 %collective-permute-start.5 = (bf16[8,320,256]{2,1,0:T(8,128)(2,1)S(1)}, bf16[8,320,256]{2,1,0:T(8,128)(2,1)S(1)}, u32[]{:S(2)}, u32[]{:S(2)}) collective-permute-start(bf16[8,320,256]{2,1,0:T(8,128)(2,1)S(1)} %all-to-all-done.w_ref), channel_id=1, source_target_pairs={{0,1},{1,0},{2,3},{3,2},{4,5},{5,4},{6,7},{7,6},{8,9},{9,8},{10,11... | collective-permute-start | bytes 3932168 | tf_op jit(solution)/shard_map/qkv_rep/ppermute | solution.py:315
  63.1 0.0 all-gather.6.cloned.1.call-done
  63.2 0.0 copy-done.2
  63.2 0.0 copy-start.1
  63.2 1.4 copy-done.1
  64.6 1.6 shard_map.104.first_ref
  66.2 0.0 collective-permute-done.6.o0_ref
  66.2 0.0 collective-permute-done.7.o1_ref
  66.2 0.0 collective-permute-done.5.w_ref
  66.3 2.1 %shard_map.105 = (bf16[4,496,128]{2,1,0:T(8,128)(2,1)S(1)}, bf16[256,256]{1,0:T(8,128)(2,1)}) custom-call(s32[2]{0:T(128)S(1)} %pad_add_fusion.core_ref, bf16[8,384,256]{2,1,0:T(8,128)(2,1)S(1)} %bitcast.13, bf16[8,320,256]{2,1,0:T(8,128)(2,1)S(1)} %collective-permute-done.5.w_ref, bf16[4,496,128]{2,1,0:T(8,128)(2,1)S(1)} %shard_map.104.first_ref, ...), custom_call_target="tpu_custom_call" | custom-call | flops 503316480 | bytes 3000000 | tf_op jit(solution)/shard_map/pallas_call | solution.py:132
  68.4 0.0 all-gather.8.cloned.1.call-update
  68.4 0.0 copy-start.3
  68.4 18.7 %all_to_all.20.p_ref = bf16[4,496,128]{2,1,0:T(8,128)(2,1)S(1)} all-to-all(bf16[4,496,128]{2,1,0:T(8,128)(2,1)S(1)} %get-tuple-element.15), channel_id=1, replica_groups=mesh['z'=8,'yh'=4,'yl'=2,'x'=4,'c'=2] {'yh'}, dimensions={0} | all-to-all | bytes 1015808 | tf_op jit(solution)/shard_map/qkv_sum/all_to_all | solution.py:320
  87.1 0.1 qkv_z.1
  87.2 34.1 %all-gather.2 = bf16[3968,128]{1,0:T(8,128)(2,1)S(1)} all-gather(bf16[496,128]{1,0:T(8,128)(2,1)S(1)} %qkv_z.1), channel_id=4, replica_groups=mesh['z'=8,'yh'=4,'yl'=2,'x'=4,'c'=2] {'z'}, dimensions={0}, use_global_device_ids=true | all-gather | bytes 1142784 | tf_op jit(solution)/shard_map/qkv_z/all_gather | solution.py:322
  121.3 2.3 %shard_map.106.att_ref = bf16[384,1024]{1,0:T(8,128)(2,1)S(1)} custom-call(s32[2]{0:T(128)S(1)} %copy-done.3, bf16[8,496,128]{2,1,0:T(8,128)(2,1)S(1)} %bitcast.14), custom_call_target="tpu_custom_call" | custom-call | flops 8000000000 | bytes 2000000 | tf_op jit(solution)/shard_map/pallas_call | solution.py:214
  123.6 0.0 copy-done
  123.6 1.9 %shard_map.107 = bf16[4,384,256]{2,1,0:T(8,128)(2,1)} custom-call(bf16[384,1024]{1,0:T(8,128)(2,1)S(1)} %shard_map.106.att_ref, bf16[16,256,256]{2,1,0:T(8,128)(2,1)S(1)} %bitcast.11), custom_call_target="tpu_custom_call" | custom-call | flops 805306368 | bytes 5000000 | tf_op jit(solution)/shard_map/pallas_call | solution.py:227
  125.5 3.6 %all-to-all-start.2 = ((bf16[4,384,256]{2,1,0:T(8,128)(2,1)}), bf16[4,384,256]{2,1,0:T(8,128)(2,1)S(1)}, u32[]{:S(2)}, u32[]{:S(2)}) async-start(bf16[4,384,256]{2,1,0:T(8,128)(2,1)} %shard_map.107), calls=%async_computation.2 | async-start | bytes 1572864 | tf_op jit(solution)/shard_map/out_sum/all_to_all | solution.py:327
  129.2 14.2 %all-to-all-done.2.p_ref = bf16[4,384,256]{2,1,0:T(8,128)(2,1)S(1)} async-done(((bf16[4,384,256]{2,1,0:T(8,128)(2,1)}), bf16[4,384,256]{2,1,0:T(8,128)(2,1)S(1)}, u32[]{:S(2)}, u32[]{:S(2)}) %all-to-all-start.2) | async-done | bytes 786464 | tf_op jit(solution)/shard_map/out_sum/all_to_all | solution.py:327
  143.4 1.1 shard_map.108
  144.5 7.5 %all-to-all-start.3 = ((bf16[32,8,384]{2,1,0:T(8,128)(2,1)}), bf16[32,8,384]{2,1,0:T(8,128)(2,1)S(1)}, u32[]{:S(2)}, u32[]{:S(2)}) async-start(bf16[32,8,384]{2,1,0:T(8,128)(2,1)} %get-tuple-element.19), calls=%async_computation.3 | async-start | bytes 393216 | tf_op jit(solution)/shard_map/stat_tp/all_to_all | solution.py:333
  152.0 0.1 iota_compare_fusion
  152.1 0.1 lt.32
  152.2 12.4 %all-to-all-done.3 = bf16[32,8,384]{2,1,0:T(8,128)(2,1)S(1)} async-done(((bf16[32,8,384]{2,1,0:T(8,128)(2,1)}), bf16[32,8,384]{2,1,0:T(8,128)(2,1)S(1)}, u32[]{:S(2)}, u32[]{:S(2)}) %all-to-all-start.3) | async-done | bytes 196640 | tf_op jit(solution)/shard_map/stat_tp/all_to_all | solution.py:333
  164.6 0.6 fusion.1
  (17 shorter events, 0.1 us)
Async XLA Ops:
  7.2 25.2 %copy-start.4 = (bf16[256,256]{1,0:T(8,128)(2,1)S(1)}, bf16[256,256]{1,0:T(8,128)(2,1)}, u32[]{:S(2)}) copy-start(bf16[256,256]{1,0:T(8,128)(2,1)} %param.15) | copy-start | bytes 393220
  7.2 56.0 %all-gather.6.cloned.1.call-start = ((), (), s32[]{:S(2)}) async-start(), calls=%async_computation.4 | async-start | bytes 1769472 | tf_op jit(solution)/shard_map/tokens_z/all_gather | solution.py:312
  8.0 13.0 %collective-permute-start.2 = (bf16[32,512]{1,0:T(8,128)(2,1)S(1)}, bf16[32,512]{1,0:T(8,128)(2,1)S(1)}, u32[]{:S(2)}, u32[]{:S(2)}) collective-permute-start(bf16[32,512]{1,0:T(8,128)(2,1)S(1)} %pad_maximum_fusion.2), channel_id=1, source_target_pairs={{0,0},{16,64},{32,128},{48,192},{64,256},{80,320},{96,384},{112,44... | collective-permute-start | bytes 98312 | tf_op jit(solution)/shard_map/weights_yh/ppermute | solution.py:289
  11.2 23.7 %collective-permute-start = (bf16[128,256]{1,0:T(8,128)(2,1)S(1)}, bf16[128,256]{1,0:T(8,128)(2,1)S(1)}, u32[]{:S(2)}, u32[]{:S(2)}) collective-permute-start(bf16[128,256]{1,0:T(8,128)(2,1)S(1)} %get-tuple-element.21), channel_id=1, source_target_pairs={{0,0},{1,32},{16,1},{17,33},{32,16},{33,48},{48,17},{49,49},{2,2},... | collective-permute-start | bytes 196616 | tf_op jit(solution)/shard_map/weights_yh/ppermute | solution.py:293
  11.9 23.0 %collective-permute-start.1 = (bf16[128,256]{1,0:T(8,128)(2,1)S(1)}, bf16[128,256]{1,0:T(8,128)(2,1)S(1)}, u32[]{:S(2)}, u32[]{:S(2)}) collective-permute-start(bf16[128,256]{1,0:T(8,128)(2,1)S(1)} %get-tuple-element.20), channel_id=1, source_target_pairs={{0,16},{1,48},{16,17},{17,49},{32,0},{33,32},{48,1},{49,33},{2,18}... | collective-permute-start | bytes 196616 | tf_op jit(solution)/shard_map/weights_yh/ppermute | solution.py:293
  21.0 11.4 %collective-permute-start.3 = (bf16[32,256]{1,0:T(8,128)(2,1)S(1)}, bf16[32,256]{1,0:T(8,128)(2,1)S(1)}, u32[]{:S(2)}, u32[]{:S(2)}) collective-permute-start(bf16[32,256]{1,0:T(8,128)(2,1)S(1)} %get-tuple-element.29), channel_id=1, source_target_pairs={{0,0},{1,32},{16,1},{17,33},{32,16},{33,48},{48,17},{49,49},{2,2},... | collective-permute-start | bytes 49160 | tf_op jit(solution)/shard_map/weights_yh/ppermute | solution.py:298
  21.7 13.2 %collective-permute-start.4 = (bf16[32,256]{1,0:T(8,128)(2,1)S(1)}, bf16[32,256]{1,0:T(8,128)(2,1)S(1)}, u32[]{:S(2)}, u32[]{:S(2)}) collective-permute-start(bf16[32,256]{1,0:T(8,128)(2,1)S(1)} %get-tuple-element.28), channel_id=1, source_target_pairs={{0,16},{1,48},{16,17},{17,49},{32,0},{33,32},{48,1},{49,33},{2,18}... | collective-permute-start | bytes 49160 | tf_op jit(solution)/shard_map/weights_yh/ppermute | solution.py:298
  36.1 27.1 %copy-start.2 = (bf16[384,256]{1,0:T(8,128)(2,1)S(1)}, bf16[384,256]{1,0:T(8,128)(2,1)}, u32[]{:S(2)}) copy-start(bf16[384,256]{1,0:T(8,128)(2,1)} %x_ref.1) | copy-start | bytes 589828
  36.1 24.3 %all-to-all-start = ((bf16[8,320,256]{2,1,0:T(8,128)(2,1)}), bf16[8,320,256]{2,1,0:T(8,128)(2,1)S(1)}, u32[]{:S(2)}, u32[]{:S(2)}) async-start(bf16[8,320,256]{2,1,0:T(8,128)(2,1)} %weights_yh.1), calls=%async_computation | async-start | bytes 2621440 | tf_op jit(solution)/shard_map/qkv_rep/all_to_all | solution.py:314
  41.9 79.4 %all-gather.8.cloned.1.call-start = ((), (), s32[]{:S(2)}) async-start(), calls=%async_computation.5 | async-start | bytes 2228224 | tf_op jit(solution)/shard_map/out_rep/all_gather | solution.py:318
  42.0 24.2 %collective-permute-start.6 = (bf16[128,256]{1,0:T(8,128)(2,1)S(1)}, bf16[128,256]{1,0:T(8,128)(2,1)S(1)}, u32[]{:S(2)}, u32[]{:S(2)}) collective-permute-start(bf16[128,256]{1,0:T(8,128)(2,1)S(1)} %get-tuple-element.12), channel_id=1, source_target_pairs={{0,0},{1,32},{16,1},{17,33},{32,16},{33,48},{48,17},{49,49},{2,2},... | collective-permute-start | bytes 196616 | tf_op jit(solution)/shard_map/out_yh/ppermute | solution.py:307
  42.6 23.6 %collective-permute-start.7 = (bf16[128,256]{1,0:T(8,128)(2,1)S(1)}, bf16[128,256]{1,0:T(8,128)(2,1)S(1)}, u32[]{:S(2)}, u32[]{:S(2)}) collective-permute-start(bf16[128,256]{1,0:T(8,128)(2,1)S(1)} %get-tuple-element.13), channel_id=1, source_target_pairs={{0,16},{1,48},{16,17},{17,49},{32,0},{33,32},{48,1},{49,33},{2,18}... | collective-permute-start | bytes 196616 | tf_op jit(solution)/shard_map/out_yh/ppermute | solution.py:307
  60.4 5.9 %collective-permute-start.5 = (bf16[8,320,256]{2,1,0:T(8,128)(2,1)S(1)}, bf16[8,320,256]{2,1,0:T(8,128)(2,1)S(1)}, u32[]{:S(2)}, u32[]{:S(2)}) collective-permute-start(bf16[8,320,256]{2,1,0:T(8,128)(2,1)S(1)} %all-to-all-done.w_ref), channel_id=1, source_target_pairs={{0,1},{1,0},{2,3},{3,2},{4,5},{5,4},{6,7},{7,6},{8,9},{9,8},{10,11... | collective-permute-start | bytes 3932168 | tf_op jit(solution)/shard_map/qkv_rep/ppermute | solution.py:315
  63.2 1.4 copy-start.1
  68.4 52.9 %copy-start.3 = (s32[2]{0:T(128)S(1)}, s32[2]{0:T(128)}, u32[]{:S(2)}) copy-start(s32[2]{0:T(128)} %len_ref.1) | copy-start | bytes 28
  121.3 2.3 %copy-start = (bf16[4096,256]{1,0:T(8,128)(2,1)S(1)}, bf16[4096,256]{1,0:T(8,128)(2,1)}, u32[]{:S(2)}) copy-start(bf16[4096,256]{1,0:T(8,128)(2,1)} %all-gather.8.cloned.1.call-done) | copy-start | bytes 6291460
  125.5 3.6 %copy-start.5 = (f32[256,6]{0,1:T(8,128)S(1)}, f32[256,6]{0,1:T(8,128)}, u32[]{:S(2)}) copy-start(f32[256,6]{0,1:T(8,128)} %param.17) | copy-start | bytes 18436
  125.5 3.6 %copy-start.6 = (f32[256]{0:T(256)S(1)}, f32[256]{0:T(256)}, u32[]{:S(2)}) copy-start(f32[256]{0:T(256)} %param.16) | copy-start | bytes 3076
  125.5 17.9 %all-to-all-start.2 = ((bf16[4,384,256]{2,1,0:T(8,128)(2,1)}), bf16[4,384,256]{2,1,0:T(8,128)(2,1)S(1)}, u32[]{:S(2)}, u32[]{:S(2)}) async-start(bf16[4,384,256]{2,1,0:T(8,128)(2,1)} %shard_map.107), calls=%async_computation.2 | async-start | bytes 1572864 | tf_op jit(solution)/shard_map/out_sum/all_to_all | solution.py:327
  144.5 20.0 %all-to-all-start.3 = ((bf16[32,8,384]{2,1,0:T(8,128)(2,1)}), bf16[32,8,384]{2,1,0:T(8,128)(2,1)S(1)}, u32[]{:S(2)}, u32[]{:S(2)}) async-start(bf16[32,8,384]{2,1,0:T(8,128)(2,1)} %get-tuple-element.19), calls=%async_computation.3 | async-start | bytes 393216 | tf_op jit(solution)/shard_map/stat_tp/all_to_all | solution.py:333
Sparse Core Ops, SparseCore 0:
  10.7 52.2 all-gather.5
  68.5 37.8 all-gather.7

commit v7 on v5

--- a/solution.py
+++ b/solution.py
@@ -45,10 +45,12 @@
     return high, low
 
 
-def pack_kernel(odd_ref, q0, q1, out_ref):
+def pack_kernel(odd_ref, q0, q1, kv0, kv1, out_ref):
     even = odd_ref[0] == 0
-    first, second = jnp.where(even, q0[...], q1[...]), jnp.where(even, q1[...], q0[...])
-    whole = jnp.concatenate([first[:128], second[:128], first[128:], second[128:]], axis=0)
+    q, kv = (q0[...], q1[...]), (kv0[...], kv1[...])
+    whole = jnp.concatenate(
+        [jnp.where(even, a[k], a[1 - k]) for a in (q, kv) for k in range(2)], axis=0
+    )
     for k in range(NYL * NX):
         out_ref[k] = whole
 
@@ -57,7 +59,7 @@
     vmem = pl.BlockSpec(memory_space=pltpu.VMEM)
     return pl.pallas_call(
         pack_kernel,
-        in_specs=[pl.BlockSpec(memory_space=pltpu.SMEM)] + [vmem] * 2,
+        in_specs=[pl.BlockSpec(memory_space=pltpu.SMEM)] + [vmem] * 4,
         out_specs=vmem,
         out_shape=jax.ShapeDtypeStruct((NYL * NX, 320, 256), BF16),
         compiler_params=pltpu.CompilerParams(vmem_limit_bytes=VMEM),
@@ -282,13 +284,17 @@
         kv = lax.ppermute(jnp.concatenate([key_weight.T, value_matrix.T], axis=0), TP, kv_perm())
         q = [query_weight[256 * b : 256 * (b + 1)] for b in range(2)]
         q = [jnp.concatenate([one[:128], one[128:]], axis=1) for one in q]
-        q = [jnp.concatenate([q[b], kv[:, 256 * b : 256 * (b + 1)]], axis=0) for b in range(2)]
         q = [
             lax.ppermute(jnp.where(first, q[k], q[1 - k]), ("yh", "c"), head_perm(k))
             for k in range(2)
         ]
+        kv = [kv[:, :256], kv[:, 256:]]
+        kv = [
+            lax.ppermute(jnp.where(first, kv[k], kv[1 - k]), ("yh", "c"), head_perm(k))
+            for k in range(2)
+        ]
         odd = (yh % 2).astype(jnp.int32)[None]
-        qkv_send = packed_copies(odd, *q)
+        qkv_send = packed_copies(odd, *q, *kv)
     with jax.named_scope("out_yh"):
         o = [output_weight[:128], output_weight[128:]]
         o = [jnp.where(first, o[k], o[1 - k]) for k in range(2)]

time: 174 us -> 173 us (level)
  waiting for transfers between devices: 46 us -> 39.1 us
  starting transfers between devices: 43.1 us -> 49.7 us
    ppermute x2, waiting for transfers between devices: 11.7 us -> 0.01 us  [local(): lax.ppermute(jnp.where(first, q[k], q[1 - k]), ('yh', 'c'), head_perm(k))]
    ppermute x0 -> x2, starting transfers between devices: none -> 11.3 us  [local(): lax.ppermute(jnp.where(first, kv[k], kv[1 - k]), ('yh', 'c'), head_perm(k))]
    ppermute x0 -> x2, waiting for transfers between devices: none -> 2.51 us  [local(): lax.ppermute(jnp.where(first, kv[k], kv[1 - k]), ('yh', 'c'), head_perm(k))]
    all_to_all x1, waiting for transfers between devices: 8.33 us -> 10.7 us  [local(): qkv_own = lax.all_to_all(qkv_send, ('yl', 'x'), 0, 0)]
    ppermute x2, starting transfers between devices: 11.7 us -> 9.81 us  [local(): lax.ppermute(jnp.where(first, q[k], q[1 - k]), ('yh', 'c'), head_perm(k))]
  transfers between devices with their start and end apart: 11 -> 13, of which waited for: 5 -> 4; matrix products, arithmetic and copies ran while one was open for 2% -> 2% of each run, Pallas kernels for 2% -> 2%
where the time goes in v7:
time: 173 us; the launch traced here: 172 us
  blocking collectives  54 us (31%)
  starting transfers between devices  49.7 us (29%)
  waiting for transfers between devices  39.1 us (23%)
  between operations  14.3 us (8%)
  Pallas kernels  8.73 us (5%)
  other arithmetic  3.9 us (2%)
  local copies, waits for them, and re-layouts  2.34 us (1%)
    all_gather x1, blocking collectives, local(): messages = lax.all_gather(summed(parts), 'z', axis=0)  34.1 us
    all_to_all x1, blocking collectives, local(): parts = lax.all_to_all(parts, 'yh', 0, 0)  19.9 us
    all_to_all x1, waiting for transfers between devices, local(): parts = lax.all_to_all(parts, 'yh', 0, 0)  13.4 us
    all_to_all x1, waiting for transfers between devices, local(): stat = lax.all_to_all(stat, TP, 0, 0).astype(F32).sum(axis=0)  12.4 us
    ppermute x2, starting transfers between devices, local(): lax.ppermute(jnp.where(first, kv[k], kv[1 - k]), ('yh', 'c'), head_perm(k))  11.3 us
    all_to_all x1, waiting for transfers between devices, local(): qkv_own = lax.all_to_all(qkv_send, ('yl', 'x'), 0, 0)  10.7 us
    ppermute x2, starting transfers between devices, local(): lax.ppermute(jnp.where(first, q[k], q[1 - k]), ('yh', 'c'), head_perm(k))  9.81 us
    all_to_all x1, starting transfers between devices, local(): stat = lax.all_to_all(stat, TP, 0, 0).astype(F32).sum(axis=0)  8.07 us
  transfers between devices with their start and end apart: 13, of which 4 were waited for; matrix products, arithmetic and copies ran while one was open for 2% of the time, Pallas kernels for 2%

profile of v7, /device:TPU:6, one launch (start us, length us, event | category | flops | bytes accessed | tf_op | source)
XLA Modules:
  0.0 172.2 jit_solution(6367788971429521977)
XLA Ops:
  7.2 0.0 copy-start.4
  7.2 0.0 all-gather.6.cloned.1.call-start
  7.2 0.8 pad_maximum_fusion.3
  8.0 0.7 collective-permute-start.2
  8.6 1.6 multiply_convert_fusion
  10.3 0.0 all-gather.6.cloned.1.call-update
  10.3 0.8 fusion.5
  11.2 0.7 collective-permute-start
  11.9 9.1 %collective-permute-start.1 = (bf16[128,256]{1,0:T(8,128)(2,1)S(1)}, bf16[128,256]{1,0:T(8,128)(2,1)S(1)}, u32[]{:S(2)}, u32[]{:S(2)}) collective-permute-start(bf16[128,256]{1,0:T(8,128)(2,1)S(1)} %get-tuple-element.24), channel_id=1, source_target_pairs={{0,16},{1,48},{16,17},{17,49},{32,0},{33,32},{48,1},{49,33},{2,18}... | collective-permute-start | bytes 196616 | tf_op jit(solution)/shard_map/weights_yh/ppermute | solution.py:288
  21.0 0.0 collective-permute-done.2
  21.0 0.7 collective-permute-start.3
  21.7 10.6 %collective-permute-start.4 = (bf16[32,256]{1,0:T(8,128)(2,1)S(1)}, bf16[32,256]{1,0:T(8,128)(2,1)S(1)}, u32[]{:S(2)}, u32[]{:S(2)}) collective-permute-start(bf16[32,256]{1,0:T(8,128)(2,1)S(1)} %get-tuple-element.32), channel_id=1, source_target_pairs={{0,16},{1,48},{16,17},{17,49},{32,0},{33,32},{48,1},{49,33},{2,18}... | collective-permute-start | bytes 49160 | tf_op jit(solution)/shard_map/weights_yh/ppermute | solution.py:293
  32.3 0.0 copy-done.4
  32.4 0.0 collective-permute-done.3.kv0
  32.4 2.5 %collective-permute-done.4.kv1 = bf16[32,256]{1,0:T(8,128)(2,1)S(1)} collective-permute-done((bf16[32,256]{1,0:T(8,128)(2,1)S(1)}, bf16[32,256]{1,0:T(8,128)(2,1)S(1)}, u32[]{:S(2)}, u32[]{:S(2)}) %collective-permute-start.4) | collective-permute-done | bytes 16416 | tf_op jit(solution)/shard_map/weights_yh/ppermute | solution.py:293
  34.9 0.0 collective-permute-done.q0
  34.9 0.0 collective-permute-done.1.q1
  34.9 1.2 weights_yh.1
  36.1 5.8 %all-to-all-start = ((bf16[8,320,256]{2,1,0:T(8,128)(2,1)}), bf16[8,320,256]{2,1,0:T(8,128)(2,1)S(1)}, u32[]{:S(2)}, u32[]{:S(2)}) async-start(bf16[8,320,256]{2,1,0:T(8,128)(2,1)} %weights_yh.1), calls=%async_computation | async-start | bytes 2621440 | tf_op jit(solution)/shard_map/qkv_rep/all_to_all | solution.py:309
  41.9 0.0 all-gather.8.cloned.1.call-start
  41.9 0.7 collective-permute-start.5
  42.6 7.0 %collective-permute-start.6 = (bf16[128,256]{1,0:T(8,128)(2,1)S(1)}, bf16[128,256]{1,0:T(8,128)(2,1)S(1)}, u32[]{:S(2)}, u32[]{:S(2)}) collective-permute-start(bf16[128,256]{1,0:T(8,128)(2,1)S(1)} %get-tuple-element.13), channel_id=1, source_target_pairs={{0,16},{1,48},{16,17},{17,49},{32,0},{33,32},{48,1},{49,33},{2,18}... | collective-permute-start | bytes 196616 | tf_op jit(solution)/shard_map/out_yh/ppermute | solution.py:302
  49.6 10.7 %all-to-all-done.w_ref = bf16[8,320,256]{2,1,0:T(8,128)(2,1)S(1)} async-done(((bf16[8,320,256]{2,1,0:T(8,128)(2,1)}), bf16[8,320,256]{2,1,0:T(8,128)(2,1)S(1)}, u32[]{:S(2)}, u32[]{:S(2)}) %all-to-all-start) | async-done | bytes 1310752 | tf_op jit(solution)/shard_map/qkv_rep/all_to_all | solution.py:309
  60.4 2.7 %collective-permute-start.7 = (bf16[8,320,256]{2,1,0:T(8,128)(2,1)S(1)}, bf16[8,320,256]{2,1,0:T(8,128)(2,1)S(1)}, u32[]{:S(2)}, u32[]{:S(2)}) collective-permute-start(bf16[8,320,256]{2,1,0:T(8,128)(2,1)S(1)} %all-to-all-done.w_ref), channel_id=1, source_target_pairs={{0,1},{1,0},{2,3},{3,2},{4,5},{5,4},{6,7},{7,6},{8,9},{9,8},{10,11... | collective-permute-start | bytes 3932168 | tf_op jit(solution)/shard_map/qkv_rep/ppermute | solution.py:310
  63.1 0.0 collective-permute-done.5
  63.1 0.0 collective-permute-done.6
  63.1 0.0 all-gather.6.cloned.1.call-done
  63.2 0.7 pad_maximum_fusion
  63.9 0.0 all-gather.8.cloned.1.call-update
  63.9 1.4 copy-done.1
  65.3 1.1 shard_map.104.first_ref
  66.4 0.0 collective-permute-done.7.w_ref
  66.4 1.0 shard_map.105
  67.5 0.0 copy-start.3
  67.5 19.9 %all_to_all.20.p_ref = bf16[4,496,128]{2,1,0:T(8,128)(2,1)S(1)} all-to-all(bf16[4,496,128]{2,1,0:T(8,128)(2,1)S(1)} %shard_map.105), channel_id=1, replica_groups=mesh['z'=8,'yh'=4,'yl'=2,'x'=4,'c'=2] {'yh'}, dimensions={0} | all-to-all | bytes 1015808 | tf_op jit(solution)/shard_map/qkv_sum/all_to_all | solution.py:317
  87.4 0.1 qkv_z.1
  87.4 34.1 %all-gather.2 = bf16[3968,128]{1,0:T(8,128)(2,1)S(1)} all-gather(bf16[496,128]{1,0:T(8,128)(2,1)S(1)} %qkv_z.1), channel_id=4, replica_groups=mesh['z'=8,'yh'=4,'yl'=2,'x'=4,'c'=2] {'z'}, dimensions={0}, use_global_device_ids=true | all-gather | bytes 1142784 | tf_op jit(solution)/shard_map/qkv_z/all_gather | solution.py:319
  121.6 0.0 copy-done.3
  121.6 2.3 %shard_map.106.att_ref = bf16[384,1024]{1,0:T(8,128)(2,1)S(1)} custom-call(s32[2]{0:T(128)S(1)} %copy-done.3, bf16[8,496,128]{2,1,0:T(8,128)(2,1)S(1)} %bitcast.14), custom_call_target="tpu_custom_call" | custom-call | flops 8000000000 | bytes 2000000 | tf_op jit(solution)/shard_map/pallas_call | solution.py:209
  123.9 1.9 %shard_map.107 = bf16[4,384,256]{2,1,0:T(8,128)(2,1)} custom-call(bf16[384,1024]{1,0:T(8,128)(2,1)S(1)} %shard_map.106.att_ref, bf16[16,256,256]{2,1,0:T(8,128)(2,1)S(1)} %bitcast.11), custom_call_target="tpu_custom_call" | custom-call | flops 805306368 | bytes 5000000 | tf_op jit(solution)/shard_map/pallas_call | solution.py:222
  125.8 3.6 %all-to-all-start.2 = ((bf16[4,384,256]{2,1,0:T(8,128)(2,1)}), bf16[4,384,256]{2,1,0:T(8,128)(2,1)S(1)}, u32[]{:S(2)}, u32[]{:S(2)}) async-start(bf16[4,384,256]{2,1,0:T(8,128)(2,1)} %shard_map.107), calls=%async_computation.2 | async-start | bytes 1572864 | tf_op jit(solution)/shard_map/out_sum/all_to_all | solution.py:324
  129.5 13.4 %all-to-all-done.2.p_ref = bf16[4,384,256]{2,1,0:T(8,128)(2,1)S(1)} async-done(((bf16[4,384,256]{2,1,0:T(8,128)(2,1)}), bf16[4,384,256]{2,1,0:T(8,128)(2,1)S(1)}, u32[]{:S(2)}, u32[]{:S(2)}) %all-to-all-start.2) | async-done | bytes 786464 | tf_op jit(solution)/shard_map/out_sum/all_to_all | solution.py:324
  142.9 1.1 shard_map.108
  144.1 8.1 %all-to-all-start.3 = ((bf16[32,8,384]{2,1,0:T(8,128)(2,1)}), bf16[32,8,384]{2,1,0:T(8,128)(2,1)S(1)}, u32[]{:S(2)}, u32[]{:S(2)}) async-start(bf16[32,8,384]{2,1,0:T(8,128)(2,1)} %get-tuple-element.21), calls=%async_computation.3 | async-start | bytes 393216 | tf_op jit(solution)/shard_map/stat_tp/all_to_all | solution.py:330
  152.1 0.1 iota_compare_fusion
  152.2 0.1 lt.32
  152.3 12.4 %all-to-all-done.3 = bf16[32,8,384]{2,1,0:T(8,128)(2,1)S(1)} async-done(((bf16[32,8,384]{2,1,0:T(8,128)(2,1)}), bf16[32,8,384]{2,1,0:T(8,128)(2,1)S(1)}, u32[]{:S(2)}, u32[]{:S(2)}) %all-to-all-start.3) | async-done | bytes 196640 | tf_op jit(solution)/shard_map/stat_tp/all_to_all | solution.py:330
  164.7 0.6 fusion.1
  (18 shorter events, 0.2 us)
Async XLA Ops:
  7.2 25.2 %copy-start.4 = (bf16[256,256]{1,0:T(8,128)(2,1)S(1)}, bf16[256,256]{1,0:T(8,128)(2,1)}, u32[]{:S(2)}) copy-start(bf16[256,256]{1,0:T(8,128)(2,1)} %param.15) | copy-start | bytes 393220
  7.2 56.0 %all-gather.6.cloned.1.call-start = ((), (), s32[]{:S(2)}) async-start(), calls=%async_computation.4 | async-start | bytes 1769472 | tf_op jit(solution)/shard_map/tokens_z/all_gather | solution.py:307
  8.0 13.0 %collective-permute-start.2 = (bf16[32,512]{1,0:T(8,128)(2,1)S(1)}, bf16[32,512]{1,0:T(8,128)(2,1)S(1)}, u32[]{:S(2)}, u32[]{:S(2)}) collective-permute-start(bf16[32,512]{1,0:T(8,128)(2,1)S(1)} %pad_maximum_fusion.3), channel_id=1, source_target_pairs={{0,0},{16,64},{32,128},{48,192},{64,256},{80,320},{96,384},{112,44... | collective-permute-start | bytes 98312 | tf_op jit(solution)/shard_map/weights_yh/ppermute | solution.py:284
  11.2 23.7 %collective-permute-start = (bf16[128,256]{1,0:T(8,128)(2,1)S(1)}, bf16[128,256]{1,0:T(8,128)(2,1)S(1)}, u32[]{:S(2)}, u32[]{:S(2)}) collective-permute-start(bf16[128,256]{1,0:T(8,128)(2,1)S(1)} %get-tuple-element.25), channel_id=1, source_target_pairs={{0,0},{1,32},{16,1},{17,33},{32,16},{33,48},{48,17},{49,49},{2,2},... | collective-permute-start | bytes 196616 | tf_op jit(solution)/shard_map/weights_yh/ppermute | solution.py:288
  11.9 23.0 %collective-permute-start.1 = (bf16[128,256]{1,0:T(8,128)(2,1)S(1)}, bf16[128,256]{1,0:T(8,128)(2,1)S(1)}, u32[]{:S(2)}, u32[]{:S(2)}) collective-permute-start(bf16[128,256]{1,0:T(8,128)(2,1)S(1)} %get-tuple-element.24), channel_id=1, source_target_pairs={{0,16},{1,48},{16,17},{17,49},{32,0},{33,32},{48,1},{49,33},{2,18}... | collective-permute-start | bytes 196616 | tf_op jit(solution)/shard_map/weights_yh/ppermute | solution.py:288
  21.0 11.4 %collective-permute-start.3 = (bf16[32,256]{1,0:T(8,128)(2,1)S(1)}, bf16[32,256]{1,0:T(8,128)(2,1)S(1)}, u32[]{:S(2)}, u32[]{:S(2)}) collective-permute-start(bf16[32,256]{1,0:T(8,128)(2,1)S(1)} %get-tuple-element.33), channel_id=1, source_target_pairs={{0,0},{1,32},{16,1},{17,33},{32,16},{33,48},{48,17},{49,49},{2,2},... | collective-permute-start | bytes 49160 | tf_op jit(solution)/shard_map/weights_yh/ppermute | solution.py:293
  21.7 13.2 %collective-permute-start.4 = (bf16[32,256]{1,0:T(8,128)(2,1)S(1)}, bf16[32,256]{1,0:T(8,128)(2,1)S(1)}, u32[]{:S(2)}, u32[]{:S(2)}) collective-permute-start(bf16[32,256]{1,0:T(8,128)(2,1)S(1)} %get-tuple-element.32), channel_id=1, source_target_pairs={{0,16},{1,48},{16,17},{17,49},{32,0},{33,32},{48,1},{49,33},{2,18}... | collective-permute-start | bytes 49160 | tf_op jit(solution)/shard_map/weights_yh/ppermute | solution.py:293
  36.1 27.8 %copy-start.2 = (bf16[384,256]{1,0:T(8,128)(2,1)S(1)}, bf16[384,256]{1,0:T(8,128)(2,1)}, u32[]{:S(2)}) copy-start(bf16[384,256]{1,0:T(8,128)(2,1)} %x_ref.1) | copy-start | bytes 589828
  36.1 24.3 %all-to-all-start = ((bf16[8,320,256]{2,1,0:T(8,128)(2,1)}), bf16[8,320,256]{2,1,0:T(8,128)(2,1)S(1)}, u32[]{:S(2)}, u32[]{:S(2)}) async-start(bf16[8,320,256]{2,1,0:T(8,128)(2,1)} %weights_yh.1), calls=%async_computation | async-start | bytes 2621440 | tf_op jit(solution)/shard_map/qkv_rep/all_to_all | solution.py:309
  41.9 79.7 %all-gather.8.cloned.1.call-start = ((), (), s32[]{:S(2)}) async-start(), calls=%async_computation.5 | async-start | bytes 2228224 | tf_op jit(solution)/shard_map/out_rep/all_gather | solution.py:314
  41.9 21.2 %collective-permute-start.5 = (bf16[128,256]{1,0:T(8,128)(2,1)S(1)}, bf16[128,256]{1,0:T(8,128)(2,1)S(1)}, u32[]{:S(2)}, u32[]{:S(2)}) collective-permute-start(bf16[128,256]{1,0:T(8,128)(2,1)S(1)} %get-tuple-element.12), channel_id=1, source_target_pairs={{0,0},{1,32},{16,1},{17,33},{32,16},{33,48},{48,17},{49,49},{2,2},... | collective-permute-start | bytes 196616 | tf_op jit(solution)/shard_map/out_yh/ppermute | solution.py:302
  42.6 20.6 %collective-permute-start.6 = (bf16[128,256]{1,0:T(8,128)(2,1)S(1)}, bf16[128,256]{1,0:T(8,128)(2,1)S(1)}, u32[]{:S(2)}, u32[]{:S(2)}) collective-permute-start(bf16[128,256]{1,0:T(8,128)(2,1)S(1)} %get-tuple-element.13), channel_id=1, source_target_pairs={{0,16},{1,48},{16,17},{17,49},{32,0},{33,32},{48,1},{49,33},{2,18}... | collective-permute-start | bytes 196616 | tf_op jit(solution)/shard_map/out_yh/ppermute | solution.py:302
  60.4 6.1 %collective-permute-start.7 = (bf16[8,320,256]{2,1,0:T(8,128)(2,1)S(1)}, bf16[8,320,256]{2,1,0:T(8,128)(2,1)S(1)}, u32[]{:S(2)}, u32[]{:S(2)}) collective-permute-start(bf16[8,320,256]{2,1,0:T(8,128)(2,1)S(1)} %all-to-all-done.w_ref), channel_id=1, source_target_pairs={{0,1},{1,0},{2,3},{3,2},{4,5},{5,4},{6,7},{7,6},{8,9},{9,8},{10,11... | collective-permute-start | bytes 3932168 | tf_op jit(solution)/shard_map/qkv_rep/ppermute | solution.py:310
  63.9 1.4 copy-start.1
  67.5 54.1 %copy-start.3 = (s32[2]{0:T(128)S(1)}, s32[2]{0:T(128)}, u32[]{:S(2)}) copy-start(s32[2]{0:T(128)} %len_ref.1) | copy-start | bytes 28
  121.6 2.3 %copy-start = (bf16[4096,256]{1,0:T(8,128)(2,1)S(1)}, bf16[4096,256]{1,0:T(8,128)(2,1)}, u32[]{:S(2)}) copy-start(bf16[4096,256]{1,0:T(8,128)(2,1)} %all-gather.8.cloned.1.call-done) | copy-start | bytes 6291460
  125.8 3.6 %copy-start.5 = (f32[256,6]{0,1:T(8,128)S(1)}, f32[256,6]{0,1:T(8,128)}, u32[]{:S(2)}) copy-start(f32[256,6]{0,1:T(8,128)} %param.17) | copy-start | bytes 18436
  125.8 3.6 %copy-start.6 = (f32[256]{0:T(256)S(1)}, f32[256]{0:T(256)}, u32[]{:S(2)}) copy-start(f32[256]{0:T(256)} %param.16) | copy-start | bytes 3076
  125.8 17.1 %all-to-all-start.2 = ((bf16[4,384,256]{2,1,0:T(8,128)(2,1)}), bf16[4,384,256]{2,1,0:T(8,128)(2,1)S(1)}, u32[]{:S(2)}, u32[]{:S(2)}) async-start(bf16[4,384,256]{2,1,0:T(8,128)(2,1)} %shard_map.107), calls=%async_computation.2 | async-start | bytes 1572864 | tf_op jit(solution)/shard_map/out_sum/all_to_all | solution.py:324
  144.1 20.6 %all-to-all-start.3 = ((bf16[32,8,384]{2,1,0:T(8,128)(2,1)}), bf16[32,8,384]{2,1,0:T(8,128)(2,1)S(1)}, u32[]{:S(2)}, u32[]{:S(2)}) async-start(bf16[32,8,384]{2,1,0:T(8,128)(2,1)} %get-tuple-element.21), calls=%async_computation.3 | async-start | bytes 393216 | tf_op jit(solution)/shard_map/stat_tp/all_to_all | solution.py:330
Sparse Core Ops, SparseCore 0:
  10.7 52.2 all-gather.5
  65.6 38.9 all-gather.7
